TPU v7x, 128 devices: a whole 4x4x4 slice. The times are simulated.
128 devices in a mesh: branch: 2 (over x_hi), ulysses: 4 (over y), fsdp: 16 (over z, x_lo, core).
Axes of the slice: x: 4 (x_hi: 2, x_lo: 2; x = x_hi * 2 + x_lo), y: 4, z: 4, core: 2. Of those that a mesh axis runs over, the one named last changes fastest.
Arguments:
- hidden: bfloat16 [2, 16, 1024, 5120], P('branch', 'fsdp', 'ulysses'), may hold values from -128 to 128, as said below
- query: bfloat16 [2, 16, 1024, 2560], P('branch', 'fsdp', None, 'ulysses'), may hold values from -128 to 128, as said below
- key: bfloat16 [2, 16, 1024, 2560], P('branch', 'fsdp', None, 'ulysses'), may hold values from -5 to 5, as said below
- value: bfloat16 [2, 16, 1024, 2560], P('branch', 'fsdp', None, 'ulysses'), may hold values from -6 to 6
- output_projection_weight: bfloat16 [2560, 5120], P('fsdp'), may hold values from -0.125 to 0.125
- adapter_down_weight: bfloat16 [2560, 64], replicated, may hold values from -0.125 to 0.125
- adapter_up_weight: bfloat16 [64, 5120], replicated, may hold values from -0.75 to 0.75
- reward_gradient: bfloat16 [16, 1024, 5120], P('fsdp', 'ulysses'), may hold values from -24 to 24, as said below
Outputs:
- grad_hidden: bfloat16 [2, 16, 1024, 5120], P('branch', 'fsdp', 'ulysses')
- grad_query: bfloat16 [2, 16, 1024, 2560], P('branch', 'fsdp', None, 'ulysses')
- grad_key: bfloat16 [2, 16, 1024, 2560], P('branch', 'fsdp', None, 'ulysses')
- grad_value: bfloat16 [2, 16, 1024, 2560], P('branch', 'fsdp', None, 'ulysses')
- adapter_down_gradient: float32 [2560, 64], replicated
- adapter_up_gradient: float32 [64, 5120], replicated
Inputs may be any that keep to these rules, and one draw needn't show every extreme that they name: `hidden`: Real-valued residual stream. `query`: Real-valued queries. `key`: Real-valued keys. `reward_gradient`: Real-valued reward gradient.
All inputs are finite; a program needn't handle non-finite values.
Results may differ from a plain program's by a relative error of at most 0.013.
Values may be sent and summed in bfloat16 or wider, within the bound.
No kernel may reach another device: no remote copies, remote signals or barrier semaphores. Data moves between devices by JAX's collectives and lax.ppermute only.
A program may use at most 192 MiB of HBM per device.

v0:
```python
import jax
import jax.numpy as jnp
from jax import lax
from jax.sharding import PartitionSpec as P

HD = 128


GUIDANCE = 5.0


def swapped(block, axis, stride):
    count = lax.axis_size(axis)
    route = []
    for low in range(count):
        high = low | 1 << stride
        if high != low and high < count:
            route += [(low, high), (high, low)]
    return lax.ppermute(block, axis, route)


def head_major(block_rows, heads_here):
    seq_len = block_rows.shape[0]
    return block_rows.reshape(seq_len, heads_here, -1).transpose(1, 0, 2)


def token_major(block_heads):
    heads_here, seq_len, head_size = block_heads.shape
    return block_heads.transpose(1, 0, 2).reshape(seq_len, heads_here * head_size)


def softmax_probs(query_head, key_head, score_scale):
    scores = jnp.dot(query_head, key_head.T, preferred_element_type=jnp.float32) * score_scale
    row_peak = jnp.max(scores, axis=1, keepdims=True)
    exp_scores = jnp.exp(scores - row_peak)
    return exp_scores / jnp.sum(exp_scores, axis=1, keepdims=True)


def body(
    hidden,
    query,
    key,
    value,
    output_projection_weight,
    adapter_down_weight,
    adapter_up_weight,
    reward_gradient,
):
    score_scale = HD ** (-0.5)
    seq_len, local_features = (query.shape[2], query.shape[3])
    heads_here = local_features // HD
    query_heads = head_major(query.reshape(seq_len, local_features), heads_here)
    key_heads = head_major(key.reshape(seq_len, local_features), heads_here)
    value_heads = head_major(value.reshape(seq_len, local_features), heads_here)

    def forward_one(head_items):
        query_head, key_head, value_head = head_items
        attn_probs = softmax_probs(query_head, key_head, score_scale)
        output_head = jnp.dot(
            attn_probs.astype(jnp.bfloat16), value_head, preferred_element_type=jnp.float32
        )
        return (attn_probs, output_head.astype(jnp.bfloat16))

    probs_kept, attended_heads = lax.map(forward_one, (query_heads, key_heads, value_heads))
    attention_output = lax.all_to_all(
        token_major(attended_heads), "ulysses", split_axis=0, concat_axis=1, tiled=True
    )
    full_weight = lax.all_gather(output_projection_weight, "fsdp", axis=0, tiled=True)
    token_count, model_width = (hidden.shape[2], hidden.shape[3])
    own_hidden = hidden.reshape(token_count, model_width)
    adapter_middle = jnp.dot(
        attention_output, adapter_down_weight, preferred_element_type=jnp.float32
    ).astype(jnp.bfloat16)
    guided_velocity = own_hidden.astype(jnp.float32)
    guided_velocity = guided_velocity + jnp.dot(
        attention_output, full_weight, preferred_element_type=jnp.float32
    )
    guided_velocity = guided_velocity + jnp.dot(
        adapter_middle, adapter_up_weight, preferred_element_type=jnp.float32
    )
    guided_velocity = guided_velocity.astype(jnp.bfloat16)
    partner = swapped(guided_velocity, "branch", 0)
    is_cond = lax.axis_index("branch") == 0
    cond_velocity = jnp.where(is_cond, guided_velocity, partner).astype(jnp.float32)
    uncond = jnp.where(is_cond, partner, guided_velocity).astype(jnp.float32)
    target = reward_gradient.reshape(token_count, model_width).astype(jnp.float32)
    inner_sum, energy, pull_sum = lax.psum(
        (jnp.sum(cond_velocity * uncond), jnp.sum(uncond * uncond), jnp.sum(target * uncond)),
        "ulysses",
    )
    energy = energy + 1e-08
    cfg_scale = inner_sum / energy
    cfg_slope = (1.0 - GUIDANCE) * pull_sum / energy
    target_coef = jnp.where(is_cond, GUIDANCE, (1.0 - GUIDANCE) * cfg_scale)
    cond_coef = jnp.where(is_cond, 0.0, cfg_slope)
    uncond_coef = jnp.where(is_cond, cfg_slope, -2.0 * cfg_slope * cfg_scale)
    velocity_gradient = (
        target_coef * target + cond_coef * cond_velocity + uncond_coef * uncond
    ).astype(jnp.bfloat16)
    contract_over_rows = (((0,), (0,)), ((), ()))
    contract_columns = (((1,), (1,)), ((), ()))
    middle_gradient = jnp.dot(
        velocity_gradient, adapter_up_weight.T, preferred_element_type=jnp.float32
    ).astype(jnp.bfloat16)
    local_up_weight = lax.dot_general(
        adapter_middle, velocity_gradient, contract_over_rows, preferred_element_type=jnp.float32
    )
    local_down_weight = lax.dot_general(
        attention_output, middle_gradient, contract_over_rows, preferred_element_type=jnp.float32
    )
    adapter_down_gradient, adapter_up_gradient = lax.psum(
        (local_down_weight, local_up_weight), ("branch", "ulysses", "fsdp")
    )
    attention_gradient = lax.dot_general(
        velocity_gradient, full_weight, contract_columns, preferred_element_type=jnp.float32
    )
    attention_gradient = attention_gradient + lax.dot_general(
        middle_gradient, adapter_down_weight, contract_columns, preferred_element_type=jnp.float32
    )
    attention_gradient = attention_gradient.astype(jnp.bfloat16)
    grad_by_heads = lax.all_to_all(
        attention_gradient, "ulysses", split_axis=1, concat_axis=0, tiled=True
    )
    grad_heads = head_major(grad_by_heads, heads_here)

    def backward_one(head_items):
        attn_probs, query_head, key_head, value_head, output_head, grad_head = head_items
        row_delta = jnp.sum(
            grad_head.astype(jnp.float32) * output_head.astype(jnp.float32), axis=1, keepdims=True
        )
        grad_probs = jnp.dot(grad_head, value_head.T, preferred_element_type=jnp.float32)
        grad_scores = (attn_probs * (grad_probs - row_delta)).astype(jnp.bfloat16)
        grad_value_head = jnp.dot(
            attn_probs.astype(jnp.bfloat16).T, grad_head, preferred_element_type=jnp.float32
        ).astype(jnp.bfloat16)
        grad_query_head = (
            jnp.dot(grad_scores, key_head, preferred_element_type=jnp.float32) * score_scale
        ).astype(jnp.bfloat16)
        grad_key_head = (
            jnp.dot(grad_scores.T, query_head, preferred_element_type=jnp.float32) * score_scale
        ).astype(jnp.bfloat16)
        return (grad_query_head, grad_key_head, grad_value_head)

    grad_query_heads, grad_key_heads, grad_value_heads = lax.map(
        backward_one, (probs_kept, query_heads, key_heads, value_heads, attended_heads, grad_heads)
    )
    return (
        velocity_gradient.reshape(hidden.shape),
        token_major(grad_query_heads).reshape(query.shape),
        token_major(grad_key_heads).reshape(key.shape),
        token_major(grad_value_heads).reshape(value.shape),
        adapter_down_gradient,
        adapter_up_gradient,
    )


def solution(mesh):
    in_specs = (
        P("branch", "fsdp", "ulysses", None),
        P("branch", "fsdp", None, "ulysses"),
        P("branch", "fsdp", None, "ulysses"),
        P("branch", "fsdp", None, "ulysses"),
        P("fsdp", None),
        P(),
        P(),
        P("fsdp", "ulysses", None),
    )
    out_specs = (
        P("branch", "fsdp", "ulysses", None),
        P("branch", "fsdp", None, "ulysses"),
        P("branch", "fsdp", None, "ulysses"),
        P("branch", "fsdp", None, "ulysses"),
        P(),
        P(),
    )
    return jax.shard_map(body, mesh=mesh, in_specs=in_specs, out_specs=out_specs, check_vma=False)
```

profile of v0, /device:TPU:1, one launch (start us, length us, event | category | flops | bytes accessed | tf_op | source)
XLA Modules:
  0.0 442.2 jit_solution(16377925678567825826)
XLA Ops:
  10.3 2.4 copy.39
  12.8 1.8 copy.42
  14.5 2.4 copy.40
  17.0 2.4 copy.43
  19.4 35.3 %while.26 = (s32[]{:T(128)}, f32[5,1024,1024]{1,2,0:T(8,128)}, bf16[5,1024,128]{2,1,0:T(8,128)(2,1)}, bf16[5,1024,128]{2,1,0:T(8,128)(2,1)S(1)}, bf16[5,1024,128...) while((s32[]{:T(128)}, f32[5,1024,1024]{1,2,0:T(8,128)}, ...), condition=%wide.region_3.4_spmd, body=%wide.region_0.3_spmd.sunk | while | flops 549582848 | bytes 22051404 | solution.py:64
  20.8 3.2 bitcast_dynamic-update-slice_fusion.2
  24.0 2.8 fusion.99
  28.3 2.7 bitcast_dynamic-update-slice_fusion.2
  30.9 2.8 fusion.99
  35.2 2.8 bitcast_dynamic-update-slice_fusion.2
  38.0 2.8 fusion.99
  42.2 2.7 bitcast_dynamic-update-slice_fusion.2
  44.9 2.8 fusion.99
  49.2 2.8 bitcast_dynamic-update-slice_fusion.2
  51.9 2.8 fusion.99
  54.7 3.3 copy.44
  58.0 3.8 all_to_all.26
  63.4 21.3 %all_to_all.35 = bf16[4,256,640]{1,2,0:T(8,128)(2,1)S(1)} all-to-all(bf16[4,256,640]{1,2,0:T(8,128)(2,1)S(1)} %copy.45), channel_id=1, replica_groups=mesh['branch'=2,'ulysses'=4,'fsdp'=16] {'ulysses'}, dimensions={0} | all-to-all | bytes 2621440 | tf_op jit(solution)/shard_map/all_to_all | solution.py:65
  85.1 64.4 %all-gather.2.cloned.1.call-done = bf16[2560,5120]{1,0:T(8,128)(2,1)} async-done(((bf16[160,5120]{1,0:T(8,128)(2,1)}), bf16[2560,5120]{1,0:T(8,128)(2,1)}) %all-gather.2.cloned.1.call-update) | async-done | bytes 26214416 | tf_op jit(solution)/shard_map/all_gather | solution.py:68
  149.5 14.3 %convolution_add_fusion.1 = f32[256,5120]{1,0:T(8,128)S(1)} fusion(bf16[256,2560]{0,1:T(8,128)(2,1)S(1)} %bitcast.151, bf16[2560,5120]{1,0:T(8,128)(2,1)} %all-gather.2.cloned.1.call-done, bf16[1,1,256,5120]{3,2,1,0:T(8,128)(2,1)} %param.12), kind=kOutput, calls=%fused_computation.58 | convolution fusion | flops 6713507840 | bytes 35389440 | tf_op jit(solution)/shard_map/dot_general | solution.py:75
  164.7 3.0 collective-permute-start
  167.7 57.1 %collective-permute-done = bf16[256,5120]{1,0:T(8,128)(2,1)} collective-permute-done((bf16[256,5120]{1,0:T(8,128)(2,1)S(1)}, bf16[256,5120]{1,0:T(8,128)(2,1)}, u32[]{:S(2)}, u32[]{:S(2)}) %collective-permute-start) | collective-permute-done | bytes 2621472 | tf_op jit(solution)/shard_map/ppermute | solution.py:19
  224.8 5.3 %fusion.54 = (f32[]{:T(128)}, f32[]{:T(128)}, f32[]{:T(128)}, bf16[256,5120]{1,0:T(8,128)(2,1)}) fusion(bf16[256,5120]{1,0:T(8,128)(2,1)S(1)} %fusion.50, bf16[256,5120]{1,0:T(8,128)(2,1)} %collective-permute-done, pred[]{:T(512)S(6)} %eq.3, bf16[1,256,5120]{2,1,0:T(8,128)(2,1)} %param.19), kind=kLoop, calls=%fused_computation.63 | loop fusion | flops 14417917 | bytes 10485773 | tf_op jit(solution)/shard_map/reduce_sum | solution.py:88
  230.2 9.1 %all-reduce.1 = (f32[]{:T(128)}, f32[]{:T(128)}, f32[]{:T(128)}) all-reduce(f32[]{:T(128)} %get-tuple-element.154, f32[]{:T(128)} %get-tuple-element.153, f32[]{:T(128)} %get-tuple-element.152), channel_id=1, replica_groups=mesh['branch'=2,'ulysses'=4,'fsdp'=16] {'ulysses'}, use_global_device_ids=true, to_apply=%region_9.10 | all-reduce | flops 3 | bytes 24 | tf_op jit(solution)/shard_map/psum | solution.py:87
  241.2 5.3 %fusion.53 = bf16[256,5120]{1,0:T(8,128)(2,1)S(1)} fusion(bf16[256,5120]{1,0:T(8,128)(2,1)} %get-tuple-element.192, bf16[1,256,5120]{2,1,0:T(8,128)(2,1)} %param.19, f32[]{:T(128)S(6)} %select_n.28, f32[]{:T(128)S(6)} %select_n.27, f32[]{:T(128)S(6)} %select_n.26, bf16[256,5120]{1,0:T(8,128)(2,1)} %copy-done.3, bf16[256,5120]{1,0:T(8,128)(2,1)} %collective-permute-done, ...), kind=kLoop, calls=%fused_computation.62 | loop fusion | flops 13107200 | bytes 13107213 | tf_op jit(solution)/shard_map/convert_element_type | solution.py:99
  247.7 2.0 fusion.58
  249.7 14.1 %fusion.57 = bf16[256,2560]{1,0:T(8,128)(2,1)} fusion(f32[256,2560]{1,0:T(8,128)} %fusion.58, bf16[256,5120]{1,0:T(8,128)(2,1)S(1)} %fusion.53, bf16[2560,5120]{1,0:T(8,128)(2,1)} %all-gather.2.cloned.1.call-done), kind=kOutput, calls=%fused_computation.67 | convolution fusion | flops 6712197120 | bytes 32768000 | tf_op jit(solution)/shard_map/dot_general | solution.py:114
  263.8 2.4 copy.59
  266.2 4.3 all-to-all-start.1
  270.8 2.7 fusion.59
  275.1 10.0 %all-to-all-done.1 = bf16[256,4,640]{0,2,1:T(8,128)(2,1)} async-done(((bf16[256,4,640]{0,2,1:T(8,128)(2,1)}), bf16[256,4,640]{0,2,1:T(8,128)(2,1)}, u32[]{:S(2)}, u32[]{:S(2)}) %all-to-all-start.1) | async-done | bytes 1310752 | tf_op jit(solution)/shard_map/all_to_all | solution.py:121
  285.1 2.3 copy.47
  287.5 1.8 reshape.40
  289.2 119.5 %while.27 = (s32[]{:T(128)}, bf16[5,1024,128]{1,2,0:T(8,128)(2,1)}, bf16[5,1024,128]{1,2,0:T(8,128)(2,1)}, bf16[5,1024,128]{1,2,0:T(8,128)(2,1)}, f32[5,1024,102...) while((s32[]{:T(128)}, bf16[5,1024,128]{1,2,0:T(8,128)(2,1)}, ...), condition=%wide.region_12.13_spmd, body=%wide.region_10.12_spmd.sunk | while | flops 1079114752 | bytes 38283896 | solution.py:144
  291.6 4.8 %constant_dynamic-slice_fusion.4 = f32[1,1024,1024]{1,2,0:T(8,128)} fusion(f32[5,1024,1024]{1,2,0:T(8,128)} %get-tuple-element.350, s32[]{:T(128)} %get-tuple-element.335), kind=kLoop, calls=%fused_computation.50.clone.1 | loop fusion | bytes 8388612 | tf_op jit(solution)/shard_map/while/body/jit(dynamic_index_in_dim)/dynamic_slice | solution.py:144
  296.3 5.4 %copy.73 = f32[1,1024,1024]{2,1,0:T(8,128)} copy(f32[1,1024,1024]{1,2,0:T(8,128)} %constant_dynamic-slice_fusion.4) | data formatting | bytes 8388608 | tf_op jit(solution)/shard_map/while/body/jit(dynamic_index_in_dim)/dynamic_slice | solution.py:144
  301.8 3.1 fusion.109
  304.9 1.7 fusion.112
  306.7 3.0 fusion.111
  315.6 4.7 %constant_dynamic-slice_fusion.4 = f32[1,1024,1024]{1,2,0:T(8,128)} fusion(f32[5,1024,1024]{1,2,0:T(8,128)} %get-tuple-element.350, s32[]{:T(128)} %get-tuple-element.335), kind=kLoop, calls=%fused_computation.50.clone.1 | loop fusion | bytes 8388612 | tf_op jit(solution)/shard_map/while/body/jit(dynamic_index_in_dim)/dynamic_slice | solution.py:144
  320.3 5.4 %copy.73 = f32[1,1024,1024]{2,1,0:T(8,128)} copy(f32[1,1024,1024]{1,2,0:T(8,128)} %constant_dynamic-slice_fusion.4) | data formatting | bytes 8388608 | tf_op jit(solution)/shard_map/while/body/jit(dynamic_index_in_dim)/dynamic_slice | solution.py:144
  325.7 3.1 fusion.109
  328.8 1.7 fusion.112
  330.7 3.0 fusion.111
  339.5 4.7 %constant_dynamic-slice_fusion.4 = f32[1,1024,1024]{1,2,0:T(8,128)} fusion(f32[5,1024,1024]{1,2,0:T(8,128)} %get-tuple-element.350, s32[]{:T(128)} %get-tuple-element.335), kind=kLoop, calls=%fused_computation.50.clone.1 | loop fusion | bytes 8388612 | tf_op jit(solution)/shard_map/while/body/jit(dynamic_index_in_dim)/dynamic_slice | solution.py:144
  344.2 5.4 %copy.73 = f32[1,1024,1024]{2,1,0:T(8,128)} copy(f32[1,1024,1024]{1,2,0:T(8,128)} %constant_dynamic-slice_fusion.4) | data formatting | bytes 8388608 | tf_op jit(solution)/shard_map/while/body/jit(dynamic_index_in_dim)/dynamic_slice | solution.py:144
  349.6 3.1 fusion.109
  352.7 1.7 fusion.112
  354.6 3.0 fusion.111
  363.3 4.7 %constant_dynamic-slice_fusion.4 = f32[1,1024,1024]{1,2,0:T(8,128)} fusion(f32[5,1024,1024]{1,2,0:T(8,128)} %get-tuple-element.350, s32[]{:T(128)} %get-tuple-element.335), kind=kLoop, calls=%fused_computation.50.clone.1 | loop fusion | bytes 8388612 | tf_op jit(solution)/shard_map/while/body/jit(dynamic_index_in_dim)/dynamic_slice | solution.py:144
  368.1 5.4 %copy.73 = f32[1,1024,1024]{2,1,0:T(8,128)} copy(f32[1,1024,1024]{1,2,0:T(8,128)} %constant_dynamic-slice_fusion.4) | data formatting | bytes 8388608 | tf_op jit(solution)/shard_map/while/body/jit(dynamic_index_in_dim)/dynamic_slice | solution.py:144
  373.4 3.1 fusion.109
  376.5 1.7 fusion.112
  378.4 3.0 fusion.111
  387.2 4.7 %constant_dynamic-slice_fusion.4 = f32[1,1024,1024]{1,2,0:T(8,128)} fusion(f32[5,1024,1024]{1,2,0:T(8,128)} %get-tuple-element.350, s32[]{:T(128)} %get-tuple-element.335), kind=kLoop, calls=%fused_computation.50.clone.1 | loop fusion | bytes 8388612 | tf_op jit(solution)/shard_map/while/body/jit(dynamic_index_in_dim)/dynamic_slice | solution.py:144
  391.9 5.4 %copy.73 = f32[1,1024,1024]{2,1,0:T(8,128)} copy(f32[1,1024,1024]{1,2,0:T(8,128)} %constant_dynamic-slice_fusion.4) | data formatting | bytes 8388608 | tf_op jit(solution)/shard_map/while/body/jit(dynamic_index_in_dim)/dynamic_slice | solution.py:144
  397.3 3.1 fusion.109
  400.4 1.7 fusion.112
  402.3 3.0 fusion.111
  406.2 1.7 fusion.110
  408.8 2.6 copy.56
  414.2 16.7 %all-reduce.4.cloned.1.call-done = (f32[2560,64]{0,1:T(8,128)}, f32[64,5120]{1,0:T(8,128)}) async-done(((f32[2560,64]{0,1:T(8,128)}, f32[64,5120]{1,0:T(8,128)}), (f32[2560,64]{0,1:T(8,128)}, f32[64,5120]{1,0:T(8,128)})) %all-reduce.4.cloned.1.call-update) | async-done | bytes 1966096 | tf_op jit(solution)/shard_map/psum | solution.py:111
  431.0 2.0 copy.108
  432.9 2.5 copy.109
  (94 shorter events, 47.2 us)
Async XLA Ops:
  7.2 156.7 %copy-start = (bf16[64,5120]{1,0:T(8,128)(2,1)S(1)}, bf16[64,5120]{1,0:T(8,128)(2,1)}, u32[]{:S(2)}) copy-start(bf16[64,5120]{1,0:T(8,128)(2,1)} %param.18) | copy-start | bytes 1966084
  7.2 142.3 %all-gather.2.cloned.1.call-start = ((), (), s32[]{:S(2)}) async-start(), calls=%async_computation.2 | async-start | bytes 27852800 | tf_op jit(solution)/shard_map/all_gather | solution.py:68
  54.7 7.1 %copy-start.5 = (bf16[5,1024,128]{2,1,0:T(8,128)(2,1)}, bf16[5,1024,128]{2,1,0:T(8,128)(2,1)S(1)}, u32[]{:S(2)}) copy-start(bf16[5,1024,128]{2,1,0:T(8,128)(2,1)S(1)} %get-tuple-element.370) | copy-start | bytes 3932164
  54.7 7.1 %copy-start.6 = (bf16[5,1024,128]{2,1,0:T(8,128)(2,1)}, bf16[5,1024,128]{2,1,0:T(8,128)(2,1)S(1)}, u32[]{:S(2)}) copy-start(bf16[5,1024,128]{2,1,0:T(8,128)(2,1)S(1)} %get-tuple-element.371) | copy-start | bytes 3932164
  61.8 22.9 %copy-start.7 = (bf16[2560,64]{0,1:T(8,128)(2,1)S(1)}, bf16[2560,64]{0,1:T(8,128)(2,1)}, u32[]{:S(2)}) copy-start(bf16[2560,64]{0,1:T(8,128)(2,1)} %param.17) | copy-start | bytes 983044
  84.7 64.8 %copy-start.4 = (bf16[4,256,640]{1,2,0:T(8,128)(2,1)}, bf16[4,256,640]{1,2,0:T(8,128)(2,1)S(1)}, u32[]{:S(2)}) copy-start(bf16[4,256,640]{1,2,0:T(8,128)(2,1)S(1)} %all_to_all.35) | copy-start | bytes 3932164
  164.7 65.4 %copy-start.3 = (bf16[256,5120]{1,0:T(8,128)(2,1)}, bf16[256,5120]{1,0:T(8,128)(2,1)S(1)}, u32[]{:S(2)}) copy-start(bf16[256,5120]{1,0:T(8,128)(2,1)S(1)} %fusion.50) | copy-start | bytes 7864324
  164.7 60.1 %collective-permute-start = (bf16[256,5120]{1,0:T(8,128)(2,1)S(1)}, bf16[256,5120]{1,0:T(8,128)(2,1)}, u32[]{:S(2)}, u32[]{:S(2)}) collective-permute-start(bf16[256,5120]{1,0:T(8,128)(2,1)S(1)} %fusion.50), channel_id=1, source_target_pairs={{0,64},{64,0},{1,65},{65,1},{2,66},{66,2},{3,67},{67,3},{4,68},{68... | collective-permute-start | bytes 7864328 | tf_op jit(solution)/shard_map/ppermute | solution.py:19
  246.5 27.0 %copy-start.2 = (bf16[256,5120]{1,0:T(8,128)(2,1)}, bf16[256,5120]{1,0:T(8,128)(2,1)S(1)}, u32[]{:S(2)}) copy-start(bf16[256,5120]{1,0:T(8,128)(2,1)S(1)} %fusion.53) | copy-start | bytes 7864324
  246.5 1.2 copy-start.8
  266.2 18.9 %all-to-all-start.1 = ((bf16[256,4,640]{0,2,1:T(8,128)(2,1)}), bf16[256,4,640]{0,2,1:T(8,128)(2,1)}, u32[]{:S(2)}, u32[]{:S(2)}) async-start(bf16[256,4,640]{0,2,1:T(8,128)(2,1)} %bitcast.153), calls=%async_computation.1 | async-start | bytes 2621440 | tf_op jit(solution)/shard_map/all_to_all | solution.py:121
  270.5 160.4 %all-reduce.4.cloned.1.call-start = ((), (), s32[]{:S(2)}) async-start(), calls=%async_computation.3 | async-start | bytes 3932160 | tf_op jit(solution)/shard_map/psum | solution.py:111
  408.8 2.6 copy-start.9
  408.8 4.0 copy-start.10
  412.8 22.6 %copy-start.1 = (bf16[64,5120]{1,0:T(8,128)(2,1)S(1)}, bf16[64,5120]{1,0:T(8,128)(2,1)}, u32[]{:S(2)}) copy-start(bf16[64,5120]{1,0:T(8,128)(2,1)} %param.18) | copy-start | bytes 1966084
Sparse Core Ops, SparseCore 0:
  9.7 139.7 all-gather.1
  276.8 154.0 all-reduce.3
where the time goes:
time: 444 us; the launch traced here: 442 us
  waiting for transfers between devices  149 us (34%)
  local copies, waits for them, and re-layouts  103 us (23%)
  matrix products  101 us (23%)
  other arithmetic  34.2 us (8%)
  blocking collectives  30.4 us (7%)
  between operations  16.2 us (4%)
  starting transfers between devices  7.54 us (2%)
    all_gather x1, waiting for transfers between devices, body(): lax.all_gather(output_projection_weight, 'fsdp', axis=0, tiled=True)  64.4 us
    ppermute x1, waiting for transfers between devices, swapped(): return lax.ppermute(block, axis, route)  57.1 us
    dynamic_slice x10, local copies, waits for them, and re-layouts, body(): lax.map(backward_one, (probs_kept, query_heads, key_heads, value_heads, a...  50.6 us
    all_to_all x1, blocking collectives, body(): lax.all_to_all(token_major(attended_heads), 'ulysses', split_axis=0, conc...  21.3 us
    psum x1, waiting for transfers between devices, body(): lax.psum((local_down_weight, local_up_weight), ('branch', 'ulysses', 'fsd...  16.7 us
    unnamed x30, local copies, waits for them, and re-layouts  16.7 us
    dot_general x5, matrix products, backward_one(): jnp.dot(grad_head, value_head.T, preferred_element_type=jnp.float32)  15.4 us
    dot_general x5, matrix products, backward_one(): jnp.dot(attn_probs.astype(jnp.bfloat16).T, grad_head, preferred_element_t...  14.9 us
  transfers between devices with their start and end apart: 4, of which 4 were waited for; matrix products, arithmetic and copies ran while one was open for 42% of the time, Pallas kernels for 0%

commit v1 on v0

v1 whole, which is shorter than its diff:
```python
import functools

import jax
import jax.numpy as jnp
from jax import lax
from jax.experimental import pallas as pl
from jax.experimental.pallas import tpu as pltpu
from jax.sharding import PartitionSpec as P

HD = 128
GUIDANCE = 5.0
SCALE = HD ** (-0.5)
VMEM = 56 * 1024 * 1024
LAST = (((1,), (1,)), ((), ()))
FIRST = (((0,), (0,)), ((), ()))
F32 = jnp.float32
BF16 = jnp.bfloat16


def dot(a, b, dims=(((1,), (0,)), ((), ()))):
    return lax.dot_general(a, b, dims, preferred_element_type=F32)


def params():
    return pltpu.CompilerParams(vmem_limit_bytes=VMEM)


def forward_kernel(q_ref, k_ref, v_ref, p_ref, o_ref):
    rows = o_ref.shape[2]
    for part in range(o_ref.shape[1]):
        at = pl.ds(part * rows, rows)
        scores = dot(q_ref[at, :], k_ref[...], LAST) * SCALE
        exps = jnp.exp(scores - jnp.max(scores, axis=1, keepdims=True))
        probs = (exps / jnp.sum(exps, axis=1, keepdims=True)).astype(BF16)
        p_ref[0, at, :] = probs
        out = dot(probs, v_ref[...]).astype(BF16)
        o_ref[0, part] = out
        o_ref[1, part] = out


def attention_forward(query, key, value, parts):
    seq, width = query.shape
    heads = width // HD
    block = pl.BlockSpec((seq, HD), lambda h: (0, h))
    return pl.pallas_call(
        forward_kernel,
        grid=(heads,),
        in_specs=[block] * 3,
        out_specs=[
            pl.BlockSpec((1, seq, seq), lambda h: (h, 0, 0)),
            pl.BlockSpec((2, parts, seq // parts, HD), lambda h: (0, 0, 0, h)),
        ],
        out_shape=[
            jax.ShapeDtypeStruct((heads, seq, seq), BF16),
            jax.ShapeDtypeStruct((2, parts, seq // parts, width), BF16),
        ],
        compiler_params=params(),
        cost_estimate=pl.CostEstimate(
            flops=heads * 8 * seq * seq * HD,
            bytes_accessed=heads * seq * seq * 2,
            transcendentals=heads * seq * seq,
        ),
    )(query, key, value)


def backward_kernel(p_ref, q_ref, k_ref, v_ref, o_ref, g_ref, dq_ref, dk_ref, dv_ref):
    seq = q_ref.shape[0]
    probs = p_ref[0]
    grad32 = g_ref[0].astype(F32) + g_ref[1].astype(F32)
    grad32 = grad32.reshape(seq, HD)
    grad = grad32.astype(BF16)
    out = o_ref[0].reshape(seq, HD).astype(F32)
    delta = jnp.sum(grad.astype(F32) * out, axis=1, keepdims=True)
    grad_probs = dot(grad, v_ref[...], LAST)
    grad_scores = (probs.astype(F32) * (grad_probs - delta)).astype(BF16)
    dv_ref[...] = dot(probs, grad, FIRST).astype(BF16)
    dq_ref[...] = (dot(grad_scores, k_ref[...]) * SCALE).astype(BF16)
    dk_ref[...] = (dot(grad_scores, q_ref[...], FIRST) * SCALE).astype(BF16)


def attention_backward(probs, query, key, value, out, grads):
    seq, width = query.shape
    heads = width // HD
    parts = out.shape[1]
    block = pl.BlockSpec((seq, HD), lambda h: (0, h))
    return pl.pallas_call(
        backward_kernel,
        grid=(heads,),
        in_specs=[
            pl.BlockSpec((1, seq, seq), lambda h: (h, 0, 0)),
            block,
            block,
            block,
            pl.BlockSpec((1, parts, seq // parts, HD), lambda h: (0, 0, 0, h)),
            pl.BlockSpec((2, parts, seq // parts, HD), lambda h: (0, 0, 0, h)),
        ],
        out_specs=[block] * 3,
        out_shape=[jax.ShapeDtypeStruct((seq, width), BF16)] * 3,
        compiler_params=params(),
        cost_estimate=pl.CostEstimate(
            flops=heads * 16 * seq * seq * HD,
            bytes_accessed=heads * seq * seq * 2,
            transcendentals=0,
        ),
    )(probs, query, key, value, out, grads)


def velocity_kernel(
    b_ref, a_ref, w_ref, hown_ref, hoth_ref, r_ref, down_ref, up_ref,
    v_ref, m_ref, sum_ref, x_scr, m_scr, s_scr,
):
    step = pl.program_id(0)
    tokens = hown_ref.shape[0]
    wide = a_ref.shape[3]

    @pl.when(step == 0)
    def _():
        for u in range(a_ref.shape[1]):
            for b in range(2):
                x_scr[pl.ds(b * tokens, tokens), pl.ds(u * wide, wide)] = a_ref[b, u]
        mid = dot(x_scr[...], down_ref[...]).astype(BF16)
        m_scr[...] = mid
        m_ref[...] = mid.reshape(m_ref.shape)
        s_scr[...] = jnp.zeros_like(s_scr)

    first = b_ref[0] == 0
    own, oth = hown_ref[...].astype(F32), hoth_ref[...].astype(F32)
    acc = dot(x_scr[...], w_ref[...]) + dot(m_scr[...], up_ref[...])
    cond = (jnp.where(first, own, oth) + acc[:tokens]).astype(BF16)
    uncond = (jnp.where(first, oth, own) + acc[tokens:]).astype(BF16)
    v_ref[0] = cond
    v_ref[1] = uncond
    c32, u32, r32 = cond.astype(F32), uncond.astype(F32), r_ref[...].astype(F32)
    for row, term in enumerate((c32 * u32, u32 * u32, r32 * u32)):
        s_scr[pl.ds(row, 1), :] += jnp.sum(term, axis=0, keepdims=True)

    @pl.when(step == pl.num_programs(0) - 1)
    def _():
        totals = jnp.sum(s_scr[...], axis=1, keepdims=True)
        lane = lax.broadcasted_iota(jnp.int32, sum_ref.shape, 1)
        sum_ref[...] = jnp.where(
            lane == 0, totals[0:1], jnp.where(lane == 1, totals[1:2], totals[2:3])
        )


def velocity(branch, attended, weight, hidden, hidden_other, reward, down, up, copies):
    tokens, half = hidden_other.shape
    depth, rank = down.shape
    tile = 512
    steps = half // tile
    mine = lambda j, b: (0, b[0] * steps + j)
    return pl.pallas_call(
        velocity_kernel,
        grid_spec=pltpu.PrefetchScalarGridSpec(
            num_scalar_prefetch=1,
            grid=(steps,),
            in_specs=[
                pl.BlockSpec(attended.shape, lambda j, b: (0, 0, 0, 0)),
                pl.BlockSpec((depth, tile), lambda j, b: (0, j)),
                pl.BlockSpec((tokens, tile), mine),
                pl.BlockSpec((tokens, tile), lambda j, b: (0, j)),
                pl.BlockSpec((tokens, tile), mine),
                pl.BlockSpec((depth, rank), lambda j, b: (0, 0)),
                pl.BlockSpec((rank, tile), mine),
            ],
            out_specs=[
                pl.BlockSpec((2, tokens, tile), lambda j, b: (0, 0, j)),
                pl.BlockSpec((2, tokens, rank), lambda j, b: (0, 0, 0)),
                pl.BlockSpec((8 * copies, 128), lambda j, b: (0, 0)),
            ],
            scratch_shapes=[
                pltpu.VMEM((2 * tokens, depth), BF16),
                pltpu.VMEM((2 * tokens, rank), BF16),
                pltpu.VMEM((8, tile), F32),
            ],
        ),
        out_shape=[
            jax.ShapeDtypeStruct((2, tokens, half), BF16),
            jax.ShapeDtypeStruct((2, tokens, rank), BF16),
            jax.ShapeDtypeStruct((8 * copies, 128), F32),
        ],
        compiler_params=params(),
        cost_estimate=pl.CostEstimate(
            flops=4 * tokens * depth * half,
            bytes_accessed=2 * depth * half,
            transcendentals=0,
        ),
    )(branch, attended, weight, hidden, hidden_other, reward, down, up)


def gradient_kernel(
    b_ref, v_ref, r_ref, sum_ref, w_ref, down_ref, up_ref,
    own_ref, oth_ref, mid_ref, g_ref, x_scr, m_scr,
):
    tokens = r_ref.shape[0]

    @pl.when(pl.program_id(0) == 0)
    def _():
        totals = sum_ref[0:1, :]
        for at in range(8, sum_ref.shape[0], 8):
            totals = totals + sum_ref[at : at + 1, :]
        inner, energy, pull = totals[:, 0:1], totals[:, 1:2] + 1e-08, totals[:, 2:3]
        scale = inner / energy
        slope = (1.0 - GUIDANCE) * pull / energy
        first = b_ref[0] == 0
        tile = 512
        for at in range(0, r_ref.shape[1], tile):
            cols = pl.ds(at, tile)
            target = r_ref[:, cols].astype(F32)
            cond = v_ref[0, :, cols].astype(F32)
            uncond = v_ref[1, :, cols].astype(F32)
            grad0 = (GUIDANCE * target + slope * uncond).astype(BF16)
            grad1 = (
                ((1.0 - GUIDANCE) * scale) * target
                + slope * cond
                + (-2.0 * slope * scale) * uncond
            ).astype(BF16)
            x_scr[0:tokens, cols] = grad0
            x_scr[tokens : 2 * tokens, cols] = grad1
            own_ref[:, cols] = jnp.where(first, grad0, grad1)
            oth_ref[:, cols] = jnp.where(first, grad1, grad0)
        mid = dot(x_scr[...], up_ref[...], LAST).astype(BF16)
        m_scr[...] = mid
        mid_ref[...] = mid.reshape(mid_ref.shape)

    part = dot(x_scr[...], w_ref[...], LAST) + dot(m_scr[...], down_ref[...], LAST)
    g_ref[...] = part.astype(BF16).reshape(g_ref.shape)


def gradient(branch, vel, reward, sums, weight, down, up, parts):
    _, tokens, half = vel.shape
    depth, rank = down.shape
    wide = depth // parts
    whole = lambda j, b: (0, 0)
    mine = lambda j, b: (0, b[0])
    return pl.pallas_call(
        gradient_kernel,
        grid_spec=pltpu.PrefetchScalarGridSpec(
            num_scalar_prefetch=1,
            grid=(parts,),
            in_specs=[
                pl.BlockSpec((2, tokens, half), lambda j, b: (0, 0, 0)),
                pl.BlockSpec((tokens, half), mine),
                pl.BlockSpec(sums.shape, whole),
                pl.BlockSpec((wide, half), lambda j, b: (j, 0)),
                pl.BlockSpec((wide, rank), lambda j, b: (j, 0)),
                pl.BlockSpec((rank, half), mine),
            ],
            out_specs=[
                pl.BlockSpec((tokens, half), whole),
                pl.BlockSpec((tokens, half), whole),
                pl.BlockSpec((2, tokens, rank), lambda j, b: (0, 0, 0)),
                pl.BlockSpec((2, 1, tokens, wide), lambda j, b: (0, j, 0, 0)),
            ],
            scratch_shapes=[
                pltpu.VMEM((2 * tokens, half), BF16),
                pltpu.VMEM((2 * tokens, rank), BF16),
            ],
        ),
        out_shape=[
            jax.ShapeDtypeStruct((tokens, half), BF16),
            jax.ShapeDtypeStruct((tokens, half), BF16),
            jax.ShapeDtypeStruct((2, tokens, rank), BF16),
            jax.ShapeDtypeStruct((2, parts, tokens, wide), BF16),
        ],
        compiler_params=params(),
        cost_estimate=pl.CostEstimate(
            flops=4 * tokens * depth * half,
            bytes_accessed=2 * depth * half,
            transcendentals=0,
        ),
    )(branch, vel, reward, sums, weight, down, up)


def exchange(block, axes):
    return lax.all_to_all(block, axes, split_axis=0, concat_axis=0, tiled=True)


def swap(block):
    return lax.ppermute(block, "branch", [(0, 1), (1, 0)])


def body(
    hidden,
    query,
    key,
    value,
    output_projection_weight,
    adapter_down_weight,
    adapter_up_weight,
    reward_gradient,
):
    parts = lax.axis_size("ulysses")
    clips = lax.axis_size("fsdp")
    branch = lax.axis_index("branch")
    branch_word = branch.reshape(1).astype(jnp.int32)
    _, _, tokens, model = hidden.shape
    half = model // 2
    _, _, seq, width = query.shape
    depth, rank = adapter_down_weight.shape
    query2, key2, value2 = (a.reshape(seq, width) for a in (query, key, value))
    hidden2 = hidden.reshape(tokens, model)
    reward2 = reward_gradient.reshape(tokens, model)

    own_columns = lax.dynamic_slice_in_dim(output_projection_weight, branch * half, half, 1)
    weight = lax.all_gather(own_columns, "fsdp", axis=0, tiled=True)
    hidden_other = swap(lax.dynamic_slice_in_dim(hidden2, (1 - branch) * half, half, 1))

    probs, attended = attention_forward(query2, key2, value2, parts)
    gathered = exchange(attended.reshape(2 * seq, width), ("branch", "ulysses"))
    gathered = gathered.reshape(2, parts, tokens, width)

    vel, middle, sums = velocity(
        branch_word, gathered, weight, hidden2, hidden_other, reward2,
        adapter_down_weight, adapter_up_weight, 2 * parts,
    )
    sums = exchange(sums, ("branch", "ulysses"))
    grad_own, grad_other, grad_middle, grad_part = gradient(
        branch_word, vel, reward2, sums, weight, adapter_down_weight, adapter_up_weight, parts
    )
    grads = exchange(grad_part.reshape(2 * seq, width), ("branch", "ulysses"))
    grads = grads.reshape(2, parts, tokens, width)

    down_part = jnp.einsum("btk,butf->kuf", grad_middle, gathered, preferred_element_type=F32)
    mine = lax.dynamic_index_in_dim(middle, branch, 0, keepdims=False)
    other = lax.dynamic_index_in_dim(middle, 1 - branch, 0, keepdims=False)
    up_part = dot(mine, grad_own, FIRST) + dot(other, grad_other, FIRST)
    both = jnp.concatenate([down_part.reshape(rank, depth), up_part], axis=0).astype(BF16)
    group = 8
    rows = 2 * rank // group
    lanes = parts * clips // rows
    piece = half // lanes
    both = both.reshape(rows, group, lanes, piece).transpose(0, 2, 1, 3)
    both = exchange(both.reshape(rows * lanes * group, piece), ("ulysses", "fsdp"))
    total = jnp.sum(both.reshape(rows * lanes, group, piece).astype(F32), axis=0)
    partner = swap(total)
    cond_total = jnp.where(branch == 0, total, partner)
    uncond_total = jnp.where(branch == 0, partner, total)
    packed = jnp.concatenate([cond_total, uncond_total], axis=0).astype(BF16)
    packed = jnp.broadcast_to(packed[None], (rows * lanes, 2 * group, piece))
    packed = exchange(packed.reshape(rows * lanes * 2 * group, piece), ("ulysses", "fsdp"))
    packed = packed.reshape(rows, lanes, 2, group, piece).transpose(2, 0, 3, 1, 4)
    packed = packed.reshape(2, 2 * rank, half).astype(F32)
    adapter_down_gradient = (packed[0, :rank] + packed[1, :rank]).T
    adapter_up_gradient = jnp.concatenate([packed[0, rank:], packed[1, rank:]], axis=1)

    received = swap(grad_other)
    grad_hidden = jnp.where(
        branch == 0,
        jnp.concatenate([grad_own, received], axis=1),
        jnp.concatenate([received, grad_own], axis=1),
    )
    grad_query, grad_key, grad_value = attention_backward(
        probs, query2, key2, value2, attended, grads
    )
    return (
        grad_hidden.reshape(hidden.shape),
        grad_query.reshape(query.shape),
        grad_key.reshape(key.shape),
        grad_value.reshape(value.shape),
        adapter_down_gradient,
        adapter_up_gradient,
    )


def solution(mesh):
    in_specs = (
        P("branch", "fsdp", "ulysses", None),
        P("branch", "fsdp", None, "ulysses"),
        P("branch", "fsdp", None, "ulysses"),
        P("branch", "fsdp", None, "ulysses"),
        P("fsdp", None),
        P(),
        P(),
        P("fsdp", "ulysses", None),
    )
    out_specs = (
        P("branch", "fsdp", "ulysses", None),
        P("branch", "fsdp", None, "ulysses"),
        P("branch", "fsdp", None, "ulysses"),
        P("branch", "fsdp", None, "ulysses"),
        P(),
        P(),
    )
    return jax.shard_map(body, mesh=mesh, in_specs=in_specs, out_specs=out_specs, check_vma=False)
```

time: 444 us -> 321 us (0.72)
  matrix products: 101 us -> 4.02 us
  local copies, waits for them, and re-layouts: 103 us -> 16.6 us
  Pallas kernels: 0 us -> 62.1 us
  blocking collectives: 30.4 us -> 66.1 us
  other arithmetic: 34.2 us -> 6.05 us
  waiting for transfers between devices: 149 us -> 129 us
  starting transfers between devices: 7.54 us -> 22 us
    dot_general x38 -> x3, matrix products: 101 us -> 4.02 us  [the longest x2 2.16 us: dot(): return lax.dot_general(a, b, dims, preferred_element_type=F32)]
    all_gather x1, waiting for transfers between devices: 64.4 us -> 0.01 us  [body(): weight = lax.all_gather(own_columns, 'fsdp', axis=0, tiled=True)]
    pallas_call x0 -> x4, Pallas kernels: none -> 62.1 us  [the longest x1 16.3 us: attention_forward(): pl.pallas_call(forward_kernel, grid=(heads,), in_specs=[block] * 3, out_s...]
    dynamic_slice x20 -> x2, local copies, waits for them, and re-layouts: 56.3 us -> 3.45 us  [the longest x1 2.51 us: body(): lax.dynamic_slice_in_dim(hidden2, (1 - branch) * half, half, 1)]
    ppermute x1 -> x3, waiting for transfers between devices: 57.1 us -> 105 us  [swap(): return lax.ppermute(block, 'branch', [(0, 1), (1, 0)])]
    all_to_all x1 -> x2, blocking collectives: 21.3 us -> 66.1 us  [exchange(): return lax.all_to_all(block, axes, split_axis=0, concat_axis=0, tiled=True)]
    psum x1 -> x0, waiting for transfers between devices: 16.7 us -> none  [body(): lax.psum((local_down_weight, local_up_weight), ('branch', 'ulysses', 'fsd...]
    reduce_sum x11 -> x1, other arithmetic: 14.8 us -> 0.12 us  [body(): jnp.sum(both.reshape(rows * lanes, group, piece).astype(F32), axis=0)]
  transfers between devices with their start and end apart: 4 -> 7, of which waited for: 4 -> 4; matrix products, arithmetic and copies ran while one was open for 42% -> 6% of each run, Pallas kernels for 0% -> 5%
where the time goes in v1:
time: 321 us; the launch traced here: 320 us
  waiting for transfers between devices  129 us (40%)
  blocking collectives  66.1 us (21%)
  Pallas kernels  62.1 us (19%)
  starting transfers between devices  22 us (7%)
  local copies, waits for them, and re-layouts  16.6 us (5%)
  between operations  14.2 us (4%)
  other arithmetic  6.05 us (2%)
  matrix products  4.02 us (1%)
    ppermute x3, waiting for transfers between devices, swap(): return lax.ppermute(block, 'branch', [(0, 1), (1, 0)])  105 us
    all_to_all x2, blocking collectives, exchange(): return lax.all_to_all(block, axes, split_axis=0, concat_axis=0, tiled=True)  66.1 us
    all_to_all x3, waiting for transfers between devices, exchange(): return lax.all_to_all(block, axes, split_axis=0, concat_axis=0, tiled=True)  24.1 us
    pallas_call x1, Pallas kernels, attention_forward(): pl.pallas_call(forward_kernel, grid=(heads,), in_specs=[block] * 3, out_s...  16.3 us
    all_to_all x3, starting transfers between devices, exchange(): return lax.all_to_all(block, axes, split_axis=0, concat_axis=0, tiled=True)  15.9 us
    pallas_call x1, Pallas kernels, attention_backward(): pl.pallas_call(backward_kernel, grid=(heads,), in_specs=[pl.BlockSpec((1,...  15.6 us
    pallas_call x1, Pallas kernels, gradient(): pl.pallas_call(gradient_kernel, grid_spec=pltpu.PrefetchScalarGridSpec(nu...  15.6 us
    pallas_call x1, Pallas kernels, velocity(): pl.pallas_call(velocity_kernel, grid_spec=pltpu.PrefetchScalarGridSpec(nu...  14.6 us
  transfers between devices with their start and end apart: 7, of which 4 were waited for; matrix products, arithmetic and copies ran while one was open for 6% of the time, Pallas kernels for 5%

profile of v1, /device:TPU:1, one launch (start us, length us, event | category | flops | bytes accessed | tf_op | source)
XLA Modules:
  0.0 319.8 jit_solution(10985675804629441172)
XLA Ops:
  7.2 0.0 copy-start
  7.2 0.0 all-gather.2.cloned.1.call-start
  7.2 1.4 copy-done
  8.6 0.9 constant_dynamic-slice_fusion
  9.5 0.0 all-gather.2.cloned.1.call-update
  9.6 16.3 %shard_map.127 = (bf16[5,1024,1024]{2,1,0:T(8,128)(2,1)}, bf16[2,4,256,640]{3,2,1,0:T(8,128)(2,1)}) custom-call(bf16[1024,640]{1,0:T(8,128)(2,1)} %bitcast.66, bf16[1024,640]{1,0:T(8,128)(2,1)} %bitcast.68, bf16[1024,640]{1,0:T(8,128)(2,1)} %bitcast.70), custom_call_target="tpu_custom_call" | custom-call | flops 5368709120 | bytes 10485760 | tf_op jit(solution)/shard_map/pallas_call | solution.py:45
  25.9 7.5 %all-to-all-start = ((bf16[8,256,640]{2,1,0:T(8,128)(2,1)}), bf16[8,256,640]{2,1,0:T(8,128)(2,1)S(1)}, u32[]{:S(2)}, u32[]{:S(2)}) async-start(bf16[8,256,640]{2,1,0:T(8,128)(2,1)} %bitcast.58), calls=%async_computation | async-start | bytes 5242880 | tf_op jit(solution)/shard_map/all_to_all | solution.py:276
  33.4 0.0 copy-start.4
  33.4 2.5 dynamic-slice_bitcast_fusion
  35.9 3.0 collective-permute-start
  38.9 0.0 copy-done.4
  38.9 1.1 copy.21.down_ref
  40.0 103.6 %collective-permute-done.hoth_ref = bf16[256,2560]{1,0:T(8,128)(2,1)} collective-permute-done((bf16[256,2560]{1,0:T(8,128)(2,1)}, bf16[256,2560]{1,0:T(8,128)(2,1)}, u32[]{:S(2)}, u32[]{:S(2)}) %collective-permute-start) | collective-permute-done | bytes 1310752 | tf_op jit(solution)/shard_map/ppermute | solution.py:280
  143.6 0.0 all-to-all-done
  143.6 0.0 copy-start.2
  143.6 0.0 all-gather.2.cloned.1.call-done.w_ref
  143.6 1.5 copy-done.2
  145.1 14.6 %shard_map.128 = (bf16[2,256,2560]{2,1,0:T(8,128)(2,1)}, bf16[2,256,64]{2,1,0:T(8,128)(2,1)}, f32[64,128]{1,0:T(8,128)}) custom-call(s32[1]{0:T(128)} %bitcast.b_ref, bf16[2,4,256,640]{3,2,1,0:T(8,128)(2,1)} %bitcast.53, bf16[2560,2560]{1,0:T(8,128)(2,1)} %all-gather.2.cloned.1.call-done.w_ref, bf16[256,5120]{1,0:T(8,128)(2,1)} %bitcast.61, ...), custom_call_target="tpu_custom_call" | custom-call | flops 6710886400 | bytes 13107200 | tf_op jit(solution)/shard_map/pallas_call | solution.py:152
  159.8 4.0 %all-to-all-start.1 = ((f32[8,8,128]{2,1,0:T(8,128)}), f32[8,8,128]{2,1,0:T(8,128)S(1)}, u32[]{:S(2)}, u32[]{:S(2)}) async-start(f32[8,8,128]{2,1,0:T(8,128)} %bitcast.63), calls=%async_computation.1 | async-start | bytes 65536 | tf_op jit(solution)/shard_map/all_to_all | solution.py:276
  163.8 3.0 copy.23
  166.7 3.6 %all-to-all-done.1 = f32[8,8,128]{2,1,0:T(8,128)S(1)} async-done(((f32[8,8,128]{2,1,0:T(8,128)}), f32[8,8,128]{2,1,0:T(8,128)S(1)}, u32[]{:S(2)}, u32[]{:S(2)}) %all-to-all-start.1) | async-done | bytes 32800 | tf_op jit(solution)/shard_map/all_to_all | solution.py:276
  170.4 0.0 copy-start.6
  170.4 0.6 copy-done.6
  171.0 15.6 %shard_map.129 = (bf16[256,2560]{1,0:T(8,128)(2,1)}, bf16[256,2560]{1,0:T(8,128)(2,1)}, bf16[2,256,64]{2,1,0:T(8,128)(2,1)}, bf16[2,4,256,640]{3,2,1,0:T(8,128)(2,1)}) custom-call(s32[1]{0:T(128)} %bitcast.b_ref, bf16[2,256,2560]{2,1,0:T(8,128)(2,1)} %get-tuple-element.19.v_ref, bf16[256,5120]{1,0:T(8,128)(2,1)} %bitcast.65, f32[64,128]{1,0:T(8,128)} %bitcast.62, ...), custom_call_target="tpu_custom_call" | custom-call | flops 6710886400 | bytes 13107200 | tf_op jit(solution)/shard_map/pallas_call | solution.py:236
  186.6 0.0 copy-start.5
  186.6 1.9 fusion
  188.4 0.0 copy-start.3
  188.4 0.0 copy-done.5
  188.5 1.8 fusion.3
  190.2 0.0 copy-done.3
  190.3 0.4 fusion.1
  190.7 22.5 %all_to_all.44 = bf16[64,8,640]{2,1,0:T(8,128)(2,1)S(1)} all-to-all(bf16[64,8,640]{2,1,0:T(8,128)(2,1)S(1)} %bitcast.60), channel_id=1, replica_groups=mesh['branch'=2,'ulysses'=4,'fsdp'=16] {'ulysses','fsdp'}, dimensions={0} | all-to-all | bytes 1310720 | tf_op jit(solution)/shard_map/all_to_all | solution.py:276
  213.2 0.1 convert_reduce_fusion
  213.3 1.1 collective-permute-start.2
  214.4 2.0 collective-permute-start.1
  216.4 1.1 collective-permute-done.2
  217.4 0.1 broadcast_in_dim.2
  217.6 43.6 %all_to_all.45 = bf16[64,16,640]{2,1,0:T(8,128)(2,1)S(1)} all-to-all(bf16[64,16,640]{2,1,0:T(8,128)(2,1)S(1)} %broadcast_in_dim.2), channel_id=1, replica_groups=mesh['branch'=2,'ulysses'=4,'fsdp'=16] {'ulysses','fsdp'}, dimensions={0} | all-to-all | bytes 2621440 | tf_op jit(solution)/shard_map/all_to_all | solution.py:276
  261.1 4.4 %all-to-all-start.2 = ((bf16[8,256,640]{2,1,0:T(8,128)(2,1)}), bf16[8,256,640]{2,1,0:T(8,128)(2,1)}, u32[]{:S(2)}, u32[]{:S(2)}) async-start(bf16[8,256,640]{2,1,0:T(8,128)(2,1)} %bitcast.59), calls=%async_computation.2 | async-start | bytes 5242880 | tf_op jit(solution)/shard_map/all_to_all | solution.py:276
  265.5 0.0 collective-permute-done.1
  265.5 3.5 %maximum_select_fusion = bf16[1,1,256,5120]{3,2,1,0:T(8,128)(2,1)} fusion(bf16[1,1,256,2560]{3,2,1,0:T(8,128)(2,1)} %bitcast.12, bf16[1,1,256,2560]{3,2,1,0:T(8,128)(2,1)S(1)} %bitcast.56, pred[]{:T(512)S(6)} %eq.2), kind=kLoop, calls=%fused_computation.4 | loop fusion | flops 11796480 | bytes 5242881 | tf_op jit(solution)/shard_map/jit(_where)/select_n | solution.py:348
  269.0 0.3 convert_bitcast_fusion
  269.3 2.6 copy.25
  271.8 2.9 reshape.163
  274.8 1.0 slice_bitcast_fusion.1
  275.8 1.1 pad_maximum_fusion
  276.9 20.5 %all-to-all-done.2 = bf16[8,256,640]{2,1,0:T(8,128)(2,1)} async-done(((bf16[8,256,640]{2,1,0:T(8,128)(2,1)}), bf16[8,256,640]{2,1,0:T(8,128)(2,1)}, u32[]{:S(2)}, u32[]{:S(2)}) %all-to-all-start.2) | async-done | bytes 2621472 | tf_op jit(solution)/shard_map/all_to_all | solution.py:276
  297.4 0.0 copy-start.1
  297.4 15.6 %shard_map.130 = (bf16[1024,640]{1,0:T(8,128)(2,1)}, bf16[1024,640]{1,0:T(8,128)(2,1)}, bf16[1024,640]{1,0:T(8,128)(2,1)}) custom-call(bf16[5,1024,1024]{2,1,0:T(8,128)(2,1)} %get-tuple-element.23.p_ref, bf16[1024,640]{1,0:T(8,128)(2,1)} %bitcast.67, bf16[1024,640]{1,0:T(8,128)(2,1)} %bitcast.69, bf16[1024,640]{1,0:T(8,128)(2,1)} %bitcast.71, ...), custom_call_target="tpu_custom_call" | custom-call | flops 10737418240 | bytes 10485760 | tf_op jit(solution)/shard_map/pallas_call | solution.py:86
  313.0 0.0 copy-done.1
  (3 shorter events, 0.1 us)
Async XLA Ops:
  7.2 1.4 copy-start
  7.2 136.4 %all-gather.2.cloned.1.call-start = ((), (), s32[]{:S(2)}) async-start(), calls=%async_computation.5 | async-start | bytes 13926400 | tf_op jit(solution)/shard_map/all_gather | solution.py:306
  25.9 117.8 %all-to-all-start = ((bf16[8,256,640]{2,1,0:T(8,128)(2,1)}), bf16[8,256,640]{2,1,0:T(8,128)(2,1)S(1)}, u32[]{:S(2)}, u32[]{:S(2)}) async-start(bf16[8,256,640]{2,1,0:T(8,128)(2,1)} %bitcast.58), calls=%async_computation | async-start | bytes 5242880 | tf_op jit(solution)/shard_map/all_to_all | solution.py:276
  33.4 5.6 %copy-start.4 = (bf16[2560,64]{0,1:T(8,128)(2,1)S(1)}, bf16[2560,64]{0,1:T(8,128)(2,1)}, u32[]{:S(2)}) copy-start(bf16[2560,64]{0,1:T(8,128)(2,1)} %param.13) | copy-start | bytes 983044
  35.9 107.7 %collective-permute-start = (bf16[256,2560]{1,0:T(8,128)(2,1)}, bf16[256,2560]{1,0:T(8,128)(2,1)}, u32[]{:S(2)}, u32[]{:S(2)}) collective-permute-start(bf16[256,2560]{1,0:T(8,128)(2,1)} %dynamic-slice_bitcast_fusion), channel_id=1, source_target_pairs={{0,64},{64,0},{1,65},{65,1},{2,66},{66,2},{3,67},{67,3},{4,68},{68... | collective-permute-start | bytes 3932168 | tf_op jit(solution)/shard_map/ppermute | solution.py:280
  143.6 1.5 copy-start.2
  159.8 10.6 %all-to-all-start.1 = ((f32[8,8,128]{2,1,0:T(8,128)}), f32[8,8,128]{2,1,0:T(8,128)S(1)}, u32[]{:S(2)}, u32[]{:S(2)}) async-start(f32[8,8,128]{2,1,0:T(8,128)} %bitcast.63), calls=%async_computation.1 | async-start | bytes 65536 | tf_op jit(solution)/shard_map/all_to_all | solution.py:276
  170.4 0.6 copy-start.6
  186.6 1.9 copy-start.5
  188.4 1.8 copy-start.3
  213.3 4.1 %collective-permute-start.2 = (bf16[8,640]{1,0:T(8,128)(2,1)S(1)}, bf16[8,640]{1,0:T(8,128)(2,1)S(1)}, u32[]{:S(2)}, u32[]{:S(2)}) collective-permute-start(bf16[8,640]{1,0:T(8,128)(2,1)S(1)} %convert_reduce_fusion), channel_id=1, source_target_pairs={{0,64},{64,0},{1,65},{65,1},{2,66},{66,2},{3,67},{67,3},{4,68},{68... | collective-permute-start | bytes 30728 | tf_op jit(solution)/shard_map/ppermute | solution.py:280
  214.4 51.1 %collective-permute-start.1 = (bf16[256,2560]{1,0:T(8,128)(2,1)}, bf16[256,2560]{1,0:T(8,128)(2,1)}, u32[]{:S(2)}, u32[]{:S(2)}) collective-permute-start(bf16[256,2560]{1,0:T(8,128)(2,1)} %get-tuple-element.22), channel_id=1, source_target_pairs={{0,64},{64,0},{1,65},{65,1},{2,66},{66,2},{3,67},{67,3},{4,68},{68... | collective-permute-start | bytes 3932168 | tf_op jit(solution)/shard_map/ppermute | solution.py:280
  261.1 36.2 %all-to-all-start.2 = ((bf16[8,256,640]{2,1,0:T(8,128)(2,1)}), bf16[8,256,640]{2,1,0:T(8,128)(2,1)}, u32[]{:S(2)}, u32[]{:S(2)}) async-start(bf16[8,256,640]{2,1,0:T(8,128)(2,1)} %bitcast.59), calls=%async_computation.2 | async-start | bytes 5242880 | tf_op jit(solution)/shard_map/all_to_all | solution.py:276
  297.4 15.6 %copy-start.1 = (bf16[160,5120]{1,0:T(8,128)(2,1)S(1)}, bf16[160,5120]{1,0:T(8,128)(2,1)}, u32[]{:S(2)}) copy-start(bf16[160,5120]{1,0:T(8,128)(2,1)} %param.12) | copy-start | bytes 4915204
Sparse Core Ops, SparseCore 0:
  10.3 128.8 all-gather.1

commit v2 on v1

v2 whole, which is shorter than its diff:
```python
import functools

import jax
import jax.numpy as jnp
from jax import lax
from jax.experimental import pallas as pl
from jax.experimental.pallas import tpu as pltpu
from jax.sharding import PartitionSpec as P

HD = 128
GUIDANCE = 5.0
SCALE = HD ** (-0.5)
VMEM = 56 * 1024 * 1024
LAST = (((1,), (1,)), ((), ()))
FIRST = (((0,), (0,)), ((), ()))
F32 = jnp.float32
BF16 = jnp.bfloat16


def lasts(us):
    return pl.CostEstimate(flops=1000, bytes_accessed=int(us * 3.69e6), transcendentals=0)


def dot(a, b, dims=(((1,), (0,)), ((), ()))):
    return lax.dot_general(a, b, dims, preferred_element_type=F32)


def params():
    return pltpu.CompilerParams(vmem_limit_bytes=VMEM)


def forward_kernel(q_ref, k_ref, v_ref, p_ref, o_ref):
    rows = o_ref.shape[2]
    for part in range(o_ref.shape[1]):
        at = pl.ds(part * rows, rows)
        scores = dot(q_ref[at, :], k_ref[...], LAST) * SCALE
        exps = jnp.exp(scores - jnp.max(scores, axis=1, keepdims=True))
        probs = (exps / jnp.sum(exps, axis=1, keepdims=True)).astype(BF16)
        p_ref[0, at, :] = probs
        out = dot(probs, v_ref[...]).astype(BF16)
        o_ref[0, part] = out
        o_ref[1, part] = out


def attention_forward(query, key, value, parts):
    seq, width = query.shape
    heads = width // HD
    block = pl.BlockSpec((seq, HD), lambda h: (0, h))
    return pl.pallas_call(
        forward_kernel,
        grid=(heads,),
        in_specs=[block] * 3,
        out_specs=[
            pl.BlockSpec((1, seq, seq), lambda h: (h, 0, 0)),
            pl.BlockSpec((2, parts, seq // parts, HD), lambda h: (0, 0, 0, h)),
        ],
        out_shape=[
            jax.ShapeDtypeStruct((heads, seq, seq), BF16),
            jax.ShapeDtypeStruct((2, parts, seq // parts, width), BF16),
        ],
        compiler_params=params(),
        cost_estimate=lasts(16),
    )(query, key, value)


def backward_kernel(u_ref, p_ref, q_ref, k_ref, v_ref, o_ref, *refs):
    (*g_refs, dq_ref, dk_ref, dv_ref, g_scr, d_scr) = refs
    parts = len(g_refs) - 1
    rows = g_refs[0].shape[0]
    for ahead in range(parts):
        part = lax.rem(u_ref[0] + (parts - ahead), parts)
        at = pl.ds(pl.multiple_of(part * rows, rows), rows)
        block = g_refs[ahead][...]
        if ahead == 0:
            block = (block.astype(F32) + g_refs[parts][...].astype(F32)).astype(BF16)
        g_scr[at, :] = block
        d_scr[at, :] = jnp.sum(
            block.astype(F32) * o_ref[0, part].astype(F32), axis=1, keepdims=True
        )
    probs = p_ref[0]
    grad = g_scr[...]
    grad_probs = dot(grad, v_ref[...], LAST)
    grad_scores = (probs.astype(F32) * (grad_probs - d_scr[...])).astype(BF16)
    dv_ref[...] = dot(probs, grad, FIRST).astype(BF16)
    dq_ref[...] = (dot(grad_scores, k_ref[...]) * SCALE).astype(BF16)
    dk_ref[...] = (dot(grad_scores, q_ref[...], FIRST) * SCALE).astype(BF16)


def attention_backward(place, probs, query, key, value, out, grads):
    seq, width = query.shape
    heads = width // HD
    parts = out.shape[1]
    block = pl.BlockSpec((seq, HD), lambda h, u: (0, h))
    return pl.pallas_call(
        backward_kernel,
        grid_spec=pltpu.PrefetchScalarGridSpec(
            num_scalar_prefetch=1,
            grid=(heads,),
            in_specs=[
                pl.BlockSpec((1, seq, seq), lambda h, u: (h, 0, 0)),
                block,
                block,
                block,
                pl.BlockSpec((1, parts, seq // parts, HD), lambda h, u: (0, 0, 0, h)),
            ]
            + [pl.BlockSpec((seq // parts, HD), lambda h, u: (0, h))] * (parts + 1),
            out_specs=[block] * 3,
            scratch_shapes=[pltpu.VMEM((seq, HD), BF16), pltpu.VMEM((seq, 1), F32)],
        ),
        out_shape=[jax.ShapeDtypeStruct((seq, width), BF16)] * 3,
        compiler_params=params(),
        cost_estimate=lasts(400),
    )(place, probs, query, key, value, out, *grads)


def weight_rows(w_ref):
    blocks = []
    for z in range(0, w_ref.shape[0], 4):
        blocks += [w_ref[z], w_ref[z + 2], w_ref[z + 1], w_ref[z + 3]]
    return jnp.concatenate(blocks, axis=0)


def velocity_kernel(
    b_ref, x_ref, m_ref, w_ref, hown_ref, hoth_ref, hlate_ref, r_ref, up_ref, v_ref, sum_ref, s_scr
):
    step = pl.program_id(0)
    tokens = hown_ref.shape[0]

    @pl.when(step == 0)
    def _():
        s_scr[...] = jnp.zeros_like(s_scr)

    first = b_ref[0] == 0
    own = hown_ref[...].astype(F32)
    oth = jnp.concatenate([hoth_ref[...], hlate_ref[...]], axis=0).astype(F32)
    acc = dot(x_ref[...], weight_rows(w_ref)) + dot(m_ref[...], up_ref[...])
    cond = (jnp.where(first, own, oth) + acc[:tokens]).astype(BF16)
    uncond = (jnp.where(first, oth, own) + acc[tokens:]).astype(BF16)
    v_ref[0] = cond
    v_ref[1] = uncond
    c32, u32, r32 = cond.astype(F32), uncond.astype(F32), r_ref[...].astype(F32)
    for row, term in enumerate((c32 * u32, u32 * u32, r32 * u32)):
        s_scr[pl.ds(row, 1), :] += jnp.sum(term, axis=0, keepdims=True)

    @pl.when(step == pl.num_programs(0) - 1)
    def _():
        totals = jnp.sum(s_scr[...], axis=1, keepdims=True)
        lane = lax.broadcasted_iota(jnp.int32, sum_ref.shape, 1)
        sum_ref[...] = jnp.where(
            lane == 0, totals[0:1], jnp.where(lane == 1, totals[1:2], totals[2:3])
        )


def velocity(branch, attended, middle, weight, hidden, hidden_other, reward, up, copies):
    half = weight.shape[2]
    tokens = hidden.shape[0]
    blocks, block_rows, _ = weight.shape
    depth, rank = blocks * block_rows, up.shape[0]
    tile = 512
    steps = half // tile
    mine = lambda j, b: (0, b[0] * steps + j)
    return pl.pallas_call(
        velocity_kernel,
        grid_spec=pltpu.PrefetchScalarGridSpec(
            num_scalar_prefetch=1,
            grid=(steps,),
            in_specs=[
                pl.BlockSpec((2 * tokens, depth), lambda j, b: (0, 0)),
                pl.BlockSpec((2 * tokens, rank), lambda j, b: (0, 0)),
                pl.BlockSpec((blocks, block_rows, tile), lambda j, b: (0, 0, j)),
                pl.BlockSpec((tokens, tile), mine),
                pl.BlockSpec((hidden_other[0].shape[0], tile), lambda j, b: (0, j)),
                pl.BlockSpec((hidden_other[1].shape[0], tile), lambda j, b: (0, j)),
                pl.BlockSpec((tokens, tile), mine),
                pl.BlockSpec((rank, tile), mine),
            ],
            out_specs=[
                pl.BlockSpec((2, tokens, tile), lambda j, b: (0, 0, j)),
                pl.BlockSpec((8 * copies, 128), lambda j, b: (0, 0)),
            ],
            scratch_shapes=[pltpu.VMEM((8, tile), F32)],
        ),
        out_shape=[
            jax.ShapeDtypeStruct((2, tokens, half), BF16),
            jax.ShapeDtypeStruct((8 * copies, 128), F32),
        ],
        compiler_params=params(),
        cost_estimate=lasts(14),
    )(branch, attended, middle, weight, hidden, *hidden_other, reward, up)


def guidance_kernel(
    b_ref, v_ref, r_ref, sum_ref, own_ref, oth_ref, *cut_refs
):
    totals = sum_ref[0:1, :]
    for at in range(8, sum_ref.shape[0], 8):
        totals = totals + sum_ref[at : at + 1, :]
    inner, energy, pull = totals[:, 0:1], totals[:, 1:2] + 1e-08, totals[:, 2:3]
    scale = inner / energy
    slope = (1.0 - GUIDANCE) * pull / energy
    first = b_ref[0] == 0
    target = r_ref[...].astype(F32)
    cond = v_ref[0].astype(F32)
    uncond = v_ref[1].astype(F32)
    grad0 = GUIDANCE * target + slope * uncond
    grad1 = (
        ((1.0 - GUIDANCE) * scale) * target
        + slope * cond
        + (-2.0 * slope * scale) * uncond
    )
    own_ref[...] = jnp.where(first, grad0, grad1).astype(BF16)
    other = jnp.where(first, grad1, grad0).astype(BF16)
    oth_ref[...] = other
    at = 0
    for cut_ref in cut_refs:
        cut_ref[...] = other[at : at + cut_ref.shape[0]]
        at += cut_ref.shape[0]


def guidance(branch, vel, reward, sums, cuts):
    _, tokens, half = vel.shape
    tile = 640
    steps = half // tile
    mine = lambda j, b: (0, b[0] * steps + j)
    here = lambda j, b: (0, j)
    return pl.pallas_call(
        guidance_kernel,
        grid_spec=pltpu.PrefetchScalarGridSpec(
            num_scalar_prefetch=1,
            grid=(steps,),
            in_specs=[
                pl.BlockSpec((2, tokens, tile), lambda j, b: (0, 0, j)),
                pl.BlockSpec((tokens, tile), mine),
                pl.BlockSpec(sums.shape, lambda j, b: (0, 0)),
            ],
            out_specs=[
                pl.BlockSpec((tokens, tile), mine),
                pl.BlockSpec((tokens, tile), here),
            ]
            + [pl.BlockSpec((cut, tile), here) for cut in cuts],
        ),
        out_shape=[
            jax.ShapeDtypeStruct((tokens, 2 * half), BF16),
            jax.ShapeDtypeStruct((tokens, half), BF16),
        ]
        + [jax.ShapeDtypeStruct((cut, half), BF16) for cut in cuts],
        compiler_params=params(),
        cost_estimate=lasts(4),
    )(branch, vel, reward, sums)


def adapter_part_kernel(b_ref, own_ref, oth_ref, x_ref, m_ref, up_ref, mid_ref, both_ref, m_scr):
    step = pl.program_id(0)
    tokens, tile = own_ref.shape
    groups = both_ref.shape[0] // 2
    up = up_ref[...]
    own, oth = own_ref[...], oth_ref[...]
    part = dot(jnp.concatenate([own, oth], axis=0), up, LAST)
    own_at = pl.ds(pl.multiple_of(b_ref[0] * tokens, tokens), tokens)
    oth_at = pl.ds(pl.multiple_of((1 - b_ref[0]) * tokens, tokens), tokens)
    up_part = dot(m_ref[own_at, :], own, FIRST) + dot(m_ref[oth_at, :], oth, FIRST)
    up_part = up_part.astype(BF16)
    for row in range(groups):
        both_ref[groups + row, step] = up_part[16 * row : 16 * row + 16]

    @pl.when(step == 0)
    def _():
        m_scr[...] = part

    @pl.when(step > 0)
    def _():
        m_scr[...] += part

    @pl.when(step == pl.num_programs(0) - 1)
    def _():
        mid = m_scr[...].astype(BF16)
        mid_ref[...] = mid
        down_part = dot(mid[:tokens], x_ref[own_at, :], FIRST)
        down_part = (down_part + dot(mid[tokens:], x_ref[oth_at, :], FIRST)).astype(BF16)
        for row in range(groups):
            for lane in range(both_ref.shape[1]):
                both_ref[row, lane] = down_part[
                    16 * row : 16 * row + 16, lane * tile : lane * tile + tile
                ]


def adapter_part(branch, grad_own, grad_other, attended, middle, up):
    tokens, half = grad_other.shape
    rank, depth = up.shape[0], attended.shape[1]
    tile = 640
    steps = half // tile
    whole = lambda j, b: (0, 0)
    mine = lambda j, b: (0, b[0] * steps + j)
    both = (2 * rank // 16, steps, 16, tile)
    return pl.pallas_call(
        adapter_part_kernel,
        grid_spec=pltpu.PrefetchScalarGridSpec(
            num_scalar_prefetch=1,
            grid=(steps,),
            in_specs=[
                pl.BlockSpec((tokens, tile), mine),
                pl.BlockSpec((tokens, tile), lambda j, b: (0, j)),
                pl.BlockSpec((2 * tokens, depth), whole),
                pl.BlockSpec((2 * tokens, rank), whole),
                pl.BlockSpec((rank, tile), mine),
            ],
            out_specs=[
                pl.BlockSpec((2 * tokens, rank), whole),
                pl.BlockSpec(both, lambda j, b: (0, 0, 0, 0)),
            ],
            scratch_shapes=[pltpu.VMEM((2 * tokens, rank), F32)],
        ),
        out_shape=[
            jax.ShapeDtypeStruct((2 * tokens, rank), BF16),
            jax.ShapeDtypeStruct(both, BF16),
        ],
        compiler_params=params(),
        cost_estimate=lasts(5),
    )(branch, grad_own, grad_other, attended, middle, up)


def gradient_kernel(u_ref, b_ref, own_ref, oth_ref, mid_ref, w_ref, down_ref, *refs):
    step = pl.program_id(0)
    tokens = own_ref.shape[0]
    rows = jnp.concatenate([own_ref[...], oth_ref[...]], axis=0)
    part = dot(rows, weight_rows(w_ref), LAST) + dot(mid_ref[...], down_ref[...])
    part = part.astype(BF16)
    *gown_refs, first_ref, rest_ref, near_ref = refs
    last = len(gown_refs) - 1
    for at in range(last + 1):

        @pl.when(step == at)
        def _():
            gown_refs[at][...] = part[:tokens]
            if at == 0:
                first_ref[...] = part[tokens:]
            elif at < last:
                rest_ref[(at - 1) * tokens : at * tokens] = part[tokens:]
            else:
                near_ref[...] = part[tokens:]


def gradient(place, branch, grad_own, grad_other, grad_middle, weight, down_rows, parts):
    tokens, half = grad_other.shape
    blocks, block_rows, _ = weight.shape
    rank, depth = down_rows.shape
    wide = depth // parts
    whole = lambda j, u, b: (0, 0)
    there = lambda j, u: lax.rem(u[0] + 1 + j, parts)
    return pl.pallas_call(
        gradient_kernel,
        grid_spec=pltpu.PrefetchScalarGridSpec(
            num_scalar_prefetch=2,
            grid=(parts,),
            in_specs=[
                pl.BlockSpec((tokens, half), lambda j, u, b: (0, b[0])),
                pl.BlockSpec((tokens, half), whole),
                pl.BlockSpec((2 * tokens, rank), whole),
                pl.BlockSpec(
                    (blocks // parts, block_rows, half), lambda j, u, b: (there(j, u), 0, 0)
                ),
                pl.BlockSpec((rank, wide), lambda j, u, b: (0, there(j, u))),
            ],
            out_specs=[pl.BlockSpec((tokens, wide), whole)] * parts
            + [
                pl.BlockSpec((tokens, wide), whole),
                pl.BlockSpec(((parts - 2) * tokens, wide), whole),
                pl.BlockSpec((tokens, wide), whole),
            ],
        ),
        out_shape=[jax.ShapeDtypeStruct((tokens, wide), BF16)] * parts
        + [
            jax.ShapeDtypeStruct((tokens, wide), BF16),
            jax.ShapeDtypeStruct(((parts - 2) * tokens, wide), BF16),
            jax.ShapeDtypeStruct((tokens, wide), BF16),
        ],
        compiler_params=params(),
        cost_estimate=lasts(14),
    )(place, branch, grad_own, grad_other, grad_middle, weight, down_rows)


def adapter_kernel(p_ref, down_ref, up_ref):
    members, parts, _, rows, tile = p_ref.shape
    half = down_ref.shape[1]
    lanes = half // tile
    groups = parts * members // lanes
    for u in range(parts):
        for c in range(members):
            row, lane = divmod(u * members + c, lanes)
            columns = pl.ds(lane * tile, tile)
            if row < groups // 2:
                both = p_ref[c, u, 0].astype(F32) + p_ref[c, u, 1].astype(F32)
                down_ref[pl.ds(row * rows, rows), columns] = both
            else:
                at = pl.ds((row - groups // 2) * rows, rows)
                for b in range(2):
                    up_ref[at, pl.ds(b * half + lane * tile, tile)] = p_ref[c, u, b].astype(F32)


def adapter(pieces, rank, lanes):
    half = lanes * pieces.shape[4]
    return pl.pallas_call(
        adapter_kernel,
        out_shape=[
            jax.ShapeDtypeStruct((rank, half), F32),
            jax.ShapeDtypeStruct((rank, 2 * half), F32),
        ],
        in_specs=[pl.BlockSpec(memory_space=pltpu.VMEM)],
        out_specs=[pl.BlockSpec(memory_space=pltpu.VMEM)] * 2,
        compiler_params=params(),
        cost_estimate=lasts(3),
    )(pieces)


def exchange(block, axes):
    return lax.all_to_all(block, axes, split_axis=0, concat_axis=0, tiled=True)


def swap(block):
    return lax.ppermute(block, "branch", [(0, 1), (1, 0)])


def ahead_send(block, ahead):
    parts = lax.axis_size("ulysses")
    return lax.ppermute(block, "ulysses", [(u, (u + ahead) % parts) for u in range(parts)])


def send_x(block, step):
    clips = lax.axis_size("fsdp")
    route = []
    for at in range(2 * clips):
        b, f = divmod(at, clips)
        z, rest = divmod(f, 4)
        near, core = divmod(rest, 2)
        x = (b * 2 + near + step) % 4
        route.append((at, (x // 2) * clips + z * 4 + (x % 2) * 2 + core))
    return lax.ppermute(block, ("branch", "fsdp"), route)


def gather_operand(rows, branch, half):
    near = lax.rem(lax.axis_index("fsdp") // 2, 2)
    top = rows.shape[0] // 2
    columns = lambda part, b: lax.dynamic_slice_in_dim(part, b * half, half, 1)
    forward = jnp.where(near == 0, branch, 1 - branch)
    before = send_x(columns(rows[:top], forward), 1)
    after = send_x(columns(rows[top:], 1 - forward), -1)
    beside = jnp.concatenate([before, after], axis=0)
    mine = columns(rows, branch)
    return jnp.where(
        near == 0,
        jnp.concatenate([mine, beside], axis=0),
        jnp.concatenate([beside, mine], axis=0),
    )


def body(
    hidden,
    query,
    key,
    value,
    output_projection_weight,
    adapter_down_weight,
    adapter_up_weight,
    reward_gradient,
):
    parts = lax.axis_size("ulysses")
    clips = lax.axis_size("fsdp")
    branch = lax.axis_index("branch")
    branch_word = branch.reshape(1).astype(jnp.int32)
    place = lax.axis_index("ulysses").reshape(1).astype(jnp.int32)
    _, _, tokens, model = hidden.shape
    half = model // 2
    _, _, seq, width = query.shape
    depth, rank = adapter_down_weight.shape
    query2, key2, value2 = (a.reshape(seq, width) for a in (query, key, value))
    hidden2 = hidden.reshape(tokens, model)
    reward2 = reward_gradient.reshape(tokens, model)

    operand = gather_operand(output_projection_weight, branch, half)
    operand, query2, hidden_ready = lax.optimization_barrier((operand, query2, hidden2))
    weight_groups = [
        [z * 4 + near * 2 + core for z in range(clips // 4) for core in (0, 1)] for near in (0, 1)
    ]
    weight = lax.all_gather(operand, "fsdp", axis=0, tiled=True, axis_index_groups=weight_groups)
    weight = weight.reshape(clips, depth // clips, half)
    hidden_send = lax.dynamic_slice_in_dim(hidden_ready, (1 - branch) * half, half, 1)
    early = 5 * tokens // 8
    hidden_early = swap(hidden_send[:early])

    probs, attended = attention_forward(query2, key2, value2, parts)
    attended, hidden_early = lax.optimization_barrier((attended, hidden_early))
    gathered = exchange(attended.reshape(2 * seq, width), ("branch", "ulysses"))
    gathered, hidden_send = lax.optimization_barrier((gathered, hidden_send))
    hidden_late = swap(hidden_send[early:])
    gathered = gathered.reshape(2, parts, tokens, width).transpose(0, 2, 1, 3)
    gathered = gathered.reshape(2 * tokens, depth)
    middle = dot(gathered, adapter_down_weight).astype(BF16)

    vel, sums = velocity(
        branch_word, gathered, middle, weight, hidden2, (hidden_early, hidden_late), reward2,
        adapter_up_weight, 2 * parts,
    )
    sums = exchange(sums, ("branch", "ulysses"))
    cuts = (3 * tokens // 8, 7 * tokens // 16, 3 * tokens // 16)
    grad_hidden, grad_other, *pieces_out = guidance(branch_word, vel, reward2, sums, cuts)
    received = [swap(pieces_out[0])]
    grad_middle, both = adapter_part(
        branch_word, grad_hidden, grad_other, gathered, middle, adapter_up_weight
    )

    groups = [
        [u * clips + z * 4 + near * 2 + core for u in range(parts) for z in range(clips // 4) for core in (0, 1)]
        for near in (0, 1)
    ]
    spread = lambda block: lax.all_to_all(
        block, ("ulysses", "fsdp"), split_axis=0, concat_axis=0, tiled=True, axis_index_groups=groups
    )
    row_groups, lanes, rows, tile = both.shape
    pieces = row_groups * lanes
    both = spread(both.reshape(pieces * rows, tile))
    grad_other, pieces_out[1], received[0] = lax.optimization_barrier(
        (grad_other, pieces_out[1], received[0])
    )
    received.append(swap(pieces_out[1]))

    down_rows = adapter_down_weight.T
    *grads, far_first, far, close = gradient(
        place, branch_word, grad_hidden, grad_other, grad_middle, weight, down_rows, parts
    )
    both, pieces_out[2], received[1], grads[3] = lax.optimization_barrier(
        (both.reshape(pieces, rows, tile), pieces_out[2], received[1], grads[3])
    )
    far_first = swap(far_first)
    total = jnp.sum(both.astype(F32), axis=0)
    beside = [send_x(total, step) for step in (1, 2, 3)]
    far, far_first, *beside = lax.optimization_barrier((far, far_first, *beside))
    far = swap(far)
    far, close = lax.optimization_barrier((far, close))
    close = swap(close)
    far = far.reshape(parts - 2, tokens, width)
    halves = [far_first] + [far[at] for at in range(parts - 2)]
    routed = [
        ahead_send((grads[at].astype(F32) + block.astype(F32)).astype(BF16), at + 1)
        for at, block in enumerate(halves)
    ]
    close, pieces_out[2] = lax.optimization_barrier((close, pieces_out[2]))
    received.append(swap(pieces_out[2]))
    near = lax.rem(lax.axis_index("fsdp") // 2, 2)
    own_total = total + jnp.where(near == 0, beside[2], beside[0])
    other_total = beside[1] + jnp.where(near == 0, beside[0], beside[2])
    total = jnp.where(
        branch == 0,
        jnp.concatenate([own_total, other_total]),
        jnp.concatenate([other_total, own_total]),
    ).astype(BF16)
    ring = [total] + [ahead_send(total, ahead) for ahead in range(1, parts)]
    ring = jnp.concatenate(ring[::-1] * 2, axis=0)
    column = lax.dynamic_slice_in_dim(
        ring, (parts - 1 - place[0]) * 2 * rows, parts * 2 * rows, 0
    )
    grads = [grads[parts - 1]] + routed + [close]
    packed = lax.all_gather(column, "fsdp", axis=0, tiled=True, axis_index_groups=weight_groups)
    down_gradient_rows, adapter_up_gradient = adapter(
        packed.reshape(clips // 2, parts, 2, rows, tile), rank, lanes
    )

    grad_query, grad_key, grad_value = attention_backward(
        place, probs, query2, key2, value2, attended, grads
    )
    received = jnp.concatenate(received, axis=0)
    grad_hidden = lax.dynamic_update_slice_in_dim(grad_hidden, received, (1 - branch) * half, 1)
    return (
        grad_hidden.reshape(hidden.shape),
        grad_query.reshape(query.shape),
        grad_key.reshape(key.shape),
        grad_value.reshape(value.shape),
        down_gradient_rows.T,
        adapter_up_gradient,
    )


def solution(mesh):
    in_specs = (
        P("branch", "fsdp", "ulysses", None),
        P("branch", "fsdp", None, "ulysses"),
        P("branch", "fsdp", None, "ulysses"),
        P("branch", "fsdp", None, "ulysses"),
        P("fsdp", None),
        P(),
        P(),
        P("fsdp", "ulysses", None),
    )
    out_specs = (
        P("branch", "fsdp", "ulysses", None),
        P("branch", "fsdp", None, "ulysses"),
        P("branch", "fsdp", None, "ulysses"),
        P("branch", "fsdp", None, "ulysses"),
        P(),
        P(),
    )
    return jax.shard_map(body, mesh=mesh, in_specs=in_specs, out_specs=out_specs, check_vma=False)
```

time: 321 us -> 245 us (0.76)
  blocking collectives: 66.1 us -> 12.8 us
  waiting for transfers between devices: 129 us -> 82.1 us
  starting transfers between devices: 22 us -> 39 us
  Pallas kernels: 62.1 us -> 76.2 us
  local copies, waits for them, and re-layouts: 16.6 us -> 12.7 us
    ppermute x3 -> x8, waiting for transfers between devices: 105 us -> 31.3 us  [swap(): return lax.ppermute(block, 'branch', [(0, 1), (1, 0)])]
    all_to_all x2 -> x1, blocking collectives: 66.1 us -> 12.8 us  [exchange(): return lax.all_to_all(block, axes, split_axis=0, concat_axis=0, tiled=True)]
    ppermute x0 -> x11, waiting for transfers between devices: none -> 21.5 us  [the longest x5 11 us: send_x(): return lax.ppermute(block, ('branch', 'fsdp'), route)]
    pallas_call x1 -> x4, Pallas kernels: 15.6 us -> 32.1 us  [the longest x1 16.2 us: attention_backward(): pl.pallas_call(backward_kernel, grid_spec=pltpu.PrefetchScalarGridSpec(nu...]
    ppermute x0 -> x11, starting transfers between devices: none -> 13.7 us  [the longest x5 8.17 us: send_x(): return lax.ppermute(block, ('branch', 'fsdp'), route)]
    all_to_all x3 -> x1, starting transfers between devices: 15.9 us -> 6.25 us  [exchange(): return lax.all_to_all(block, axes, split_axis=0, concat_axis=0, tiled=True)]
    all_to_all x0 -> x1, starting transfers between devices: none -> 8.94 us  [body(): lax.all_to_all(block, ('ulysses', 'fsdp'), split_axis=0, concat_axis=0, t...]
    convert_element_type x2 -> x0, local copies, waits for them, and re-layouts: 5.48 us -> none  [body(): packed = packed.reshape(2, 2 * rank, half).astype(F32)]
  transfers between devices with their start and end apart: 7 -> 23, of which waited for: 4 -> 12; matrix products, arithmetic and copies ran while one was open for 6% -> 4% of each run, Pallas kernels for 5% -> 22%
where the time goes in v2:
time: 245 us; the launch traced here: 242 us
  waiting for transfers between devices  82.1 us (34%)
  Pallas kernels  76.2 us (31%)
  starting transfers between devices  39 us (16%)
  between operations  14.3 us (6%)
  blocking collectives  12.8 us (5%)
  local copies, waits for them, and re-layouts  12.7 us (5%)
  other arithmetic  2.99 us (1%)
    ppermute x8, waiting for transfers between devices, swap(): return lax.ppermute(block, 'branch', [(0, 1), (1, 0)])  31.3 us
    all_to_all x1, waiting for transfers between devices, exchange(): return lax.all_to_all(block, axes, split_axis=0, concat_axis=0, tiled=True)  29.3 us
    pallas_call x1, Pallas kernels, attention_forward(): pl.pallas_call(forward_kernel, grid=(heads,), in_specs=[block] * 3, out_s...  16.3 us
    pallas_call x1, Pallas kernels, attention_backward(): pl.pallas_call(backward_kernel, grid_spec=pltpu.PrefetchScalarGridSpec(nu...  16.2 us
    pallas_call x1, Pallas kernels, gradient(): pl.pallas_call(gradient_kernel, grid_spec=pltpu.PrefetchScalarGridSpec(nu...  14.1 us
    pallas_call x1, Pallas kernels, velocity(): pl.pallas_call(velocity_kernel, grid_spec=pltpu.PrefetchScalarGridSpec(nu...  13.7 us
    all_to_all x1, blocking collectives, exchange(): return lax.all_to_all(block, axes, split_axis=0, concat_axis=0, tiled=True)  12.8 us
    ppermute x5, waiting for transfers between devices, send_x(): return lax.ppermute(block, ('branch', 'fsdp'), route)  11 us
  transfers between devices with their start and end apart: 23, of which 12 were waited for; matrix products, arithmetic and copies ran while one was open for 4% of the time, Pallas kernels for 22%

profile of v2, /device:TPU:1, one launch (start us, length us, event | category | flops | bytes accessed | tf_op | source)
XLA Modules:
  0.0 241.6 jit_solution(10071917043261959441)
XLA Ops:
  7.2 0.0 all-gather.3.cloned.1.call-start
  7.2 1.6 fusion.2
  8.9 0.8 constant_dynamic-slice_fusion.4
  9.6 2.0 collective-permute-start
  11.7 1.3 collective-permute-start.1
  13.1 0.1 constant_dynamic-slice_fusion.5
  13.1 8.8 %collective-permute-done = bf16[80,2560]{1,0:T(8,128)(2,1)S(1)} collective-permute-done((bf16[80,2560]{1,0:T(8,128)(2,1)}, bf16[80,2560]{1,0:T(8,128)(2,1)S(1)}, u32[]{:S(2)}, u32[]{:S(2)}) %collective-permute-start) | collective-permute-done | bytes 409632 | tf_op jit(solution)/shard_map/ppermute | solution.py:437
  21.9 1.5 maximum_select_fusion
  23.4 0.0 all-gather.3.cloned.1.call-update
  23.4 1.2 constant_dynamic-slice_fusion
  24.7 2.4 %collective-permute-start.2 = (bf16[160,2560]{1,0:T(8,128)(2,1)S(1)}, bf16[160,2560]{1,0:T(8,128)(2,1)S(1)}, u32[]{:S(2)}, u32[]{:S(2)}) collective-permute-start(bf16[160,2560]{1,0:T(8,128)(2,1)S(1)} %constant_dynamic-slice_fusion), channel_id=1, source_target_pairs={{0,64},{64,0},{1,65},{65,1},{2,66},{66,2},{3,67},{67,3},{4,68},{68... | collective-permute-start | bytes 2457608 | tf_op jit(solution)/shard_map/ppermute | solution.py:420
  27.1 16.3 %shard_map.127 = (bf16[5,1024,1024]{2,1,0:T(8,128)(2,1)}, bf16[2,4,256,640]{3,2,1,0:T(8,128)(2,1)}) custom-call(bf16[1024,640]{1,0:T(8,128)(2,1)} %bitcast.46, bf16[1024,640]{1,0:T(8,128)(2,1)} %bitcast.48, bf16[1024,640]{1,0:T(8,128)(2,1)} %bitcast.50), custom_call_target="tpu_custom_call" | custom-call | flops 1000 | bytes 59040000 | tf_op jit(solution)/shard_map/pallas_call | solution.py:49
  43.3 0.9 collective-permute-done.2.hoth_ref
  44.2 0.9 copy-done.4
  45.1 6.3 %all-to-all-start = ((bf16[8,256,640]{2,1,0:T(8,128)(2,1)}), bf16[8,256,640]{2,1,0:T(8,128)(2,1)S(1)}, u32[]{:S(2)}, u32[]{:S(2)}) async-start(bf16[8,256,640]{2,1,0:T(8,128)(2,1)} %bitcast.42), calls=%async_computation | async-start | bytes 5242880 | tf_op jit(solution)/shard_map/all_to_all | solution.py:416
  51.4 2.6 %constant_dynamic-slice_fusion.2 = bf16[256,2560]{1,0:T(8,128)(2,1)} fusion(bf16[256,5120]{1,0:T(8,128)(2,1)} %bitcast.44, s32[]{:T(128)S(6)} %select_n.60), kind=kLoop, calls=%fused_computation.22 | loop fusion | bytes 2621444 | tf_op jit(solution)/shard_map/dynamic_slice | solution.py:486
  53.9 29.3 %all-to-all-done = bf16[8,256,640]{2,1,0:T(8,128)(2,1)S(1)} async-done(((bf16[8,256,640]{2,1,0:T(8,128)(2,1)}), bf16[8,256,640]{2,1,0:T(8,128)(2,1)S(1)}, u32[]{:S(2)}, u32[]{:S(2)}) %all-to-all-start) | async-done | bytes 2621472 | tf_op jit(solution)/shard_map/all_to_all | solution.py:416
  83.2 1.1 slice.23
  84.3 2.8 %collective-permute-start.3 = (bf16[96,2560]{1,0:T(8,128)(2,1)S(1)}, bf16[96,2560]{1,0:T(8,128)(2,1)}, u32[]{:S(2)}, u32[]{:S(2)}) collective-permute-start(bf16[96,2560]{1,0:T(8,128)(2,1)S(1)} %slice.23), channel_id=1, source_target_pairs={{0,64},{64,0},{1,65},{65,1},{2,66},{66,2},{3,67},{67,3},{4,68},{68... | collective-permute-start | bytes 1474568 | tf_op jit(solution)/shard_map/ppermute | solution.py:420
  87.0 2.0 copy.15
  89.1 0.4 copy.18
  89.5 0.5 copy-done.9
  90.1 1.5 convolution_convert_fusion.m_ref
  91.5 6.0 %collective-permute-done.3.hlate_ref = bf16[96,2560]{1,0:T(8,128)(2,1)} collective-permute-done((bf16[96,2560]{1,0:T(8,128)(2,1)S(1)}, bf16[96,2560]{1,0:T(8,128)(2,1)}, u32[]{:S(2)}, u32[]{:S(2)}) %collective-permute-start.3) | collective-permute-done | bytes 491552 | tf_op jit(solution)/shard_map/ppermute | solution.py:420
  97.6 13.7 %shard_map.128 = (bf16[2,256,2560]{2,1,0:T(8,128)(2,1)}, f32[64,128]{1,0:T(8,128)}) custom-call(s32[1]{0:T(128)} %bitcast.b_ref, bf16[512,2560]{1,0:T(8,128)(2,1)} %bitcast.35, bf16[512,64]{1,0:T(8,128)(2,1)} %convolution_convert_fusion.m_ref, bf16[16,160,2560]{2,1,0:T(8,128)(2,1)} %bitcast.32, bf16[256,5120]{1,0:T(8,128)(2,1)} %bitcast.45, ...), custom_call_target="tpu_custom_call" | custom-call | flops 1000 | bytes 51660000 | tf_op jit(solution)/shard_map/pallas_call | solution.py:162
  111.3 12.8 %all_to_all.32 = f32[8,8,128]{2,1,0:T(8,128)} all-to-all(f32[8,8,128]{2,1,0:T(8,128)} %bitcast.56), channel_id=1, replica_groups=mesh['branch'=2,'ulysses'=4,'fsdp'=16] {'branch','ulysses'}, dimensions={0} | all-to-all | bytes 65536 | tf_op jit(solution)/shard_map/all_to_all | solution.py:416
  124.0 6.2 %shard_map.129 = (bf16[256,5120]{1,0:T(8,128)(2,1)}, bf16[256,2560]{1,0:T(8,128)(2,1)}, bf16[96,2560]{1,0:T(8,128)(2,1)}, bf16[112,2560]{1,0:T(8,128)(2,1)}, bf16[48,2560]{1,0:T(8,128)(2,1)}) custom-call(s32[1]{0:T(128)} %bitcast.b_ref, bf16[2,256,2560]{2,1,0:T(8,128)(2,1)} %get-tuple-element.60.v_ref, bf16[256,5120]{1,0:T(8,128)(2,1)} %bitcast.38, ...), custom_call_target="tpu_custom_call" | custom-call | flops 1000 | bytes 14760000 | tf_op jit(solution)/shard_map/pallas_call | solution.py:226
  130.2 0.4 collective-permute-start.4
  130.6 6.1 %shard_map.130 = (bf16[512,64]{1,0:T(8,128)(2,1)}, bf16[8,4,16,640]{3,2,1,0:T(8,128)(2,1)}) custom-call(s32[1]{0:T(128)} %bitcast.b_ref, bf16[256,5120]{1,0:T(8,128)(2,1)} %get-tuple-element.62.own_ref, bf16[256,2560]{1,0:T(8,128)(2,1)} %get-tuple-element.70.oth_ref, bf16[512,2560]{1,0:T(8,128)(2,1)} %bitcast.36, ...), custom_call_target="tpu_custom_call" | custom-call | flops 1000 | bytes 18450000 | tf_op jit(solution)/shard_map/pallas_call | solution.py:295
  136.7 8.9 %all-to-all-start.2 = ((bf16[32,16,640]{2,1,0:T(8,128)(2,1)}), bf16[32,16,640]{2,1,0:T(8,128)(2,1)S(1)}, u32[]{:S(2)}, u32[]{:S(2)}) async-start(bf16[32,16,640]{2,1,0:T(8,128)(2,1)} %bitcast.53), calls=%async_computation.2 | async-start | bytes 1310720 | tf_op jit(solution)/shard_map/all_to_all | solution.py:515
  145.7 0.0 all-gather.5.cloned.1.call-start
  145.8 2.9 %collective-permute-start.5 = (bf16[112,2560]{1,0:T(8,128)(2,1)S(1)}, bf16[112,2560]{1,0:T(8,128)(2,1)S(1)}, u32[]{:S(2)}, u32[]{:S(2)}) collective-permute-start(bf16[112,2560]{1,0:T(8,128)(2,1)S(1)} %copy-done.14), channel_id=1, source_target_pairs={{0,64},{64,0},{1,65},{65,1},{2,66},{66,2},{3,67},{67,3},{4,68},{68... | collective-permute-start | bytes 1720328 | tf_op jit(solution)/shard_map/ppermute | solution.py:420
  148.7 14.1 %shard_map.131 = (bf16[256,640]{1,0:T(8,128)(2,1)}, bf16[256,640]{1,0:T(8,128)(2,1)}, bf16[256,640]{1,0:T(8,128)(2,1)}, bf16[256,640]{1,0:T(8,128)(2,1)}, bf16[2...) custom-call(s32[1]{0:T(128)} %bitcast.15.u_ref, s32[1]{0:T(128)} %bitcast.b_ref, ...), custom_call_target="tpu_custom_call" | custom-call | flops 1000 | bytes 51660000 | tf_op jit(solution)/shard_map/pallas_call | solution.py:350
  162.8 0.4 collective-permute-start.6
  163.2 0.1 convert_reduce_fusion
  163.3 0.8 collective-permute-start.7
  164.1 3.3 %collective-permute-start.8 = (f32[16,640]{1,0:T(8,128)S(1)}, f32[16,640]{1,0:T(8,128)S(1)}, u32[]{:S(2)}, u32[]{:S(2)}) collective-permute-start(f32[16,640]{1,0:T(8,128)S(1)} %convert_reduce_fusion), channel_id=1, source_target_pairs={{0,64},{1,65},{2,66},{3,67},{4,68},{5,69},{6,70},{7,71},{8,72},{9,... | collective-permute-start | bytes 122888 | tf_op jit(solution)/shard_map/ppermute | solution.py:437
  167.3 0.8 collective-permute-start.9
  168.1 5.3 %collective-permute-done.6 = bf16[256,640]{1,0:T(8,128)(2,1)S(1)} collective-permute-done((bf16[256,640]{1,0:T(8,128)(2,1)}, bf16[256,640]{1,0:T(8,128)(2,1)S(1)}, u32[]{:S(2)}, u32[]{:S(2)}) %collective-permute-start.6) | collective-permute-done | bytes 327712 | tf_op jit(solution)/shard_map/ppermute | solution.py:420
  173.4 2.2 collective-permute-done.7
  175.6 2.7 %collective-permute-start.16 = (bf16[32,640]{1,0:T(8,128)(2,1)S(1)}, bf16[32,640]{1,0:T(8,128)(2,1)S(1)}, u32[]{:S(2)}, u32[]{:S(2)}) collective-permute-start(bf16[32,640]{1,0:T(8,128)(2,1)S(1)} %fusion.1), channel_id=1, source_target_pairs={{0,48},{16,0},{32,16},{48,32},{1,49},{17,1},{33,17},{49,33},{2,50}... | collective-permute-start | bytes 122888 | tf_op jit(solution)/shard_map/ppermute | solution.py:425
  178.3 0.5 collective-permute-start.17
  178.8 0.6 collective-permute-start.18
  179.4 3.2 %collective-permute-done.17 = bf16[32,640]{1,0:T(8,128)(2,1)S(1)} collective-permute-done((bf16[32,640]{1,0:T(8,128)(2,1)S(1)}, bf16[32,640]{1,0:T(8,128)(2,1)S(1)}, u32[]{:S(2)}, u32[]{:S(2)}) %collective-permute-start.17) | collective-permute-done | bytes 40992 | tf_op jit(solution)/shard_map/ppermute | solution.py:425
  182.7 0.4 collective-permute-done.18
  183.2 0.7 constant_dynamic-slice_fusion.1
  183.9 0.0 all-gather.5.cloned.1.call-update
  183.9 0.8 collective-permute-start.10
  184.7 1.1 add_convert_fusion.2
  185.8 0.1 collective-permute-start.13
  185.9 13.6 %collective-permute-done.10 = bf16[512,640]{1,0:T(8,128)(2,1)S(1)} collective-permute-done((bf16[512,640]{1,0:T(8,128)(2,1)}, bf16[512,640]{1,0:T(8,128)(2,1)S(1)}, u32[]{:S(2)}, u32[]{:S(2)}) %collective-permute-start.10) | collective-permute-done | bytes 655392 | tf_op jit(solution)/shard_map/ppermute | solution.py:420
  199.4 0.2 collective-permute-start.11
  199.6 0.2 add_convert_fusion
  199.8 0.9 collective-permute-start.14
  200.7 0.7 collective-permute-start.15
  201.4 5.5 %collective-permute-done.11.refs_4_ = bf16[256,640]{1,0:T(8,128)(2,1)S(1)} collective-permute-done((bf16[256,640]{1,0:T(8,128)(2,1)S(1)}, bf16[256,640]{1,0:T(8,128)(2,1)S(1)}, u32[]{:S(2)}, u32[]{:S(2)}) %collective-permute-start.11) | collective-permute-done | bytes 327712 | tf_op jit(solution)/shard_map/ppermute | solution.py:420
  206.9 0.2 collective-permute-start.12
  207.1 0.5 collective-permute-done.14.refs_2_
  207.6 6.4 %collective-permute-done.15.refs_3_ = bf16[256,640]{1,0:T(8,128)(2,1)S(1)} collective-permute-done((bf16[256,640]{1,0:T(8,128)(2,1)S(1)}, bf16[256,640]{1,0:T(8,128)(2,1)S(1)}, u32[]{:S(2)}, u32[]{:S(2)}) %collective-permute-start.15) | collective-permute-done | bytes 327712 | tf_op jit(solution)/shard_map/ppermute | solution.py:425
  214.0 0.7 copy-done.13
  214.7 16.2 %shard_map.132 = (bf16[1024,640]{1,0:T(8,128)(2,1)}, bf16[1024,640]{1,0:T(8,128)(2,1)}, bf16[1024,640]{1,0:T(8,128)(2,1)}) custom-call(s32[1]{0:T(128)} %bitcast.15.u_ref, bf16[5,1024,1024]{2,1,0:T(8,128)(2,1)} %get-tuple-element.82.p_ref, bf16[1024,640]{1,0:T(8,128)(2,1)} %bitcast.47, bf16[1024,640]{1,0:T(8,128)(2,1)} %bitcast.49, ...), custom_call_target="tpu_custom_call" | custom-call | flops 1000 | bytes 1476000000 | tf_op jit(solution)/shard_map/pallas_call | solution.py:94
  231.0 0.2 fusion
  231.1 0.0 all-gather.5.cloned.1.call-done
  231.2 3.6 %shard_map.133 = (f32[64,2560]{1,0:T(8,128)}, f32[64,5120]{1,0:T(8,128)}) custom-call(bf16[8,4,2,16,640]{4,3,2,1,0:T(8,128)(2,1)} %bitcast.52), custom_call_target="tpu_custom_call" | custom-call | flops 1000 | bytes 11070000 | tf_op jit(solution)/shard_map/pallas_call | solution.py:402
  (50 shorter events, 0.2 us)
Async XLA Ops:
  7.2 5.9 %copy-start.3 = (bf16[160,5120]{1,0:T(8,128)(2,1)S(1)}, bf16[160,5120]{1,0:T(8,128)(2,1)}, u32[]{:S(2)}) copy-start(bf16[160,5120]{1,0:T(8,128)(2,1)} %param.12) | copy-start | bytes 4915204
  7.2 90.4 %all-gather.3.cloned.1.call-start = ((), (), s32[]{:S(2)}) async-start(), calls=%async_computation.3 | async-start | bytes 14745600 | tf_op jit(solution)/shard_map/all_gather | solution.py:484
  9.6 12.3 %collective-permute-start = (bf16[80,2560]{1,0:T(8,128)(2,1)}, bf16[80,2560]{1,0:T(8,128)(2,1)S(1)}, u32[]{:S(2)}, u32[]{:S(2)}) collective-permute-start(bf16[80,2560]{1,0:T(8,128)(2,1)} %constant_dynamic-slice_fusion.4), channel_id=1, source_target_pairs={{0,2},{1,3},{2,64},{3,65},{4,6},{5,7},{6,68},{7,69},{8,10},{9,11},... | collective-permute-start | bytes 1228808 | tf_op jit(solution)/shard_map/ppermute | solution.py:437
  11.7 10.2 %collective-permute-start.1 = (bf16[80,2560]{1,0:T(8,128)(2,1)S(1)}, bf16[80,2560]{1,0:T(8,128)(2,1)S(1)}, u32[]{:S(2)}, u32[]{:S(2)}) collective-permute-start(bf16[80,2560]{1,0:T(8,128)(2,1)S(1)} %constant_dynamic-slice_fusion.3), channel_id=1, source_target_pairs={{0,66},{1,67},{2,0},{3,1},{4,70},{5,71},{6,4},{7,5},{8,74},{9,75},... | collective-permute-start | bytes 1228808 | tf_op jit(solution)/shard_map/ppermute | solution.py:437
  24.7 19.6 %collective-permute-start.2 = (bf16[160,2560]{1,0:T(8,128)(2,1)S(1)}, bf16[160,2560]{1,0:T(8,128)(2,1)S(1)}, u32[]{:S(2)}, u32[]{:S(2)}) collective-permute-start(bf16[160,2560]{1,0:T(8,128)(2,1)S(1)} %constant_dynamic-slice_fusion), channel_id=1, source_target_pairs={{0,64},{64,0},{1,65},{65,1},{2,66},{66,2},{3,67},{67,3},{4,68},{68... | collective-permute-start | bytes 2457608 | tf_op jit(solution)/shard_map/ppermute | solution.py:420
  44.2 0.9 copy-start.4
  45.1 38.1 %all-to-all-start = ((bf16[8,256,640]{2,1,0:T(8,128)(2,1)}), bf16[8,256,640]{2,1,0:T(8,128)(2,1)S(1)}, u32[]{:S(2)}, u32[]{:S(2)}) async-start(bf16[8,256,640]{2,1,0:T(8,128)(2,1)} %bitcast.42), calls=%async_computation | async-start | bytes 5242880 | tf_op jit(solution)/shard_map/all_to_all | solution.py:416
  84.3 13.3 %collective-permute-start.3 = (bf16[96,2560]{1,0:T(8,128)(2,1)S(1)}, bf16[96,2560]{1,0:T(8,128)(2,1)}, u32[]{:S(2)}, u32[]{:S(2)}) collective-permute-start(bf16[96,2560]{1,0:T(8,128)(2,1)S(1)} %slice.23), channel_id=1, source_target_pairs={{0,64},{64,0},{1,65},{65,1},{2,66},{66,2},{3,67},{67,3},{4,68},{68... | collective-permute-start | bytes 1474568 | tf_op jit(solution)/shard_map/ppermute | solution.py:420
  89.1 1.0 copy-start.9
  89.5 8.0 %copy-start = (bf16[64,8,4,640]{3,1,2,0:T(8,128)(2,1)}, bf16[64,8,4,640]{3,1,2,0:T(8,128)(2,1)S(1)}, u32[]{:S(2)}) copy-start(bf16[64,8,4,640]{3,1,2,0:T(8,128)(2,1)S(1)} %copy.18) | copy-start | bytes 7864324
  130.2 15.5 %collective-permute-start.4 = (bf16[96,2560]{1,0:T(8,128)(2,1)}, bf16[96,2560]{1,0:T(8,128)(2,1)S(1)}, u32[]{:S(2)}, u32[]{:S(2)}) collective-permute-start(bf16[96,2560]{1,0:T(8,128)(2,1)} %get-tuple-element.65), channel_id=1, source_target_pairs={{0,64},{64,0},{1,65},{65,1},{2,66},{66,2},{3,67},{67,3},{4,68},{68... | collective-permute-start | bytes 1474568 | tf_op jit(solution)/shard_map/ppermute | solution.py:420
  130.6 15.2 %copy-start.14 = (bf16[112,2560]{1,0:T(8,128)(2,1)S(1)}, bf16[112,2560]{1,0:T(8,128)(2,1)}, u32[]{:S(2)}) copy-start(bf16[112,2560]{1,0:T(8,128)(2,1)} %get-tuple-element.69) | copy-start | bytes 1720324
  136.7 26.5 %all-to-all-start.2 = ((bf16[32,16,640]{2,1,0:T(8,128)(2,1)}), bf16[32,16,640]{2,1,0:T(8,128)(2,1)S(1)}, u32[]{:S(2)}, u32[]{:S(2)}) async-start(bf16[32,16,640]{2,1,0:T(8,128)(2,1)} %bitcast.53), calls=%async_computation.2 | async-start | bytes 1310720 | tf_op jit(solution)/shard_map/all_to_all | solution.py:515
  145.7 85.5 %all-gather.5.cloned.1.call-start = ((), (), s32[]{:S(2)}) async-start(), calls=%async_computation.4 | async-start | bytes 1474560 | tf_op jit(solution)/shard_map/all_gather | solution.py:562
  145.7 17.0 %copy-start.5 = (bf16[96,2560]{1,0:T(8,128)(2,1)}, bf16[96,2560]{1,0:T(8,128)(2,1)S(1)}, u32[]{:S(2)}) copy-start(bf16[96,2560]{1,0:T(8,128)(2,1)S(1)} %collective-permute-done.4) | copy-start | bytes 1474564
  145.8 17.4 %collective-permute-start.5 = (bf16[112,2560]{1,0:T(8,128)(2,1)S(1)}, bf16[112,2560]{1,0:T(8,128)(2,1)S(1)}, u32[]{:S(2)}, u32[]{:S(2)}) collective-permute-start(bf16[112,2560]{1,0:T(8,128)(2,1)S(1)} %copy-done.14), channel_id=1, source_target_pairs={{0,64},{64,0},{1,65},{65,1},{2,66},{66,2},{3,67},{67,3},{4,68},{68... | collective-permute-start | bytes 1720328 | tf_op jit(solution)/shard_map/ppermute | solution.py:420
  162.8 36.7 %copy-start.15 = (bf16[256,640]{1,0:T(8,128)(2,1)S(1)}, bf16[256,640]{1,0:T(8,128)(2,1)}, u32[]{:S(2)}) copy-start(bf16[256,640]{1,0:T(8,128)(2,1)} %get-tuple-element.79) | copy-start | bytes 983044
  162.8 36.9 %copy-start.7 = (bf16[256,640]{1,0:T(8,128)(2,1)S(1)}, bf16[256,640]{1,0:T(8,128)(2,1)}, u32[]{:S(2)}) copy-start(bf16[256,640]{1,0:T(8,128)(2,1)} %get-tuple-element.86) | copy-start | bytes 983044
  162.8 36.9 %copy-start.8 = (bf16[256,640]{1,0:T(8,128)(2,1)S(1)}, bf16[256,640]{1,0:T(8,128)(2,1)}, u32[]{:S(2)}) copy-start(bf16[256,640]{1,0:T(8,128)(2,1)} %get-tuple-element.88) | copy-start | bytes 983044
  162.8 10.6 %collective-permute-start.6 = (bf16[256,640]{1,0:T(8,128)(2,1)}, bf16[256,640]{1,0:T(8,128)(2,1)S(1)}, u32[]{:S(2)}, u32[]{:S(2)}) collective-permute-start(bf16[256,640]{1,0:T(8,128)(2,1)} %get-tuple-element.75), channel_id=1, source_target_pairs={{0,64},{64,0},{1,65},{65,1},{2,66},{66,2},{3,67},{67,3},{4,68},{68... | collective-permute-start | bytes 983048 | tf_op jit(solution)/shard_map/ppermute | solution.py:420
  163.3 12.2 %collective-permute-start.7 = (f32[16,640]{1,0:T(8,128)S(1)}, f32[16,640]{1,0:T(8,128)S(1)}, u32[]{:S(2)}, u32[]{:S(2)}) collective-permute-start(f32[16,640]{1,0:T(8,128)S(1)} %convert_reduce_fusion), channel_id=1, source_target_pairs={{0,2},{1,3},{2,64},{3,65},{4,6},{5,7},{6,68},{7,69},{8,10},{9,11},... | collective-permute-start | bytes 122888 | tf_op jit(solution)/shard_map/ppermute | solution.py:437
  164.1 11.5 %collective-permute-start.8 = (f32[16,640]{1,0:T(8,128)S(1)}, f32[16,640]{1,0:T(8,128)S(1)}, u32[]{:S(2)}, u32[]{:S(2)}) collective-permute-start(f32[16,640]{1,0:T(8,128)S(1)} %convert_reduce_fusion), channel_id=1, source_target_pairs={{0,64},{1,65},{2,66},{3,67},{4,68},{5,69},{6,70},{7,71},{8,72},{9,... | collective-permute-start | bytes 122888 | tf_op jit(solution)/shard_map/ppermute | solution.py:437
  167.3 8.2 %collective-permute-start.9 = (f32[16,640]{1,0:T(8,128)S(1)}, f32[16,640]{1,0:T(8,128)S(1)}, u32[]{:S(2)}, u32[]{:S(2)}) collective-permute-start(f32[16,640]{1,0:T(8,128)S(1)} %convert_reduce_fusion), channel_id=1, source_target_pairs={{0,66},{1,67},{2,0},{3,1},{4,70},{5,71},{6,4},{7,5},{8,74},{9,75},... | collective-permute-start | bytes 122888 | tf_op jit(solution)/shard_map/ppermute | solution.py:437
  175.6 3.8 %collective-permute-start.16 = (bf16[32,640]{1,0:T(8,128)(2,1)S(1)}, bf16[32,640]{1,0:T(8,128)(2,1)S(1)}, u32[]{:S(2)}, u32[]{:S(2)}) collective-permute-start(bf16[32,640]{1,0:T(8,128)(2,1)S(1)} %fusion.1), channel_id=1, source_target_pairs={{0,48},{16,0},{32,16},{48,32},{1,49},{17,1},{33,17},{49,33},{2,50}... | collective-permute-start | bytes 122888 | tf_op jit(solution)/shard_map/ppermute | solution.py:425
  178.3 4.4 %collective-permute-start.17 = (bf16[32,640]{1,0:T(8,128)(2,1)S(1)}, bf16[32,640]{1,0:T(8,128)(2,1)S(1)}, u32[]{:S(2)}, u32[]{:S(2)}) collective-permute-start(bf16[32,640]{1,0:T(8,128)(2,1)S(1)} %fusion.1), channel_id=1, source_target_pairs={{0,32},{16,48},{32,0},{48,16},{1,33},{17,49},{33,1},{49,17},{2,34}... | collective-permute-start | bytes 122888 | tf_op jit(solution)/shard_map/ppermute | solution.py:425
  178.8 4.3 %collective-permute-start.18 = (bf16[32,640]{1,0:T(8,128)(2,1)S(1)}, bf16[32,640]{1,0:T(8,128)(2,1)S(1)}, u32[]{:S(2)}, u32[]{:S(2)}) collective-permute-start(bf16[32,640]{1,0:T(8,128)(2,1)S(1)} %fusion.1), channel_id=1, source_target_pairs={{0,16},{16,32},{32,48},{48,0},{1,17},{17,33},{33,49},{49,1},{2,18}... | collective-permute-start | bytes 122888 | tf_op jit(solution)/shard_map/ppermute | solution.py:425
  183.9 15.5 %collective-permute-start.10 = (bf16[512,640]{1,0:T(8,128)(2,1)}, bf16[512,640]{1,0:T(8,128)(2,1)S(1)}, u32[]{:S(2)}, u32[]{:S(2)}) collective-permute-start(bf16[512,640]{1,0:T(8,128)(2,1)} %get-tuple-element.77), channel_id=1, source_target_pairs={{0,64},{64,0},{1,65},{65,1},{2,66},{66,2},{3,67},{67,3},{4,68},{68... | collective-permute-start | bytes 1966088 | tf_op jit(solution)/shard_map/ppermute | solution.py:420
  185.8 21.3 %collective-permute-start.13 = (bf16[256,640]{1,0:T(8,128)(2,1)S(1)}, bf16[256,640]{1,0:T(8,128)(2,1)S(1)}, u32[]{:S(2)}, u32[]{:S(2)}) collective-permute-start(bf16[256,640]{1,0:T(8,128)(2,1)S(1)} %add_convert_fusion.2), channel_id=1, source_target_pairs={{0,16},{16,32},{32,48},{48,0},{1,17},{17,33},{33,49},{49,1},{2,18}... | collective-permute-start | bytes 983048 | tf_op jit(solution)/shard_map/ppermute | solution.py:425
  199.4 7.5 %collective-permute-start.11 = (bf16[256,640]{1,0:T(8,128)(2,1)S(1)}, bf16[256,640]{1,0:T(8,128)(2,1)S(1)}, u32[]{:S(2)}, u32[]{:S(2)}) collective-permute-start(bf16[256,640]{1,0:T(8,128)(2,1)S(1)} %copy-done.15), channel_id=1, source_target_pairs={{0,64},{64,0},{1,65},{65,1},{2,66},{66,2},{3,67},{67,3},{4,68},{68... | collective-permute-start | bytes 983048 | tf_op jit(solution)/shard_map/ppermute | solution.py:420
  199.8 7.8 %collective-permute-start.14 = (bf16[256,640]{1,0:T(8,128)(2,1)S(1)}, bf16[256,640]{1,0:T(8,128)(2,1)S(1)}, u32[]{:S(2)}, u32[]{:S(2)}) collective-permute-start(bf16[256,640]{1,0:T(8,128)(2,1)S(1)} %get-tuple-element.101), channel_id=1, source_target_pairs={{0,32},{16,48},{32,0},{48,16},{1,33},{17,49},{33,1},{49,17},{2,34}... | collective-permute-start | bytes 983048 | tf_op jit(solution)/shard_map/ppermute | solution.py:425
  200.7 13.3 %collective-permute-start.15 = (bf16[256,640]{1,0:T(8,128)(2,1)S(1)}, bf16[256,640]{1,0:T(8,128)(2,1)S(1)}, u32[]{:S(2)}, u32[]{:S(2)}) collective-permute-start(bf16[256,640]{1,0:T(8,128)(2,1)S(1)} %get-tuple-element.100), channel_id=1, source_target_pairs={{0,48},{16,0},{32,16},{48,32},{1,49},{17,1},{33,17},{49,33},{2,50}... | collective-permute-start | bytes 983048 | tf_op jit(solution)/shard_map/ppermute | solution.py:425
  206.9 7.1 %copy-start.11 = (bf16[256,640]{1,0:T(8,128)(2,1)}, bf16[256,640]{1,0:T(8,128)(2,1)S(1)}, u32[]{:S(2)}) copy-start(bf16[256,640]{1,0:T(8,128)(2,1)S(1)} %collective-permute-done.11.refs_4_) | copy-start | bytes 983044
  206.9 24.0 %collective-permute-start.12 = (bf16[48,2560]{1,0:T(8,128)(2,1)}, bf16[48,2560]{1,0:T(8,128)(2,1)S(1)}, u32[]{:S(2)}, u32[]{:S(2)}) collective-permute-start(bf16[48,2560]{1,0:T(8,128)(2,1)} %get-tuple-element.81), channel_id=1, source_target_pairs={{0,64},{64,0},{1,65},{65,1},{2,66},{66,2},{3,67},{67,3},{4,68},{68... | collective-permute-start | bytes 737288 | tf_op jit(solution)/shard_map/ppermute | solution.py:420
  207.1 6.9 %copy-start.10 = (bf16[256,640]{1,0:T(8,128)(2,1)}, bf16[256,640]{1,0:T(8,128)(2,1)S(1)}, u32[]{:S(2)}) copy-start(bf16[256,640]{1,0:T(8,128)(2,1)S(1)} %collective-permute-done.13.refs_1_) | copy-start | bytes 983044
  207.6 6.4 %copy-start.12 = (bf16[256,640]{1,0:T(8,128)(2,1)}, bf16[256,640]{1,0:T(8,128)(2,1)S(1)}, u32[]{:S(2)}) copy-start(bf16[256,640]{1,0:T(8,128)(2,1)S(1)} %collective-permute-done.14.refs_2_) | copy-start | bytes 983044
  214.0 0.7 copy-start.13
  214.7 16.2 %copy-start.1 = (bf16[256,5120]{1,0:T(8,128)(2,1)S(1)}, bf16[256,5120]{1,0:T(8,128)(2,1)}, u32[]{:S(2)}) copy-start(bf16[256,5120]{1,0:T(8,128)(2,1)} %get-tuple-element.62.own_ref) | copy-start | bytes 7864324
  214.7 16.2 %copy-start.6 = (bf16[96,2560]{1,0:T(8,128)(2,1)S(1)}, bf16[96,2560]{1,0:T(8,128)(2,1)}, u32[]{:S(2)}) copy-start(bf16[96,2560]{1,0:T(8,128)(2,1)} %copy-done.5) | copy-start | bytes 1474564
  231.1 3.6 %copy-start.2 = (bf16[1,1,256,5120]{3,2,1,0:T(8,128)(2,1)}, bf16[1,1,256,5120]{3,2,1,0:T(8,128)(2,1)S(1)}, u32[]{:S(2)}) copy-start(bf16[1,1,256,5120]{3,2,1,0:T(8,128)(2,1)S(1)} %fusion) | copy-start | bytes 7864324
Sparse Core Ops, SparseCore 0:
  23.6 73.5 all-gather.2
  184.0 24.4 all-gather.4

commit v3 on v2

--- a/solution.py
+++ b/solution.py
@@ -33,11 +33,11 @@
     rows = o_ref.shape[2]
     for part in range(o_ref.shape[1]):
         at = pl.ds(part * rows, rows)
-        scores = dot(q_ref[at, :], k_ref[...], LAST) * SCALE
-        exps = jnp.exp(scores - jnp.max(scores, axis=1, keepdims=True))
-        probs = (exps / jnp.sum(exps, axis=1, keepdims=True)).astype(BF16)
-        p_ref[0, at, :] = probs
-        out = dot(probs, v_ref[...]).astype(BF16)
+        scores = dot(k_ref[...], q_ref[at, :], LAST) * SCALE
+        exps = jnp.exp(scores - jnp.max(scores, axis=0, keepdims=True))
+        probs = (exps * (1.0 / jnp.sum(exps, axis=0, keepdims=True))).astype(BF16)
+        p_ref[0, :, at] = probs
+        out = dot(probs, v_ref[...], FIRST).astype(BF16)
         o_ref[0, part] = out
         o_ref[1, part] = out
 
@@ -64,26 +64,24 @@
 
 
 def backward_kernel(u_ref, p_ref, q_ref, k_ref, v_ref, o_ref, *refs):
-    (*g_refs, dq_ref, dk_ref, dv_ref, g_scr, d_scr) = refs
+    (*g_refs, dq_ref, dk_ref, dv_ref, g_scr) = refs
     parts = len(g_refs) - 1
-    rows = g_refs[0].shape[0]
+    rows, size = g_refs[0].shape
     for ahead in range(parts):
         part = lax.rem(u_ref[0] + (parts - ahead), parts)
-        at = pl.ds(pl.multiple_of(part * rows, rows), rows)
         block = g_refs[ahead][...]
         if ahead == 0:
             block = (block.astype(F32) + g_refs[parts][...].astype(F32)).astype(BF16)
-        g_scr[at, :] = block
-        d_scr[at, :] = jnp.sum(
-            block.astype(F32) * o_ref[0, part].astype(F32), axis=1, keepdims=True
-        )
+        g_scr[pl.ds(pl.multiple_of(part * rows, rows), rows), :] = block
     probs = p_ref[0]
     grad = g_scr[...]
-    grad_probs = dot(grad, v_ref[...], LAST)
-    grad_scores = (probs.astype(F32) * (grad_probs - d_scr[...])).astype(BF16)
-    dv_ref[...] = dot(probs, grad, FIRST).astype(BF16)
-    dq_ref[...] = (dot(grad_scores, k_ref[...]) * SCALE).astype(BF16)
-    dk_ref[...] = (dot(grad_scores, q_ref[...], FIRST) * SCALE).astype(BF16)
+    out = o_ref[0].reshape(parts * rows, size)
+    delta = jnp.sum((grad.astype(F32) * out.astype(F32)).T, axis=0, keepdims=True)
+    grad_probs = dot(v_ref[...], grad, LAST)
+    grad_scores = (probs.astype(F32) * (grad_probs - delta)).astype(BF16)
+    dv_ref[...] = dot(probs, grad).astype(BF16)
+    dk_ref[...] = (dot(grad_scores, q_ref[...]) * SCALE).astype(BF16)
+    dq_ref[...] = (dot(k_ref[...].T, grad_scores) * SCALE).T.astype(BF16)
 
 
 def attention_backward(place, probs, query, key, value, out, grads):
@@ -105,7 +103,7 @@
             ]
             + [pl.BlockSpec((seq // parts, HD), lambda h, u: (0, h))] * (parts + 1),
             out_specs=[block] * 3,
-            scratch_shapes=[pltpu.VMEM((seq, HD), BF16), pltpu.VMEM((seq, 1), F32)],
+            scratch_shapes=[pltpu.VMEM((seq, HD), BF16)],
         ),
         out_shape=[jax.ShapeDtypeStruct((seq, width), BF16)] * 3,
         compiler_params=params(),
@@ -190,8 +188,13 @@
 
 
 def guidance_kernel(
-    b_ref, v_ref, r_ref, sum_ref, own_ref, oth_ref, *cut_refs
+    b_ref, v_ref, r_ref, sum_ref, x_ref, m_ref, up_ref,
+    own_ref, oth_ref, mid_ref, both_ref, *refs,
 ):
+    step = pl.program_id(0)
+    tokens, tile = r_ref.shape
+    (*cut_refs, m_scr) = refs
+    groups = both_ref.shape[0] // 2
     totals = sum_ref[0:1, :]
     for at in range(8, sum_ref.shape[0], 8):
         totals = totals + sum_ref[at : at + 1, :]
@@ -202,27 +205,56 @@
     target = r_ref[...].astype(F32)
     cond = v_ref[0].astype(F32)
     uncond = v_ref[1].astype(F32)
-    grad0 = GUIDANCE * target + slope * uncond
+    grad0 = (GUIDANCE * target + slope * uncond).astype(BF16)
     grad1 = (
         ((1.0 - GUIDANCE) * scale) * target
         + slope * cond
         + (-2.0 * slope * scale) * uncond
-    )
-    own_ref[...] = jnp.where(first, grad0, grad1).astype(BF16)
-    other = jnp.where(first, grad1, grad0).astype(BF16)
+    ).astype(BF16)
+    own_ref[...] = jnp.where(first, grad0, grad1)
+    other = jnp.where(first, grad1, grad0)
     oth_ref[...] = other
     at = 0
     for cut_ref in cut_refs:
         cut_ref[...] = other[at : at + cut_ref.shape[0]]
         at += cut_ref.shape[0]
-
-
-def guidance(branch, vel, reward, sums, cuts):
+    up = up_ref[...]
+    part = jnp.concatenate([dot(grad0, up, LAST), dot(grad1, up, LAST)], axis=0)
+    up_part = dot(m_ref[:tokens], grad0, FIRST) + dot(m_ref[tokens:], grad1, FIRST)
+    up_part = up_part.astype(BF16)
+    for row in range(groups):
+        both_ref[groups + row, step] = up_part[16 * row : 16 * row + 16]
+
+    @pl.when(step == 0)
+    def _():
+        m_scr[...] = part
+
+    @pl.when(step > 0)
+    def _():
+        m_scr[...] += part
+
+    @pl.when(step == pl.num_programs(0) - 1)
+    def _():
+        mid = m_scr[...].astype(BF16)
+        mid_ref[0:tokens] = jnp.where(first, mid[:tokens], mid[tokens:])
+        mid_ref[tokens:] = jnp.where(first, mid[tokens:], mid[:tokens])
+        down_part = dot(mid, x_ref[...], FIRST).astype(BF16)
+        for row in range(groups):
+            for lane in range(both_ref.shape[1]):
+                both_ref[row, lane] = down_part[
+                    16 * row : 16 * row + 16, lane * tile : lane * tile + tile
+                ]
+
+
+def guidance(branch, vel, reward, sums, attended, middle, up, cuts):
     _, tokens, half = vel.shape
+    rank, depth = up.shape[0], attended.shape[1]
     tile = 640
     steps = half // tile
+    whole = lambda j, b: (0, 0)
     mine = lambda j, b: (0, b[0] * steps + j)
     here = lambda j, b: (0, j)
+    both = (2 * rank // 16, steps, 16, tile)
     return pl.pallas_call(
         guidance_kernel,
         grid_spec=pltpu.PrefetchScalarGridSpec(
@@ -231,92 +263,30 @@
             in_specs=[
                 pl.BlockSpec((2, tokens, tile), lambda j, b: (0, 0, j)),
                 pl.BlockSpec((tokens, tile), mine),
-                pl.BlockSpec(sums.shape, lambda j, b: (0, 0)),
-            ],
-            out_specs=[
-                pl.BlockSpec((tokens, tile), mine),
-                pl.BlockSpec((tokens, tile), here),
-            ]
-            + [pl.BlockSpec((cut, tile), here) for cut in cuts],
-        ),
-        out_shape=[
-            jax.ShapeDtypeStruct((tokens, 2 * half), BF16),
-            jax.ShapeDtypeStruct((tokens, half), BF16),
-        ]
-        + [jax.ShapeDtypeStruct((cut, half), BF16) for cut in cuts],
-        compiler_params=params(),
-        cost_estimate=lasts(4),
-    )(branch, vel, reward, sums)
-
-
-def adapter_part_kernel(b_ref, own_ref, oth_ref, x_ref, m_ref, up_ref, mid_ref, both_ref, m_scr):
-    step = pl.program_id(0)
-    tokens, tile = own_ref.shape
-    groups = both_ref.shape[0] // 2
-    up = up_ref[...]
-    own, oth = own_ref[...], oth_ref[...]
-    part = dot(jnp.concatenate([own, oth], axis=0), up, LAST)
-    own_at = pl.ds(pl.multiple_of(b_ref[0] * tokens, tokens), tokens)
-    oth_at = pl.ds(pl.multiple_of((1 - b_ref[0]) * tokens, tokens), tokens)
-    up_part = dot(m_ref[own_at, :], own, FIRST) + dot(m_ref[oth_at, :], oth, FIRST)
-    up_part = up_part.astype(BF16)
-    for row in range(groups):
-        both_ref[groups + row, step] = up_part[16 * row : 16 * row + 16]
-
-    @pl.when(step == 0)
-    def _():
-        m_scr[...] = part
-
-    @pl.when(step > 0)
-    def _():
-        m_scr[...] += part
-
-    @pl.when(step == pl.num_programs(0) - 1)
-    def _():
-        mid = m_scr[...].astype(BF16)
-        mid_ref[...] = mid
-        down_part = dot(mid[:tokens], x_ref[own_at, :], FIRST)
-        down_part = (down_part + dot(mid[tokens:], x_ref[oth_at, :], FIRST)).astype(BF16)
-        for row in range(groups):
-            for lane in range(both_ref.shape[1]):
-                both_ref[row, lane] = down_part[
-                    16 * row : 16 * row + 16, lane * tile : lane * tile + tile
-                ]
-
-
-def adapter_part(branch, grad_own, grad_other, attended, middle, up):
-    tokens, half = grad_other.shape
-    rank, depth = up.shape[0], attended.shape[1]
-    tile = 640
-    steps = half // tile
-    whole = lambda j, b: (0, 0)
-    mine = lambda j, b: (0, b[0] * steps + j)
-    both = (2 * rank // 16, steps, 16, tile)
-    return pl.pallas_call(
-        adapter_part_kernel,
-        grid_spec=pltpu.PrefetchScalarGridSpec(
-            num_scalar_prefetch=1,
-            grid=(steps,),
-            in_specs=[
-                pl.BlockSpec((tokens, tile), mine),
-                pl.BlockSpec((tokens, tile), lambda j, b: (0, j)),
+                pl.BlockSpec(sums.shape, whole),
                 pl.BlockSpec((2 * tokens, depth), whole),
                 pl.BlockSpec((2 * tokens, rank), whole),
                 pl.BlockSpec((rank, tile), mine),
             ],
             out_specs=[
+                pl.BlockSpec((tokens, tile), mine),
+                pl.BlockSpec((tokens, tile), here),
                 pl.BlockSpec((2 * tokens, rank), whole),
                 pl.BlockSpec(both, lambda j, b: (0, 0, 0, 0)),
-            ],
+            ]
+            + [pl.BlockSpec((cut, tile), here) for cut in cuts],
             scratch_shapes=[pltpu.VMEM((2 * tokens, rank), F32)],
         ),
         out_shape=[
+            jax.ShapeDtypeStruct((tokens, 2 * half), BF16),
+            jax.ShapeDtypeStruct((tokens, half), BF16),
             jax.ShapeDtypeStruct((2 * tokens, rank), BF16),
             jax.ShapeDtypeStruct(both, BF16),
-        ],
+        ]
+        + [jax.ShapeDtypeStruct((cut, half), BF16) for cut in cuts],
         compiler_params=params(),
-        cost_estimate=lasts(5),
-    )(branch, grad_own, grad_other, attended, middle, up)
+        cost_estimate=lasts(8),
+    )(branch, vel, reward, sums, attended, middle, up)
 
 
 def gradient_kernel(u_ref, b_ref, own_ref, oth_ref, mid_ref, w_ref, down_ref, *refs):
@@ -325,17 +295,15 @@
     rows = jnp.concatenate([own_ref[...], oth_ref[...]], axis=0)
     part = dot(rows, weight_rows(w_ref), LAST) + dot(mid_ref[...], down_ref[...])
     part = part.astype(BF16)
-    *gown_refs, first_ref, rest_ref, near_ref = refs
+    *gown_refs, far_ref, near_ref = refs
     last = len(gown_refs) - 1
     for at in range(last + 1):
 
         @pl.when(step == at)
         def _():
             gown_refs[at][...] = part[:tokens]
-            if at == 0:
-                first_ref[...] = part[tokens:]
-            elif at < last:
-                rest_ref[(at - 1) * tokens : at * tokens] = part[tokens:]
+            if at < last:
+                far_ref[at * tokens : (at + 1) * tokens] = part[tokens:]
             else:
                 near_ref[...] = part[tokens:]
 
@@ -363,15 +331,13 @@
             ],
             out_specs=[pl.BlockSpec((tokens, wide), whole)] * parts
             + [
-                pl.BlockSpec((tokens, wide), whole),
-                pl.BlockSpec(((parts - 2) * tokens, wide), whole),
+                pl.BlockSpec(((parts - 1) * tokens, wide), whole),
                 pl.BlockSpec((tokens, wide), whole),
             ],
         ),
         out_shape=[jax.ShapeDtypeStruct((tokens, wide), BF16)] * parts
         + [
-            jax.ShapeDtypeStruct((tokens, wide), BF16),
-            jax.ShapeDtypeStruct(((parts - 2) * tokens, wide), BF16),
+            jax.ShapeDtypeStruct(((parts - 1) * tokens, wide), BF16),
             jax.ShapeDtypeStruct((tokens, wide), BF16),
         ],
         compiler_params=params(),
@@ -380,33 +346,43 @@
 
 
 def adapter_kernel(p_ref, down_ref, up_ref):
-    members, parts, _, rows, tile = p_ref.shape
+    members, _, _, rows, tile = p_ref.shape
     half = down_ref.shape[1]
     lanes = half // tile
-    groups = parts * members // lanes
-    for u in range(parts):
+
+    @pl.when(pl.program_id(0) < pl.num_programs(0) // 2)
+    def _():
         for c in range(members):
-            row, lane = divmod(u * members + c, lanes)
-            columns = pl.ds(lane * tile, tile)
-            if row < groups // 2:
-                both = p_ref[c, u, 0].astype(F32) + p_ref[c, u, 1].astype(F32)
-                down_ref[pl.ds(row * rows, rows), columns] = both
-            else:
-                at = pl.ds((row - groups // 2) * rows, rows)
-                for b in range(2):
-                    up_ref[at, pl.ds(b * half + lane * tile, tile)] = p_ref[c, u, b].astype(F32)
+            row, lane = divmod(c, lanes)
+            both = p_ref[c, 0, 0].astype(F32) + p_ref[c, 0, 1].astype(F32)
+            down_ref[pl.ds(row * rows, rows), pl.ds(lane * tile, tile)] = both
+
+    @pl.when(pl.program_id(0) >= pl.num_programs(0) // 2)
+    def _():
+        for c in range(members):
+            row, lane = divmod(c, lanes)
+            for b in range(2):
+                columns = pl.ds(b * half + lane * tile, tile)
+                up_ref[pl.ds(row * rows, rows), columns] = p_ref[c, 0, b].astype(F32)
 
 
 def adapter(pieces, rank, lanes):
-    half = lanes * pieces.shape[4]
+    members, parts, _, rows, tile = pieces.shape
+    half = lanes * tile
+    span = members // lanes * rows
+    first_up = parts // 2
     return pl.pallas_call(
         adapter_kernel,
+        grid=(parts,),
         out_shape=[
             jax.ShapeDtypeStruct((rank, half), F32),
             jax.ShapeDtypeStruct((rank, 2 * half), F32),
         ],
-        in_specs=[pl.BlockSpec(memory_space=pltpu.VMEM)],
-        out_specs=[pl.BlockSpec(memory_space=pltpu.VMEM)] * 2,
+        in_specs=[pl.BlockSpec((members, 1, 2, rows, tile), lambda u: (0, u, 0, 0, 0))],
+        out_specs=[
+            pl.BlockSpec((span, half), lambda u: (jnp.minimum(u, first_up - 1), 0)),
+            pl.BlockSpec((span, 2 * half), lambda u: (jnp.maximum(u - first_up, 0), 0)),
+        ],
         compiler_params=params(),
         cost_estimate=lasts(3),
     )(pieces)
@@ -483,15 +459,16 @@
     ]
     weight = lax.all_gather(operand, "fsdp", axis=0, tiled=True, axis_index_groups=weight_groups)
     weight = weight.reshape(clips, depth // clips, half)
+    early = 5 * tokens // 8
     hidden_send = lax.dynamic_slice_in_dim(hidden_ready, (1 - branch) * half, half, 1)
-    early = 5 * tokens // 8
     hidden_early = swap(hidden_send[:early])
+    hidden_late = hidden_send[early:]
 
     probs, attended = attention_forward(query2, key2, value2, parts)
     attended, hidden_early = lax.optimization_barrier((attended, hidden_early))
     gathered = exchange(attended.reshape(2 * seq, width), ("branch", "ulysses"))
-    gathered, hidden_send = lax.optimization_barrier((gathered, hidden_send))
-    hidden_late = swap(hidden_send[early:])
+    gathered, hidden_late = lax.optimization_barrier((gathered, hidden_late))
+    hidden_late = swap(hidden_late)
     gathered = gathered.reshape(2, parts, tokens, width).transpose(0, 2, 1, 3)
     gathered = gathered.reshape(2 * tokens, depth)
     middle = dot(gathered, adapter_down_weight).astype(BF16)
@@ -501,12 +478,11 @@
         adapter_up_weight, 2 * parts,
     )
     sums = exchange(sums, ("branch", "ulysses"))
-    cuts = (3 * tokens // 8, 7 * tokens // 16, 3 * tokens // 16)
-    grad_hidden, grad_other, *pieces_out = guidance(branch_word, vel, reward2, sums, cuts)
+    cuts = (tokens // 2, tokens // 2)
+    grad_hidden, grad_other, grad_middle, both, *pieces_out = guidance(
+        branch_word, vel, reward2, sums, gathered, middle, adapter_up_weight, cuts
+    )
     received = [swap(pieces_out[0])]
-    grad_middle, both = adapter_part(
-        branch_word, grad_hidden, grad_other, gathered, middle, adapter_up_weight
-    )
 
     groups = [
         [u * clips + z * 4 + near * 2 + core for u in range(parts) for z in range(clips // 4) for core in (0, 1)]
@@ -517,34 +493,25 @@
     )
     row_groups, lanes, rows, tile = both.shape
     pieces = row_groups * lanes
+    down_rows = adapter_down_weight.T
+    *grads, far, close = gradient(
+        place, branch_word, grad_hidden, grad_other, grad_middle, weight, down_rows, parts
+    )
+    far = swap(far)
+    both, grads[3], received[0] = lax.optimization_barrier((both, grads[3], received[0]))
     both = spread(both.reshape(pieces * rows, tile))
-    grad_other, pieces_out[1], received[0] = lax.optimization_barrier(
-        (grad_other, pieces_out[1], received[0])
-    )
+    total = jnp.sum(both.reshape(pieces, rows, tile).astype(F32), axis=0)
+    beside = [send_x(total, step) for step in (1, 2, 3)]
+    far, close, *beside = lax.optimization_barrier((far, close, *beside))
+    close = swap(close)
+    far = far.reshape(parts - 1, tokens, width)
+    routed = [
+        ahead_send((grads[at].astype(F32) + far[at].astype(F32)).astype(BF16), at + 1)
+        for at in range(parts - 1)
+    ]
+    close, pieces_out[1], *routed = lax.optimization_barrier((close, pieces_out[1], *routed))
     received.append(swap(pieces_out[1]))
 
-    down_rows = adapter_down_weight.T
-    *grads, far_first, far, close = gradient(
-        place, branch_word, grad_hidden, grad_other, grad_middle, weight, down_rows, parts
-    )
-    both, pieces_out[2], received[1], grads[3] = lax.optimization_barrier(
-        (both.reshape(pieces, rows, tile), pieces_out[2], received[1], grads[3])
-    )
-    far_first = swap(far_first)
-    total = jnp.sum(both.astype(F32), axis=0)
-    beside = [send_x(total, step) for step in (1, 2, 3)]
-    far, far_first, *beside = lax.optimization_barrier((far, far_first, *beside))
-    far = swap(far)
-    far, close = lax.optimization_barrier((far, close))
-    close = swap(close)
-    far = far.reshape(parts - 2, tokens, width)
-    halves = [far_first] + [far[at] for at in range(parts - 2)]
-    routed = [
-        ahead_send((grads[at].astype(F32) + block.astype(F32)).astype(BF16), at + 1)
-        for at, block in enumerate(halves)
-    ]
-    close, pieces_out[2] = lax.optimization_barrier((close, pieces_out[2]))
-    received.append(swap(pieces_out[2]))
     near = lax.rem(lax.axis_index("fsdp") // 2, 2)
     own_total = total + jnp.where(near == 0, beside[2], beside[0])
     other_total = beside[1] + jnp.where(near == 0, beside[0], beside[2])
@@ -558,11 +525,10 @@
     column = lax.dynamic_slice_in_dim(
         ring, (parts - 1 - place[0]) * 2 * rows, parts * 2 * rows, 0
     )
+    packed = lax.all_gather(column, "fsdp", axis=0, tiled=True, axis_index_groups=weight_groups)
+    packed = packed.reshape(clips // 2, parts, 2, rows, tile)
+    down_gradient_rows, adapter_up_gradient = adapter(packed, rank, lanes)
     grads = [grads[parts - 1]] + routed + [close]
-    packed = lax.all_gather(column, "fsdp", axis=0, tiled=True, axis_index_groups=weight_groups)
-    down_gradient_rows, adapter_up_gradient = adapter(
-        packed.reshape(clips // 2, parts, 2, rows, tile), rank, lanes
-    )
 
     grad_query, grad_key, grad_value = attention_backward(
         place, probs, query2, key2, value2, attended, grads

time: 245 us -> 231 us (0.943)
  blocking collectives: 12.8 us -> 33.9 us
  waiting for transfers between devices: 82.1 us -> 66.8 us
  starting transfers between devices: 39 us -> 27.9 us
  Pallas kernels: 76.2 us -> 71.3 us
  local copies, waits for them, and re-layouts: 12.7 us -> 9.51 us
    ppermute x8 -> x6, waiting for transfers between devices: 31.3 us -> 6.79 us  [swap(): return lax.ppermute(block, 'branch', [(0, 1), (1, 0)])]
    all_to_all x0 -> x1, blocking collectives: none -> 20.8 us  [body(): lax.all_to_all(block, ('ulysses', 'fsdp'), split_axis=0, concat_axis=0, t...]
    all_to_all x1 -> x0, starting transfers between devices: 8.94 us -> none  [body(): lax.all_to_all(block, ('ulysses', 'fsdp'), split_axis=0, concat_axis=0, t...]
    ppermute x6, waiting for transfers between devices: 10.6 us -> 17.1 us  [ahead_send(): lax.ppermute(block, 'ulysses', [(u, (u + ahead) % parts) for u in range(p...]
    pallas_call x2 -> x1, Pallas kernels: 9.72 us -> 4.01 us  [adapter(): pl.pallas_call(adapter_kernel, grid=(parts,), out_shape=[jax.ShapeDtypeSt...]
    dynamic_slice x1 -> x0, local copies, waits for them, and re-layouts: 2.58 us -> none  [body(): lax.dynamic_slice_in_dim(hidden_ready, (1 - branch) * half, half, 1)]
    ppermute x8 -> x6, starting transfers between devices: 10.1 us -> 10.5 us  [swap(): return lax.ppermute(block, 'branch', [(0, 1), (1, 0)])]
  transfers between devices with their start and end apart: 23 -> 20, of which waited for: 12 -> 14; matrix products, arithmetic and copies ran while one was open for 4% -> 3% of each run, Pallas kernels for 22% -> 20%
where the time goes in v3:
time: 231 us; the launch traced here: 227 us
  Pallas kernels  71.3 us (31%)
  waiting for transfers between devices  66.8 us (29%)
  blocking collectives  33.9 us (15%)
  starting transfers between devices  27.9 us (12%)
  between operations  14.3 us (6%)
  local copies, waits for them, and re-layouts  9.51 us (4%)
    all_to_all x1, waiting for transfers between devices, exchange(): return lax.all_to_all(block, axes, split_axis=0, concat_axis=0, tiled=True)  30.7 us
    all_to_all x1, blocking collectives, body(): lax.all_to_all(block, ('ulysses', 'fsdp'), split_axis=0, concat_axis=0, t...  20.8 us
    pallas_call x1, Pallas kernels, attention_forward(): pl.pallas_call(forward_kernel, grid=(heads,), in_specs=[block] * 3, out_s...  17.4 us
    ppermute x6, waiting for transfers between devices, ahead_send(): lax.ppermute(block, 'ulysses', [(u, (u + ahead) % parts) for u in range(p...  17.1 us
    pallas_call x1, Pallas kernels, gradient(): pl.pallas_call(gradient_kernel, grid_spec=pltpu.PrefetchScalarGridSpec(nu...  14.2 us
    pallas_call x1, Pallas kernels, attention_backward(): pl.pallas_call(backward_kernel, grid_spec=pltpu.PrefetchScalarGridSpec(nu...  14 us
    pallas_call x1, Pallas kernels, velocity(): pl.pallas_call(velocity_kernel, grid_spec=pltpu.PrefetchScalarGridSpec(nu...  13.7 us
    all_to_all x1, blocking collectives, exchange(): return lax.all_to_all(block, axes, split_axis=0, concat_axis=0, tiled=True)  13.1 us
  transfers between devices with their start and end apart: 20, of which 14 were waited for; matrix products, arithmetic and copies ran while one was open for 3% of the time, Pallas kernels for 20%

profile of v3, /device:TPU:1, one launch (start us, length us, event | category | flops | bytes accessed | tf_op | source)
XLA Modules:
  0.0 227.2 jit_solution(14398622296388558527)
XLA Ops:
  7.2 0.0 all-gather.3.cloned.1.call-start
  7.2 1.6 fusion.2
  8.9 0.8 constant_dynamic-slice_fusion.3
  9.6 2.0 collective-permute-start
  11.7 1.3 collective-permute-start.1
  13.1 0.1 constant_dynamic-slice_fusion.4
  13.1 8.8 %collective-permute-done = bf16[80,2560]{1,0:T(8,128)(2,1)S(1)} collective-permute-done((bf16[80,2560]{1,0:T(8,128)(2,1)}, bf16[80,2560]{1,0:T(8,128)(2,1)S(1)}, u32[]{:S(2)}, u32[]{:S(2)}) %collective-permute-start) | collective-permute-done | bytes 409632 | tf_op jit(solution)/shard_map/ppermute | solution.py:413
  21.9 0.0 collective-permute-done.1
  21.9 1.5 maximum_select_fusion
  23.4 0.0 all-gather.3.cloned.1.call-update
  23.5 1.2 constant_dynamic-slice_fusion
  24.7 2.4 %collective-permute-start.2 = (bf16[160,2560]{1,0:T(8,128)(2,1)S(1)}, bf16[160,2560]{1,0:T(8,128)(2,1)S(1)}, u32[]{:S(2)}, u32[]{:S(2)}) collective-permute-start(bf16[160,2560]{1,0:T(8,128)(2,1)S(1)} %constant_dynamic-slice_fusion), channel_id=1, source_target_pairs={{0,64},{64,0},{1,65},{65,1},{2,66},{66,2},{3,67},{67,3},{4,68},{68... | collective-permute-start | bytes 2457608 | tf_op jit(solution)/shard_map/ppermute | solution.py:396
  27.1 17.4 %shard_map.127 = (bf16[5,1024,1024]{2,1,0:T(8,128)(2,1)}, bf16[2,4,256,640]{3,2,1,0:T(8,128)(2,1)}) custom-call(bf16[1024,640]{1,0:T(8,128)(2,1)} %bitcast.45, bf16[1024,640]{1,0:T(8,128)(2,1)} %bitcast.47, bf16[1024,640]{1,0:T(8,128)(2,1)} %bitcast.49), custom_call_target="tpu_custom_call" | custom-call | flops 1000 | bytes 59040000 | tf_op jit(solution)/shard_map/pallas_call | solution.py:49
  44.5 0.9 copy-done.4
  45.4 6.0 %all-to-all-start = ((bf16[8,256,640]{2,1,0:T(8,128)(2,1)}), bf16[8,256,640]{2,1,0:T(8,128)(2,1)S(1)}, u32[]{:S(2)}, u32[]{:S(2)}) async-start(bf16[8,256,640]{2,1,0:T(8,128)(2,1)} %bitcast.41), calls=%async_computation | async-start | bytes 5242880 | tf_op jit(solution)/shard_map/all_to_all | solution.py:392
  51.4 0.0 all-gather.5.cloned.1.call-start
  51.4 1.2 dynamic-slice.1
  52.6 30.7 %all-to-all-done = bf16[8,256,640]{2,1,0:T(8,128)(2,1)S(1)} async-done(((bf16[8,256,640]{2,1,0:T(8,128)(2,1)}), bf16[8,256,640]{2,1,0:T(8,128)(2,1)S(1)}, u32[]{:S(2)}, u32[]{:S(2)}) %all-to-all-start) | async-done | bytes 2621472 | tf_op jit(solution)/shard_map/all_to_all | solution.py:392
  83.2 2.7 %collective-permute-start.3 = (bf16[96,2560]{1,0:T(8,128)(2,1)S(1)}, bf16[96,2560]{1,0:T(8,128)(2,1)}, u32[]{:S(2)}, u32[]{:S(2)}) collective-permute-start(bf16[96,2560]{1,0:T(8,128)(2,1)S(1)} %dynamic-slice.1), channel_id=1, source_target_pairs={{0,64},{64,0},{1,65},{65,1},{2,66},{66,2},{3,67},{67,3},{4,68},{68... | collective-permute-start | bytes 1474568 | tf_op jit(solution)/shard_map/ppermute | solution.py:396
  85.9 2.0 copy.15
  88.0 0.0 copy-start.9
  88.0 0.4 copy.18
  88.4 0.5 copy-done.9
  88.9 1.5 convolution_convert_fusion.m_ref
  90.4 6.0 %collective-permute-done.3.hlate_ref = bf16[96,2560]{1,0:T(8,128)(2,1)} collective-permute-done((bf16[96,2560]{1,0:T(8,128)(2,1)S(1)}, bf16[96,2560]{1,0:T(8,128)(2,1)}, u32[]{:S(2)}, u32[]{:S(2)}) %collective-permute-start.3) | collective-permute-done | bytes 491552 | tf_op jit(solution)/shard_map/ppermute | solution.py:396
  96.4 0.8 all-gather.3.cloned.1.call-done
  97.2 13.7 %shard_map.128 = (bf16[2,256,2560]{2,1,0:T(8,128)(2,1)}, f32[64,128]{1,0:T(8,128)}) custom-call(s32[1]{0:T(128)} %bitcast.b_ref, bf16[512,2560]{1,0:T(8,128)(2,1)} %bitcast.35, bf16[512,64]{1,0:T(8,128)(2,1)} %convolution_convert_fusion.m_ref, bf16[16,160,2560]{2,1,0:T(8,128)(2,1)} %bitcast.32, bf16[256,5120]{1,0:T(8,128)(2,1)} %bitcast.44, ...), custom_call_target="tpu_custom_call" | custom-call | flops 1000 | bytes 51660000 | tf_op jit(solution)/shard_map/pallas_call | solution.py:160
  110.9 13.1 %all_to_all.32 = f32[8,8,128]{2,1,0:T(8,128)} all-to-all(f32[8,8,128]{2,1,0:T(8,128)} %bitcast.56), channel_id=1, replica_groups=mesh['branch'=2,'ulysses'=4,'fsdp'=16] {'branch','ulysses'}, dimensions={0} | all-to-all | bytes 65536 | tf_op jit(solution)/shard_map/all_to_all | solution.py:392
  124.0 8.1 %shard_map.129 = (bf16[256,5120]{1,0:T(8,128)(2,1)}, bf16[256,2560]{1,0:T(8,128)(2,1)}, bf16[512,64]{1,0:T(8,128)(2,1)}, bf16[8,4,16,640]{3,2,1,0:T(8,128)(2,1)}...) custom-call(s32[1]{0:T(128)} %bitcast.b_ref, bf16[2,256,2560]{2,1,0:T(8,128)(2,1)} %get-tuple-element.55.v_ref, ...), custom_call_target="tpu_custom_call" | custom-call | flops 1000 | bytes 29520000 | tf_op jit(solution)/shard_map/pallas_call | solution.py:258
  132.1 0.5 collective-permute-start.4
  132.6 14.2 %shard_map.130 = (bf16[256,640]{1,0:T(8,128)(2,1)}, bf16[256,640]{1,0:T(8,128)(2,1)}, bf16[256,640]{1,0:T(8,128)(2,1)}, bf16[256,640]{1,0:T(8,128)(2,1)}, bf16[7...) custom-call(s32[1]{0:T(128)} %bitcast.14.u_ref, s32[1]{0:T(128)} %bitcast.b_ref, ...), custom_call_target="tpu_custom_call" | custom-call | flops 1000 | bytes 51660000 | tf_op jit(solution)/shard_map/pallas_call | solution.py:318
  146.8 2.7 %collective-permute-start.5 = (bf16[768,640]{1,0:T(8,128)(2,1)}, bf16[768,640]{1,0:T(8,128)(2,1)S(1)}, u32[]{:S(2)}, u32[]{:S(2)}) collective-permute-start(bf16[768,640]{1,0:T(8,128)(2,1)} %get-tuple-element.64), channel_id=1, source_target_pairs={{0,64},{64,0},{1,65},{65,1},{2,66},{66,2},{3,67},{67,3},{4,68},{68... | collective-permute-start | bytes 2949128 | tf_op jit(solution)/shard_map/ppermute | solution.py:396
  149.5 20.8 %all_to_all.33 = bf16[32,16,640]{2,1,0:T(8,128)(2,1)S(1)} all-to-all(bf16[32,16,640]{2,1,0:T(8,128)(2,1)S(1)} %bitcast.53), channel_id=1, replica_groups={{0,1,4,5,8,9,12,13,16,17,20,21,24,25,28,29,32,33,36,37,40,41,44,45,48,4..., dimensions={0} | all-to-all | bytes 1310720 | tf_op jit(solution)/shard_map/all_to_all | solution.py:491
  170.3 0.1 convert_reduce_fusion
  170.4 0.8 collective-permute-start.6
  171.2 1.0 collective-permute-start.7
  172.1 1.5 collective-permute-start.8
  173.7 0.0 collective-permute-done.5
  173.7 1.3 collective-permute-done.6
  175.0 0.6 collective-permute-done.7
  175.5 0.7 collective-permute-done.8
  176.3 0.2 collective-permute-start.14
  176.4 1.7 collective-permute-start.15
  178.1 1.1 collective-permute-done.14
  179.2 1.6 collective-permute-done.15
  180.8 1.4 collective-permute-done.16
  182.3 0.7 constant_dynamic-slice_fusion.1
  183.0 0.0 all-gather.5.cloned.1.call-update
  183.0 0.2 add_convert_fusion
  183.3 0.1 collective-permute-start.10
  183.4 2.7 %collective-permute-start.11 = (bf16[256,640]{1,0:T(8,128)(2,1)S(1)}, bf16[256,640]{1,0:T(8,128)(2,1)S(1)}, u32[]{:S(2)}, u32[]{:S(2)}) collective-permute-start(bf16[256,640]{1,0:T(8,128)(2,1)S(1)} %get-tuple-element.91), channel_id=1, source_target_pairs={{0,32},{16,48},{32,0},{48,16},{1,33},{17,49},{33,1},{49,17},{2,34}... | collective-permute-start | bytes 983048 | tf_op jit(solution)/shard_map/ppermute | solution.py:401
  186.1 0.0 collective-permute-start.12
  186.1 1.1 collective-permute-start.9
  187.2 4.1 %collective-permute-done.10.refs_1_ = bf16[256,640]{1,0:T(8,128)(2,1)S(1)} collective-permute-done((bf16[256,640]{1,0:T(8,128)(2,1)S(1)}, bf16[256,640]{1,0:T(8,128)(2,1)S(1)}, u32[]{:S(2)}, u32[]{:S(2)}) %collective-permute-start.10) | collective-permute-done | bytes 327712 | tf_op jit(solution)/shard_map/ppermute | solution.py:401
  191.3 7.7 %collective-permute-done.11.refs_2_ = bf16[256,640]{1,0:T(8,128)(2,1)S(1)} collective-permute-done((bf16[256,640]{1,0:T(8,128)(2,1)S(1)}, bf16[256,640]{1,0:T(8,128)(2,1)S(1)}, u32[]{:S(2)}, u32[]{:S(2)}) %collective-permute-start.11) | collective-permute-done | bytes 327712 | tf_op jit(solution)/shard_map/ppermute | solution.py:401
  198.9 1.4 collective-permute-done.12.refs_3_
  200.3 0.0 collective-permute-done.9.refs_4_
  200.3 1.0 collective-permute-start.13
  201.3 14.0 %shard_map.131 = (bf16[1024,640]{1,0:T(8,128)(2,1)}, bf16[1024,640]{1,0:T(8,128)(2,1)}, bf16[1024,640]{1,0:T(8,128)(2,1)}) custom-call(s32[1]{0:T(128)} %bitcast.14.u_ref, bf16[5,1024,1024]{2,1,0:T(8,128)(2,1)} %get-tuple-element.74.p_ref, bf16[1024,640]{1,0:T(8,128)(2,1)} %bitcast.46, bf16[1024,640]{1,0:T(8,128)(2,1)} %bitcast.48, ...), custom_call_target="tpu_custom_call" | custom-call | flops 1000 | bytes 1476000000 | tf_op jit(solution)/shard_map/pallas_call | solution.py:92
  215.4 0.8 collective-permute-done.13
  216.1 0.1 fusion
  216.3 0.0 copy-start.3
  216.3 0.0 all-gather.5.cloned.1.call-done
  216.3 4.0 %shard_map.132 = (f32[64,2560]{1,0:T(8,128)}, f32[64,5120]{1,0:T(8,128)}) custom-call(bf16[8,4,2,16,640]{4,3,2,1,0:T(8,128)(2,1)} %bitcast.52), custom_call_target="tpu_custom_call" | custom-call | flops 1000 | bytes 11070000 | tf_op jit(solution)/shard_map/pallas_call | solution.py:374
  (38 shorter events, 0.2 us)
Async XLA Ops:
  7.2 5.9 %copy-start.1 = (bf16[160,5120]{1,0:T(8,128)(2,1)S(1)}, bf16[160,5120]{1,0:T(8,128)(2,1)}, u32[]{:S(2)}) copy-start(bf16[160,5120]{1,0:T(8,128)(2,1)} %param.12) | copy-start | bytes 4915204
  7.2 90.0 %all-gather.3.cloned.1.call-start = ((), (), s32[]{:S(2)}) async-start(), calls=%async_computation.3 | async-start | bytes 14745600 | tf_op jit(solution)/shard_map/all_gather | solution.py:460
  9.6 12.3 %collective-permute-start = (bf16[80,2560]{1,0:T(8,128)(2,1)}, bf16[80,2560]{1,0:T(8,128)(2,1)S(1)}, u32[]{:S(2)}, u32[]{:S(2)}) collective-permute-start(bf16[80,2560]{1,0:T(8,128)(2,1)} %constant_dynamic-slice_fusion.3), channel_id=1, source_target_pairs={{0,2},{1,3},{2,64},{3,65},{4,6},{5,7},{6,68},{7,69},{8,10},{9,11},... | collective-permute-start | bytes 1228808 | tf_op jit(solution)/shard_map/ppermute | solution.py:413
  11.7 10.2 %collective-permute-start.1 = (bf16[80,2560]{1,0:T(8,128)(2,1)S(1)}, bf16[80,2560]{1,0:T(8,128)(2,1)S(1)}, u32[]{:S(2)}, u32[]{:S(2)}) collective-permute-start(bf16[80,2560]{1,0:T(8,128)(2,1)S(1)} %constant_dynamic-slice_fusion.2), channel_id=1, source_target_pairs={{0,66},{1,67},{2,0},{3,1},{4,70},{5,71},{6,4},{7,5},{8,74},{9,75},... | collective-permute-start | bytes 1228808 | tf_op jit(solution)/shard_map/ppermute | solution.py:413
  24.7 19.8 %collective-permute-start.2 = (bf16[160,2560]{1,0:T(8,128)(2,1)S(1)}, bf16[160,2560]{1,0:T(8,128)(2,1)S(1)}, u32[]{:S(2)}, u32[]{:S(2)}) collective-permute-start(bf16[160,2560]{1,0:T(8,128)(2,1)S(1)} %constant_dynamic-slice_fusion), channel_id=1, source_target_pairs={{0,64},{64,0},{1,65},{65,1},{2,66},{66,2},{3,67},{67,3},{4,68},{68... | collective-permute-start | bytes 2457608 | tf_op jit(solution)/shard_map/ppermute | solution.py:396
  44.5 0.9 copy-start.4
  45.4 37.8 %all-to-all-start = ((bf16[8,256,640]{2,1,0:T(8,128)(2,1)}), bf16[8,256,640]{2,1,0:T(8,128)(2,1)S(1)}, u32[]{:S(2)}, u32[]{:S(2)}) async-start(bf16[8,256,640]{2,1,0:T(8,128)(2,1)} %bitcast.41), calls=%async_computation | async-start | bytes 5242880 | tf_op jit(solution)/shard_map/all_to_all | solution.py:392
  51.4 164.9 %all-gather.5.cloned.1.call-start = ((), (), s32[]{:S(2)}) async-start(), calls=%async_computation.4 | async-start | bytes 1474560 | tf_op jit(solution)/shard_map/all_gather | solution.py:528
  83.2 13.2 %collective-permute-start.3 = (bf16[96,2560]{1,0:T(8,128)(2,1)S(1)}, bf16[96,2560]{1,0:T(8,128)(2,1)}, u32[]{:S(2)}, u32[]{:S(2)}) collective-permute-start(bf16[96,2560]{1,0:T(8,128)(2,1)S(1)} %dynamic-slice.1), channel_id=1, source_target_pairs={{0,64},{64,0},{1,65},{65,1},{2,66},{66,2},{3,67},{67,3},{4,68},{68... | collective-permute-start | bytes 1474568 | tf_op jit(solution)/shard_map/ppermute | solution.py:396
  88.0 1.0 copy-start.9
  88.4 8.8 %copy-start = (bf16[64,8,4,640]{3,1,2,0:T(8,128)(2,1)}, bf16[64,8,4,640]{3,1,2,0:T(8,128)(2,1)S(1)}, u32[]{:S(2)}) copy-start(bf16[64,8,4,640]{3,1,2,0:T(8,128)(2,1)S(1)} %copy.18) | copy-start | bytes 7864324
  132.1 17.4 %collective-permute-start.4 = (bf16[128,2560]{1,0:T(8,128)(2,1)}, bf16[128,2560]{1,0:T(8,128)(2,1)S(1)}, u32[]{:S(2)}, u32[]{:S(2)}) collective-permute-start(bf16[128,2560]{1,0:T(8,128)(2,1)} %get-tuple-element.62), channel_id=1, source_target_pairs={{0,64},{64,0},{1,65},{65,1},{2,66},{66,2},{3,67},{67,3},{4,68},{68... | collective-permute-start | bytes 1966088 | tf_op jit(solution)/shard_map/ppermute | solution.py:396
  132.6 16.9 %copy-start.5 = (bf16[8,4,16,640]{3,2,1,0:T(8,128)(2,1)S(1)}, bf16[8,4,16,640]{3,2,1,0:T(8,128)(2,1)}, u32[]{:S(2)}) copy-start(bf16[8,4,16,640]{3,2,1,0:T(8,128)(2,1)} %get-tuple-element.66) | copy-start | bytes 1966084
  146.8 36.2 %copy-start.6 = (bf16[256,640]{1,0:T(8,128)(2,1)S(1)}, bf16[256,640]{1,0:T(8,128)(2,1)}, u32[]{:S(2)}) copy-start(bf16[256,640]{1,0:T(8,128)(2,1)} %get-tuple-element.69) | copy-start | bytes 983044
  146.8 36.2 %copy-start.7 = (bf16[256,640]{1,0:T(8,128)(2,1)S(1)}, bf16[256,640]{1,0:T(8,128)(2,1)}, u32[]{:S(2)}) copy-start(bf16[256,640]{1,0:T(8,128)(2,1)} %get-tuple-element.71) | copy-start | bytes 983044
  146.8 36.2 %copy-start.8 = (bf16[256,640]{1,0:T(8,128)(2,1)S(1)}, bf16[256,640]{1,0:T(8,128)(2,1)}, u32[]{:S(2)}) copy-start(bf16[256,640]{1,0:T(8,128)(2,1)} %get-tuple-element.72) | copy-start | bytes 983044
  146.8 26.9 %collective-permute-start.5 = (bf16[768,640]{1,0:T(8,128)(2,1)}, bf16[768,640]{1,0:T(8,128)(2,1)S(1)}, u32[]{:S(2)}, u32[]{:S(2)}) collective-permute-start(bf16[768,640]{1,0:T(8,128)(2,1)} %get-tuple-element.64), channel_id=1, source_target_pairs={{0,64},{64,0},{1,65},{65,1},{2,66},{66,2},{3,67},{67,3},{4,68},{68... | collective-permute-start | bytes 2949128 | tf_op jit(solution)/shard_map/ppermute | solution.py:396
  170.4 4.6 %collective-permute-start.6 = (f32[16,640]{1,0:T(8,128)S(1)}, f32[16,640]{1,0:T(8,128)S(1)}, u32[]{:S(2)}, u32[]{:S(2)}) collective-permute-start(f32[16,640]{1,0:T(8,128)S(1)} %convert_reduce_fusion), channel_id=1, source_target_pairs={{0,2},{1,3},{2,64},{3,65},{4,6},{5,7},{6,68},{7,69},{8,10},{9,11},... | collective-permute-start | bytes 122888 | tf_op jit(solution)/shard_map/ppermute | solution.py:413
  171.2 4.4 %collective-permute-start.7 = (f32[16,640]{1,0:T(8,128)S(1)}, f32[16,640]{1,0:T(8,128)S(1)}, u32[]{:S(2)}, u32[]{:S(2)}) collective-permute-start(f32[16,640]{1,0:T(8,128)S(1)} %convert_reduce_fusion), channel_id=1, source_target_pairs={{0,64},{1,65},{2,66},{3,67},{4,68},{5,69},{6,70},{7,71},{8,72},{9,... | collective-permute-start | bytes 122888 | tf_op jit(solution)/shard_map/ppermute | solution.py:413
  172.1 4.1 %collective-permute-start.8 = (f32[16,640]{1,0:T(8,128)S(1)}, f32[16,640]{1,0:T(8,128)S(1)}, u32[]{:S(2)}, u32[]{:S(2)}) collective-permute-start(f32[16,640]{1,0:T(8,128)S(1)} %convert_reduce_fusion), channel_id=1, source_target_pairs={{0,66},{1,67},{2,0},{3,1},{4,70},{5,71},{6,4},{7,5},{8,74},{9,75},... | collective-permute-start | bytes 122888 | tf_op jit(solution)/shard_map/ppermute | solution.py:413
  176.3 2.9 %collective-permute-start.14 = (bf16[32,640]{1,0:T(8,128)(2,1)S(1)}, bf16[32,640]{1,0:T(8,128)(2,1)S(1)}, u32[]{:S(2)}, u32[]{:S(2)}) collective-permute-start(bf16[32,640]{1,0:T(8,128)(2,1)S(1)} %fusion.1), channel_id=1, source_target_pairs={{0,48},{16,0},{32,16},{48,32},{1,49},{17,1},{33,17},{49,33},{2,50}... | collective-permute-start | bytes 122888 | tf_op jit(solution)/shard_map/ppermute | solution.py:401
  176.4 4.4 %collective-permute-start.15 = (bf16[32,640]{1,0:T(8,128)(2,1)S(1)}, bf16[32,640]{1,0:T(8,128)(2,1)S(1)}, u32[]{:S(2)}, u32[]{:S(2)}) collective-permute-start(bf16[32,640]{1,0:T(8,128)(2,1)S(1)} %fusion.1), channel_id=1, source_target_pairs={{0,32},{16,48},{32,0},{48,16},{1,33},{17,49},{33,1},{49,17},{2,34}... | collective-permute-start | bytes 122888 | tf_op jit(solution)/shard_map/ppermute | solution.py:401
  178.1 4.1 %collective-permute-start.16 = (bf16[32,640]{1,0:T(8,128)(2,1)S(1)}, bf16[32,640]{1,0:T(8,128)(2,1)S(1)}, u32[]{:S(2)}, u32[]{:S(2)}) collective-permute-start(bf16[32,640]{1,0:T(8,128)(2,1)S(1)} %fusion.1), channel_id=1, source_target_pairs={{0,16},{16,32},{32,48},{48,0},{1,17},{17,33},{33,49},{49,1},{2,18}... | collective-permute-start | bytes 122888 | tf_op jit(solution)/shard_map/ppermute | solution.py:401
  183.3 8.0 %collective-permute-start.10 = (bf16[256,640]{1,0:T(8,128)(2,1)S(1)}, bf16[256,640]{1,0:T(8,128)(2,1)S(1)}, u32[]{:S(2)}, u32[]{:S(2)}) collective-permute-start(bf16[256,640]{1,0:T(8,128)(2,1)S(1)} %get-tuple-element.92), channel_id=1, source_target_pairs={{0,16},{16,32},{32,48},{48,0},{1,17},{17,33},{33,49},{49,1},{2,18}... | collective-permute-start | bytes 983048 | tf_op jit(solution)/shard_map/ppermute | solution.py:401
  183.4 15.6 %collective-permute-start.11 = (bf16[256,640]{1,0:T(8,128)(2,1)S(1)}, bf16[256,640]{1,0:T(8,128)(2,1)S(1)}, u32[]{:S(2)}, u32[]{:S(2)}) collective-permute-start(bf16[256,640]{1,0:T(8,128)(2,1)S(1)} %get-tuple-element.91), channel_id=1, source_target_pairs={{0,32},{16,48},{32,0},{48,16},{1,33},{17,49},{33,1},{49,17},{2,34}... | collective-permute-start | bytes 983048 | tf_op jit(solution)/shard_map/ppermute | solution.py:401
  186.1 14.2 %collective-permute-start.12 = (bf16[256,640]{1,0:T(8,128)(2,1)S(1)}, bf16[256,640]{1,0:T(8,128)(2,1)S(1)}, u32[]{:S(2)}, u32[]{:S(2)}) collective-permute-start(bf16[256,640]{1,0:T(8,128)(2,1)S(1)} %get-tuple-element.90), channel_id=1, source_target_pairs={{0,48},{16,0},{32,16},{48,32},{1,49},{17,1},{33,17},{49,33},{2,50}... | collective-permute-start | bytes 983048 | tf_op jit(solution)/shard_map/ppermute | solution.py:401
  186.1 14.2 %collective-permute-start.9 = (bf16[256,640]{1,0:T(8,128)(2,1)}, bf16[256,640]{1,0:T(8,128)(2,1)S(1)}, u32[]{:S(2)}, u32[]{:S(2)}) collective-permute-start(bf16[256,640]{1,0:T(8,128)(2,1)} %get-tuple-element.67), channel_id=1, source_target_pairs={{0,64},{64,0},{1,65},{65,1},{2,66},{66,2},{3,67},{67,3},{4,68},{68... | collective-permute-start | bytes 983048 | tf_op jit(solution)/shard_map/ppermute | solution.py:396
  191.3 10.1 %copy-start.10 = (bf16[256,640]{1,0:T(8,128)(2,1)}, bf16[256,640]{1,0:T(8,128)(2,1)S(1)}, u32[]{:S(2)}) copy-start(bf16[256,640]{1,0:T(8,128)(2,1)S(1)} %collective-permute-done.10.refs_1_) | copy-start | bytes 983044
  198.9 2.4 %copy-start.11 = (bf16[256,640]{1,0:T(8,128)(2,1)}, bf16[256,640]{1,0:T(8,128)(2,1)S(1)}, u32[]{:S(2)}) copy-start(bf16[256,640]{1,0:T(8,128)(2,1)S(1)} %collective-permute-done.11.refs_2_) | copy-start | bytes 983044
  200.3 1.0 copy-start.12
  200.3 1.0 copy-start.13
  200.3 15.8 %collective-permute-start.13 = (bf16[128,2560]{1,0:T(8,128)(2,1)}, bf16[128,2560]{1,0:T(8,128)(2,1)S(1)}, u32[]{:S(2)}, u32[]{:S(2)}) collective-permute-start(bf16[128,2560]{1,0:T(8,128)(2,1)} %get-tuple-element.73), channel_id=1, source_target_pairs={{0,64},{64,0},{1,65},{65,1},{2,66},{66,2},{3,67},{67,3},{4,68},{68... | collective-permute-start | bytes 1966088 | tf_op jit(solution)/shard_map/ppermute | solution.py:396
  201.3 14.8 %copy-start.2 = (bf16[256,5120]{1,0:T(8,128)(2,1)S(1)}, bf16[256,5120]{1,0:T(8,128)(2,1)}, u32[]{:S(2)}) copy-start(bf16[256,5120]{1,0:T(8,128)(2,1)} %get-tuple-element.57.own_ref) | copy-start | bytes 7864324
  216.3 4.0 %copy-start.3 = (bf16[1,1,256,5120]{3,2,1,0:T(8,128)(2,1)}, bf16[1,1,256,5120]{3,2,1,0:T(8,128)(2,1)S(1)}, u32[]{:S(2)}) copy-start(bf16[1,1,256,5120]{3,2,1,0:T(8,128)(2,1)S(1)} %fusion) | copy-start | bytes 7864324
Sparse Core Ops, SparseCore 0:
  23.6 73.5 all-gather.2
  183.1 23.8 all-gather.4

commit v4 on v3

--- a/solution.py
+++ b/solution.py
@@ -189,7 +189,7 @@
 
 def guidance_kernel(
     b_ref, v_ref, r_ref, sum_ref, x_ref, m_ref, up_ref,
-    own_ref, oth_ref, mid_ref, both_ref, *refs,
+    own_ref, mid_ref, both_ref, *refs,
 ):
     step = pl.program_id(0)
     tokens, tile = r_ref.shape
@@ -213,7 +213,6 @@
     ).astype(BF16)
     own_ref[...] = jnp.where(first, grad0, grad1)
     other = jnp.where(first, grad1, grad0)
-    oth_ref[...] = other
     at = 0
     for cut_ref in cut_refs:
         cut_ref[...] = other[at : at + cut_ref.shape[0]]
@@ -270,7 +269,6 @@
             ],
             out_specs=[
                 pl.BlockSpec((tokens, tile), mine),
-                pl.BlockSpec((tokens, tile), here),
                 pl.BlockSpec((2 * tokens, rank), whole),
                 pl.BlockSpec(both, lambda j, b: (0, 0, 0, 0)),
             ]
@@ -279,7 +277,6 @@
         ),
         out_shape=[
             jax.ShapeDtypeStruct((tokens, 2 * half), BF16),
-            jax.ShapeDtypeStruct((tokens, half), BF16),
             jax.ShapeDtypeStruct((2 * tokens, rank), BF16),
             jax.ShapeDtypeStruct(both, BF16),
         ]
@@ -289,10 +286,10 @@
     )(branch, vel, reward, sums, attended, middle, up)
 
 
-def gradient_kernel(u_ref, b_ref, own_ref, oth_ref, mid_ref, w_ref, down_ref, *refs):
+def gradient_kernel(u_ref, b_ref, own_ref, early_ref, late_ref, mid_ref, w_ref, down_ref, *refs):
     step = pl.program_id(0)
     tokens = own_ref.shape[0]
-    rows = jnp.concatenate([own_ref[...], oth_ref[...]], axis=0)
+    rows = jnp.concatenate([own_ref[...], early_ref[...], late_ref[...]], axis=0)
     part = dot(rows, weight_rows(w_ref), LAST) + dot(mid_ref[...], down_ref[...])
     part = part.astype(BF16)
     *gown_refs, far_ref, near_ref = refs
@@ -308,8 +305,8 @@
                 near_ref[...] = part[tokens:]
 
 
-def gradient(place, branch, grad_own, grad_other, grad_middle, weight, down_rows, parts):
-    tokens, half = grad_other.shape
+def gradient(place, branch, grad_own, early, late, grad_middle, weight, down_rows, parts):
+    tokens, half = grad_own.shape[0], late.shape[1]
     blocks, block_rows, _ = weight.shape
     rank, depth = down_rows.shape
     wide = depth // parts
@@ -322,7 +319,8 @@
             grid=(parts,),
             in_specs=[
                 pl.BlockSpec((tokens, half), lambda j, u, b: (0, b[0])),
-                pl.BlockSpec((tokens, half), whole),
+                pl.BlockSpec(early.shape, whole),
+                pl.BlockSpec(late.shape, whole),
                 pl.BlockSpec((2 * tokens, rank), whole),
                 pl.BlockSpec(
                     (blocks // parts, block_rows, half), lambda j, u, b: (there(j, u), 0, 0)
@@ -342,7 +340,7 @@
         ],
         compiler_params=params(),
         cost_estimate=lasts(14),
-    )(place, branch, grad_own, grad_other, grad_middle, weight, down_rows)
+    )(place, branch, grad_own, early, late, grad_middle, weight, down_rows)
 
 
 def adapter_kernel(p_ref, down_ref, up_ref):
@@ -479,7 +477,7 @@
     )
     sums = exchange(sums, ("branch", "ulysses"))
     cuts = (tokens // 2, tokens // 2)
-    grad_hidden, grad_other, grad_middle, both, *pieces_out = guidance(
+    grad_hidden, grad_middle, both, *pieces_out = guidance(
         branch_word, vel, reward2, sums, gathered, middle, adapter_up_weight, cuts
     )
     received = [swap(pieces_out[0])]
@@ -495,7 +493,7 @@
     pieces = row_groups * lanes
     down_rows = adapter_down_weight.T
     *grads, far, close = gradient(
-        place, branch_word, grad_hidden, grad_other, grad_middle, weight, down_rows, parts
+        place, branch_word, grad_hidden, *pieces_out, grad_middle, weight, down_rows, parts
     )
     far = swap(far)
     both, grads[3], received[0] = lax.optimization_barrier((both, grads[3], received[0]))

time: 231 us -> 231 us (level)
  no operation moved by 1% of the time
where the time goes in v4:
time: 231 us; the launch traced here: 228 us
  Pallas kernels  71.1 us (31%)
  waiting for transfers between devices  66.6 us (29%)
  blocking collectives  33.9 us (15%)
  starting transfers between devices  28 us (12%)
  between operations  14.3 us (6%)
  local copies, waits for them, and re-layouts  9.53 us (4%)
  other arithmetic  2.99 us (1%)
    all_to_all x1, waiting for transfers between devices, exchange(): return lax.all_to_all(block, axes, split_axis=0, concat_axis=0, tiled=True)  30.7 us
    all_to_all x1, blocking collectives, body(): lax.all_to_all(block, ('ulysses', 'fsdp'), split_axis=0, concat_axis=0, t...  20.8 us
    pallas_call x1, Pallas kernels, attention_forward(): pl.pallas_call(forward_kernel, grid=(heads,), in_specs=[block] * 3, out_s...  17.4 us
    ppermute x6, waiting for transfers between devices, ahead_send(): lax.ppermute(block, 'ulysses', [(u, (u + ahead) % parts) for u in range(p...  17.1 us
    pallas_call x1, Pallas kernels, gradient(): pl.pallas_call(gradient_kernel, grid_spec=pltpu.PrefetchScalarGridSpec(nu...  14.2 us
    pallas_call x1, Pallas kernels, attention_backward(): pl.pallas_call(backward_kernel, grid_spec=pltpu.PrefetchScalarGridSpec(nu...  14 us
    pallas_call x1, Pallas kernels, velocity(): pl.pallas_call(velocity_kernel, grid_spec=pltpu.PrefetchScalarGridSpec(nu...  13.7 us
    all_to_all x1, blocking collectives, exchange(): return lax.all_to_all(block, axes, split_axis=0, concat_axis=0, tiled=True)  13.1 us
  transfers between devices with their start and end apart: 20, of which 14 were waited for; matrix products, arithmetic and copies ran while one was open for 3% of the time, Pallas kernels for 20%

profile of v4, /device:TPU:1, one launch (start us, length us, event | category | flops | bytes accessed | tf_op | source)
XLA Modules:
  0.0 227.9 jit_solution(16019555489516453936)
XLA Ops:
  7.2 0.0 all-gather.3.cloned.1.call-start
  7.2 1.6 fusion.2
  8.9 0.8 constant_dynamic-slice_fusion.3
  9.6 2.0 collective-permute-start
  11.7 1.3 collective-permute-start.1
  13.1 0.1 constant_dynamic-slice_fusion.4
  13.1 8.8 %collective-permute-done = bf16[80,2560]{1,0:T(8,128)(2,1)S(1)} collective-permute-done((bf16[80,2560]{1,0:T(8,128)(2,1)}, bf16[80,2560]{1,0:T(8,128)(2,1)S(1)}, u32[]{:S(2)}, u32[]{:S(2)}) %collective-permute-start) | collective-permute-done | bytes 409632 | tf_op jit(solution)/shard_map/ppermute | solution.py:411
  21.9 0.0 collective-permute-done.1
  21.9 1.5 maximum_select_fusion
  23.4 0.0 all-gather.3.cloned.1.call-update
  23.4 1.2 constant_dynamic-slice_fusion
  24.6 2.4 %collective-permute-start.2 = (bf16[160,2560]{1,0:T(8,128)(2,1)S(1)}, bf16[160,2560]{1,0:T(8,128)(2,1)S(1)}, u32[]{:S(2)}, u32[]{:S(2)}) collective-permute-start(bf16[160,2560]{1,0:T(8,128)(2,1)S(1)} %constant_dynamic-slice_fusion), channel_id=1, source_target_pairs={{0,64},{64,0},{1,65},{65,1},{2,66},{66,2},{3,67},{67,3},{4,68},{68... | collective-permute-start | bytes 2457608 | tf_op jit(solution)/shard_map/ppermute | solution.py:394
  27.1 17.4 %shard_map.127 = (bf16[5,1024,1024]{2,1,0:T(8,128)(2,1)}, bf16[2,4,256,640]{3,2,1,0:T(8,128)(2,1)}) custom-call(bf16[1024,640]{1,0:T(8,128)(2,1)} %bitcast.45, bf16[1024,640]{1,0:T(8,128)(2,1)} %bitcast.47, bf16[1024,640]{1,0:T(8,128)(2,1)} %bitcast.49), custom_call_target="tpu_custom_call" | custom-call | flops 1000 | bytes 59040000 | tf_op jit(solution)/shard_map/pallas_call | solution.py:49
  44.5 0.0 collective-permute-done.2.hoth_ref
  44.5 0.9 copy-done.4
  45.4 6.0 %all-to-all-start = ((bf16[8,256,640]{2,1,0:T(8,128)(2,1)}), bf16[8,256,640]{2,1,0:T(8,128)(2,1)S(1)}, u32[]{:S(2)}, u32[]{:S(2)}) async-start(bf16[8,256,640]{2,1,0:T(8,128)(2,1)} %bitcast.41), calls=%async_computation | async-start | bytes 5242880 | tf_op jit(solution)/shard_map/all_to_all | solution.py:390
  51.4 0.0 all-gather.5.cloned.1.call-start
  51.4 1.2 dynamic-slice.1
  52.5 30.7 %all-to-all-done = bf16[8,256,640]{2,1,0:T(8,128)(2,1)S(1)} async-done(((bf16[8,256,640]{2,1,0:T(8,128)(2,1)}), bf16[8,256,640]{2,1,0:T(8,128)(2,1)S(1)}, u32[]{:S(2)}, u32[]{:S(2)}) %all-to-all-start) | async-done | bytes 2621472 | tf_op jit(solution)/shard_map/all_to_all | solution.py:390
  83.2 2.7 %collective-permute-start.3 = (bf16[96,2560]{1,0:T(8,128)(2,1)S(1)}, bf16[96,2560]{1,0:T(8,128)(2,1)}, u32[]{:S(2)}, u32[]{:S(2)}) collective-permute-start(bf16[96,2560]{1,0:T(8,128)(2,1)S(1)} %dynamic-slice.1), channel_id=1, source_target_pairs={{0,64},{64,0},{1,65},{65,1},{2,66},{66,2},{3,67},{67,3},{4,68},{68... | collective-permute-start | bytes 1474568 | tf_op jit(solution)/shard_map/ppermute | solution.py:394
  85.9 2.0 copy.15
  87.9 0.0 copy-start.11
  87.9 0.4 copy.18
  88.4 0.5 copy-done.11
  88.9 1.5 convolution_convert_fusion.m_ref
  90.4 6.0 %collective-permute-done.3.hlate_ref = bf16[96,2560]{1,0:T(8,128)(2,1)} collective-permute-done((bf16[96,2560]{1,0:T(8,128)(2,1)S(1)}, bf16[96,2560]{1,0:T(8,128)(2,1)}, u32[]{:S(2)}, u32[]{:S(2)}) %collective-permute-start.3) | collective-permute-done | bytes 491552 | tf_op jit(solution)/shard_map/ppermute | solution.py:394
  96.4 0.8 all-gather.3.cloned.1.call-done
  97.2 13.7 %shard_map.128 = (bf16[2,256,2560]{2,1,0:T(8,128)(2,1)}, f32[64,128]{1,0:T(8,128)}) custom-call(s32[1]{0:T(128)} %bitcast.b_ref, bf16[512,2560]{1,0:T(8,128)(2,1)} %bitcast.35, bf16[512,64]{1,0:T(8,128)(2,1)} %convolution_convert_fusion.m_ref, bf16[16,160,2560]{2,1,0:T(8,128)(2,1)} %bitcast.32, bf16[256,5120]{1,0:T(8,128)(2,1)} %bitcast.44, ...), custom_call_target="tpu_custom_call" | custom-call | flops 1000 | bytes 51660000 | tf_op jit(solution)/shard_map/pallas_call | solution.py:160
  110.9 13.1 %all_to_all.32 = f32[8,8,128]{2,1,0:T(8,128)} all-to-all(f32[8,8,128]{2,1,0:T(8,128)} %bitcast.56), channel_id=1, replica_groups=mesh['branch'=2,'ulysses'=4,'fsdp'=16] {'branch','ulysses'}, dimensions={0} | all-to-all | bytes 65536 | tf_op jit(solution)/shard_map/all_to_all | solution.py:390
  124.0 7.8 %shard_map.129 = (bf16[256,5120]{1,0:T(8,128)(2,1)}, bf16[512,64]{1,0:T(8,128)(2,1)}, bf16[8,4,16,640]{3,2,1,0:T(8,128)(2,1)}, bf16[128,2560]{1,0:T(8,128)(2,1)}, bf16[128,2560]{1,0:T(8,128)(2,1)}) custom-call(s32[1]{0:T(128)} %bitcast.b_ref, bf16[2,256,2560]{2,1,0:T(8,128)(2,1)} %get-tuple-element.54.v_ref, bf16[256,5120]{1,0:T(8,128)(2,1)} %bitcast.38, ...), custom_call_target="tpu_custom_call" | custom-call | flops 1000 | bytes 29520000 | tf_op jit(solution)/shard_map/pallas_call | solution.py:257
  131.8 0.5 collective-permute-start.4
  132.3 14.2 %shard_map.130 = (bf16[256,640]{1,0:T(8,128)(2,1)}, bf16[256,640]{1,0:T(8,128)(2,1)}, bf16[256,640]{1,0:T(8,128)(2,1)}, bf16[256,640]{1,0:T(8,128)(2,1)}, bf16[7...) custom-call(s32[1]{0:T(128)} %bitcast.14.u_ref, s32[1]{0:T(128)} %bitcast.b_ref, ...), custom_call_target="tpu_custom_call" | custom-call | flops 1000 | bytes 51660000 | tf_op jit(solution)/shard_map/pallas_call | solution.py:315
  146.5 2.8 %collective-permute-start.5 = (bf16[768,640]{1,0:T(8,128)(2,1)}, bf16[768,640]{1,0:T(8,128)(2,1)S(1)}, u32[]{:S(2)}, u32[]{:S(2)}) collective-permute-start(bf16[768,640]{1,0:T(8,128)(2,1)} %get-tuple-element.63), channel_id=1, source_target_pairs={{0,64},{64,0},{1,65},{65,1},{2,66},{66,2},{3,67},{67,3},{4,68},{68... | collective-permute-start | bytes 2949128 | tf_op jit(solution)/shard_map/ppermute | solution.py:394
  149.3 20.8 %all_to_all.33 = bf16[32,16,640]{2,1,0:T(8,128)(2,1)S(1)} all-to-all(bf16[32,16,640]{2,1,0:T(8,128)(2,1)S(1)} %bitcast.53), channel_id=1, replica_groups={{0,1,4,5,8,9,12,13,16,17,20,21,24,25,28,29,32,33,36,37,40,41,44,45,48,4..., dimensions={0} | all-to-all | bytes 1310720 | tf_op jit(solution)/shard_map/all_to_all | solution.py:489
  170.0 0.1 convert_reduce_fusion
  170.1 0.8 collective-permute-start.6
  170.9 1.0 collective-permute-start.7
  171.9 1.6 collective-permute-start.8
  173.4 0.0 collective-permute-done.5
  173.4 1.3 collective-permute-done.6
  174.7 0.6 collective-permute-done.7
  175.3 0.7 collective-permute-done.8
  176.0 0.2 collective-permute-start.14
  176.2 1.7 collective-permute-start.15
  177.9 0.0 collective-permute-start.16
  177.9 1.1 collective-permute-done.14
  179.0 1.6 collective-permute-done.15
  180.6 1.4 collective-permute-done.16
  182.0 0.7 constant_dynamic-slice_fusion.1
  182.7 0.0 all-gather.5.cloned.1.call-update
  182.8 1.2 add_convert_fusion
  184.0 0.1 collective-permute-start.10
  184.1 2.7 %collective-permute-start.11 = (bf16[256,640]{1,0:T(8,128)(2,1)S(1)}, bf16[256,640]{1,0:T(8,128)(2,1)S(1)}, u32[]{:S(2)}, u32[]{:S(2)}) collective-permute-start(bf16[256,640]{1,0:T(8,128)(2,1)S(1)} %get-tuple-element.89), channel_id=1, source_target_pairs={{0,32},{16,48},{32,0},{48,16},{1,33},{17,49},{33,1},{49,17},{2,34}... | collective-permute-start | bytes 983048 | tf_op jit(solution)/shard_map/ppermute | solution.py:399
  186.8 1.1 collective-permute-start.9
  187.9 4.1 %collective-permute-done.10.refs_1_ = bf16[256,640]{1,0:T(8,128)(2,1)S(1)} collective-permute-done((bf16[256,640]{1,0:T(8,128)(2,1)S(1)}, bf16[256,640]{1,0:T(8,128)(2,1)S(1)}, u32[]{:S(2)}, u32[]{:S(2)}) %collective-permute-start.10) | collective-permute-done | bytes 327712 | tf_op jit(solution)/shard_map/ppermute | solution.py:399
  192.0 7.7 %collective-permute-done.11.refs_2_ = bf16[256,640]{1,0:T(8,128)(2,1)S(1)} collective-permute-done((bf16[256,640]{1,0:T(8,128)(2,1)S(1)}, bf16[256,640]{1,0:T(8,128)(2,1)S(1)}, u32[]{:S(2)}, u32[]{:S(2)}) %collective-permute-start.11) | collective-permute-done | bytes 327712 | tf_op jit(solution)/shard_map/ppermute | solution.py:399
  199.7 1.4 collective-permute-done.12.refs_3_
  201.0 1.1 collective-permute-start.13
  202.2 14.0 %shard_map.131 = (bf16[1024,640]{1,0:T(8,128)(2,1)}, bf16[1024,640]{1,0:T(8,128)(2,1)}, bf16[1024,640]{1,0:T(8,128)(2,1)}) custom-call(s32[1]{0:T(128)} %bitcast.14.u_ref, bf16[5,1024,1024]{2,1,0:T(8,128)(2,1)} %get-tuple-element.72.p_ref, bf16[1024,640]{1,0:T(8,128)(2,1)} %bitcast.46, bf16[1024,640]{1,0:T(8,128)(2,1)} %bitcast.48, ...), custom_call_target="tpu_custom_call" | custom-call | flops 1000 | bytes 1476000000 | tf_op jit(solution)/shard_map/pallas_call | solution.py:92
  216.2 0.6 collective-permute-done.13
  216.8 0.1 fusion
  217.0 0.0 copy-start.3
  217.0 0.0 all-gather.5.cloned.1.call-done
  217.0 4.0 %shard_map.132 = (f32[64,2560]{1,0:T(8,128)}, f32[64,5120]{1,0:T(8,128)}) custom-call(bf16[8,4,2,16,640]{4,3,2,1,0:T(8,128)(2,1)} %bitcast.52), custom_call_target="tpu_custom_call" | custom-call | flops 1000 | bytes 11070000 | tf_op jit(solution)/shard_map/pallas_call | solution.py:372
  (42 shorter events, 0.2 us)
Async XLA Ops:
  7.2 5.9 %copy-start.1 = (bf16[160,5120]{1,0:T(8,128)(2,1)S(1)}, bf16[160,5120]{1,0:T(8,128)(2,1)}, u32[]{:S(2)}) copy-start(bf16[160,5120]{1,0:T(8,128)(2,1)} %param.12) | copy-start | bytes 4915204
  7.2 90.0 %all-gather.3.cloned.1.call-start = ((), (), s32[]{:S(2)}) async-start(), calls=%async_computation.3 | async-start | bytes 14745600 | tf_op jit(solution)/shard_map/all_gather | solution.py:458
  9.6 12.3 %collective-permute-start = (bf16[80,2560]{1,0:T(8,128)(2,1)}, bf16[80,2560]{1,0:T(8,128)(2,1)S(1)}, u32[]{:S(2)}, u32[]{:S(2)}) collective-permute-start(bf16[80,2560]{1,0:T(8,128)(2,1)} %constant_dynamic-slice_fusion.3), channel_id=1, source_target_pairs={{0,2},{1,3},{2,64},{3,65},{4,6},{5,7},{6,68},{7,69},{8,10},{9,11},... | collective-permute-start | bytes 1228808 | tf_op jit(solution)/shard_map/ppermute | solution.py:411
  11.7 10.2 %collective-permute-start.1 = (bf16[80,2560]{1,0:T(8,128)(2,1)S(1)}, bf16[80,2560]{1,0:T(8,128)(2,1)S(1)}, u32[]{:S(2)}, u32[]{:S(2)}) collective-permute-start(bf16[80,2560]{1,0:T(8,128)(2,1)S(1)} %constant_dynamic-slice_fusion.2), channel_id=1, source_target_pairs={{0,66},{1,67},{2,0},{3,1},{4,70},{5,71},{6,4},{7,5},{8,74},{9,75},... | collective-permute-start | bytes 1228808 | tf_op jit(solution)/shard_map/ppermute | solution.py:411
  24.6 19.8 %collective-permute-start.2 = (bf16[160,2560]{1,0:T(8,128)(2,1)S(1)}, bf16[160,2560]{1,0:T(8,128)(2,1)S(1)}, u32[]{:S(2)}, u32[]{:S(2)}) collective-permute-start(bf16[160,2560]{1,0:T(8,128)(2,1)S(1)} %constant_dynamic-slice_fusion), channel_id=1, source_target_pairs={{0,64},{64,0},{1,65},{65,1},{2,66},{66,2},{3,67},{67,3},{4,68},{68... | collective-permute-start | bytes 2457608 | tf_op jit(solution)/shard_map/ppermute | solution.py:394
  44.5 0.9 copy-start.4
  45.4 37.8 %all-to-all-start = ((bf16[8,256,640]{2,1,0:T(8,128)(2,1)}), bf16[8,256,640]{2,1,0:T(8,128)(2,1)S(1)}, u32[]{:S(2)}, u32[]{:S(2)}) async-start(bf16[8,256,640]{2,1,0:T(8,128)(2,1)} %bitcast.41), calls=%async_computation | async-start | bytes 5242880 | tf_op jit(solution)/shard_map/all_to_all | solution.py:390
  51.4 165.6 %all-gather.5.cloned.1.call-start = ((), (), s32[]{:S(2)}) async-start(), calls=%async_computation.4 | async-start | bytes 1474560 | tf_op jit(solution)/shard_map/all_gather | solution.py:526
  83.2 13.2 %collective-permute-start.3 = (bf16[96,2560]{1,0:T(8,128)(2,1)S(1)}, bf16[96,2560]{1,0:T(8,128)(2,1)}, u32[]{:S(2)}, u32[]{:S(2)}) collective-permute-start(bf16[96,2560]{1,0:T(8,128)(2,1)S(1)} %dynamic-slice.1), channel_id=1, source_target_pairs={{0,64},{64,0},{1,65},{65,1},{2,66},{66,2},{3,67},{67,3},{4,68},{68... | collective-permute-start | bytes 1474568 | tf_op jit(solution)/shard_map/ppermute | solution.py:394
  87.9 1.0 copy-start.11
  88.4 8.8 %copy-start = (bf16[64,8,4,640]{3,1,2,0:T(8,128)(2,1)}, bf16[64,8,4,640]{3,1,2,0:T(8,128)(2,1)S(1)}, u32[]{:S(2)}) copy-start(bf16[64,8,4,640]{3,1,2,0:T(8,128)(2,1)S(1)} %copy.18) | copy-start | bytes 7864324
  131.8 17.5 %collective-permute-start.4 = (bf16[128,2560]{1,0:T(8,128)(2,1)}, bf16[128,2560]{1,0:T(8,128)(2,1)S(1)}, u32[]{:S(2)}, u32[]{:S(2)}) collective-permute-start(bf16[128,2560]{1,0:T(8,128)(2,1)} %get-tuple-element.58.early_ref), channel_id=1, source_target_pairs={{0,64},{64,0},{1,65},{65,1},{2,66},{66,2},{3,67},{67,3},{4,68},{68... | collective-permute-start | bytes 1966088 | tf_op jit(solution)/shard_map/ppermute | solution.py:394
  132.3 16.9 %copy-start.6 = (bf16[8,4,16,640]{3,2,1,0:T(8,128)(2,1)S(1)}, bf16[8,4,16,640]{3,2,1,0:T(8,128)(2,1)}, u32[]{:S(2)}) copy-start(bf16[8,4,16,640]{3,2,1,0:T(8,128)(2,1)} %get-tuple-element.65) | copy-start | bytes 1966084
  146.5 36.3 %copy-start.9 = (bf16[256,640]{1,0:T(8,128)(2,1)S(1)}, bf16[256,640]{1,0:T(8,128)(2,1)}, u32[]{:S(2)}) copy-start(bf16[256,640]{1,0:T(8,128)(2,1)} %get-tuple-element.67) | copy-start | bytes 983044
  146.5 36.3 %copy-start.10 = (bf16[256,640]{1,0:T(8,128)(2,1)S(1)}, bf16[256,640]{1,0:T(8,128)(2,1)}, u32[]{:S(2)}) copy-start(bf16[256,640]{1,0:T(8,128)(2,1)} %get-tuple-element.69) | copy-start | bytes 983044
  146.5 26.9 %collective-permute-start.5 = (bf16[768,640]{1,0:T(8,128)(2,1)}, bf16[768,640]{1,0:T(8,128)(2,1)S(1)}, u32[]{:S(2)}, u32[]{:S(2)}) collective-permute-start(bf16[768,640]{1,0:T(8,128)(2,1)} %get-tuple-element.63), channel_id=1, source_target_pairs={{0,64},{64,0},{1,65},{65,1},{2,66},{66,2},{3,67},{67,3},{4,68},{68... | collective-permute-start | bytes 2949128 | tf_op jit(solution)/shard_map/ppermute | solution.py:394
  149.3 34.7 %copy-start.7 = (bf16[128,2560]{1,0:T(8,128)(2,1)}, bf16[128,2560]{1,0:T(8,128)(2,1)S(1)}, u32[]{:S(2)}) copy-start(bf16[128,2560]{1,0:T(8,128)(2,1)S(1)} %collective-permute-done.4) | copy-start | bytes 1966084
  170.0 31.0 %copy-start.5 = (bf16[128,2560]{1,0:T(8,128)(2,1)S(1)}, bf16[128,2560]{1,0:T(8,128)(2,1)}, u32[]{:S(2)}) copy-start(bf16[128,2560]{1,0:T(8,128)(2,1)} %get-tuple-element.71.late_ref) | copy-start | bytes 1966084
  170.1 4.6 %collective-permute-start.6 = (f32[16,640]{1,0:T(8,128)S(1)}, f32[16,640]{1,0:T(8,128)S(1)}, u32[]{:S(2)}, u32[]{:S(2)}) collective-permute-start(f32[16,640]{1,0:T(8,128)S(1)} %convert_reduce_fusion), channel_id=1, source_target_pairs={{0,2},{1,3},{2,64},{3,65},{4,6},{5,7},{6,68},{7,69},{8,10},{9,11},... | collective-permute-start | bytes 122888 | tf_op jit(solution)/shard_map/ppermute | solution.py:411
  170.9 4.4 %collective-permute-start.7 = (f32[16,640]{1,0:T(8,128)S(1)}, f32[16,640]{1,0:T(8,128)S(1)}, u32[]{:S(2)}, u32[]{:S(2)}) collective-permute-start(f32[16,640]{1,0:T(8,128)S(1)} %convert_reduce_fusion), channel_id=1, source_target_pairs={{0,64},{1,65},{2,66},{3,67},{4,68},{5,69},{6,70},{7,71},{8,72},{9,... | collective-permute-start | bytes 122888 | tf_op jit(solution)/shard_map/ppermute | solution.py:411
  171.9 4.2 %collective-permute-start.8 = (f32[16,640]{1,0:T(8,128)S(1)}, f32[16,640]{1,0:T(8,128)S(1)}, u32[]{:S(2)}, u32[]{:S(2)}) collective-permute-start(f32[16,640]{1,0:T(8,128)S(1)} %convert_reduce_fusion), channel_id=1, source_target_pairs={{0,66},{1,67},{2,0},{3,1},{4,70},{5,71},{6,4},{7,5},{8,74},{9,75},... | collective-permute-start | bytes 122888 | tf_op jit(solution)/shard_map/ppermute | solution.py:411
  176.0 2.9 %collective-permute-start.14 = (bf16[32,640]{1,0:T(8,128)(2,1)S(1)}, bf16[32,640]{1,0:T(8,128)(2,1)S(1)}, u32[]{:S(2)}, u32[]{:S(2)}) collective-permute-start(bf16[32,640]{1,0:T(8,128)(2,1)S(1)} %fusion.1), channel_id=1, source_target_pairs={{0,48},{16,0},{32,16},{48,32},{1,49},{17,1},{33,17},{49,33},{2,50}... | collective-permute-start | bytes 122888 | tf_op jit(solution)/shard_map/ppermute | solution.py:399
  176.2 4.4 %collective-permute-start.15 = (bf16[32,640]{1,0:T(8,128)(2,1)S(1)}, bf16[32,640]{1,0:T(8,128)(2,1)S(1)}, u32[]{:S(2)}, u32[]{:S(2)}) collective-permute-start(bf16[32,640]{1,0:T(8,128)(2,1)S(1)} %fusion.1), channel_id=1, source_target_pairs={{0,32},{16,48},{32,0},{48,16},{1,33},{17,49},{33,1},{49,17},{2,34}... | collective-permute-start | bytes 122888 | tf_op jit(solution)/shard_map/ppermute | solution.py:399
  177.9 4.1 %collective-permute-start.16 = (bf16[32,640]{1,0:T(8,128)(2,1)S(1)}, bf16[32,640]{1,0:T(8,128)(2,1)S(1)}, u32[]{:S(2)}, u32[]{:S(2)}) collective-permute-start(bf16[32,640]{1,0:T(8,128)(2,1)S(1)} %fusion.1), channel_id=1, source_target_pairs={{0,16},{16,32},{32,48},{48,0},{1,17},{17,33},{33,49},{49,1},{2,18}... | collective-permute-start | bytes 122888 | tf_op jit(solution)/shard_map/ppermute | solution.py:399
  184.0 8.0 %collective-permute-start.10 = (bf16[256,640]{1,0:T(8,128)(2,1)S(1)}, bf16[256,640]{1,0:T(8,128)(2,1)S(1)}, u32[]{:S(2)}, u32[]{:S(2)}) collective-permute-start(bf16[256,640]{1,0:T(8,128)(2,1)S(1)} %get-tuple-element.90), channel_id=1, source_target_pairs={{0,16},{16,32},{32,48},{48,0},{1,17},{17,33},{33,49},{49,1},{2,18}... | collective-permute-start | bytes 983048 | tf_op jit(solution)/shard_map/ppermute | solution.py:399
  184.1 15.6 %collective-permute-start.11 = (bf16[256,640]{1,0:T(8,128)(2,1)S(1)}, bf16[256,640]{1,0:T(8,128)(2,1)S(1)}, u32[]{:S(2)}, u32[]{:S(2)}) collective-permute-start(bf16[256,640]{1,0:T(8,128)(2,1)S(1)} %get-tuple-element.89), channel_id=1, source_target_pairs={{0,32},{16,48},{32,0},{48,16},{1,33},{17,49},{33,1},{49,17},{2,34}... | collective-permute-start | bytes 983048 | tf_op jit(solution)/shard_map/ppermute | solution.py:399
  186.8 14.2 %collective-permute-start.12 = (bf16[256,640]{1,0:T(8,128)(2,1)S(1)}, bf16[256,640]{1,0:T(8,128)(2,1)S(1)}, u32[]{:S(2)}, u32[]{:S(2)}) collective-permute-start(bf16[256,640]{1,0:T(8,128)(2,1)S(1)} %get-tuple-element.88), channel_id=1, source_target_pairs={{0,48},{16,0},{32,16},{48,32},{1,49},{17,1},{33,17},{49,33},{2,50}... | collective-permute-start | bytes 983048 | tf_op jit(solution)/shard_map/ppermute | solution.py:399
  186.8 14.2 %collective-permute-start.9 = (bf16[256,640]{1,0:T(8,128)(2,1)}, bf16[256,640]{1,0:T(8,128)(2,1)S(1)}, u32[]{:S(2)}, u32[]{:S(2)}) collective-permute-start(bf16[256,640]{1,0:T(8,128)(2,1)} %get-tuple-element.66), channel_id=1, source_target_pairs={{0,64},{64,0},{1,65},{65,1},{2,66},{66,2},{3,67},{67,3},{4,68},{68... | collective-permute-start | bytes 983048 | tf_op jit(solution)/shard_map/ppermute | solution.py:394
  192.0 10.1 %copy-start.12 = (bf16[256,640]{1,0:T(8,128)(2,1)}, bf16[256,640]{1,0:T(8,128)(2,1)S(1)}, u32[]{:S(2)}) copy-start(bf16[256,640]{1,0:T(8,128)(2,1)S(1)} %collective-permute-done.10.refs_1_) | copy-start | bytes 983044
  199.7 2.5 %copy-start.13 = (bf16[256,640]{1,0:T(8,128)(2,1)}, bf16[256,640]{1,0:T(8,128)(2,1)S(1)}, u32[]{:S(2)}) copy-start(bf16[256,640]{1,0:T(8,128)(2,1)S(1)} %collective-permute-done.11.refs_2_) | copy-start | bytes 983044
  201.0 1.1 copy-start.14
  201.0 1.1 copy-start.15
  201.0 15.8 %collective-permute-start.13 = (bf16[128,2560]{1,0:T(8,128)(2,1)S(1)}, bf16[128,2560]{1,0:T(8,128)(2,1)S(1)}, u32[]{:S(2)}, u32[]{:S(2)}) collective-permute-start(bf16[128,2560]{1,0:T(8,128)(2,1)S(1)} %copy-done.5), channel_id=1, source_target_pairs={{0,64},{64,0},{1,65},{65,1},{2,66},{66,2},{3,67},{67,3},{4,68},{68... | collective-permute-start | bytes 1966088 | tf_op jit(solution)/shard_map/ppermute | solution.py:394
  202.2 14.7 %copy-start.2 = (bf16[256,5120]{1,0:T(8,128)(2,1)S(1)}, bf16[256,5120]{1,0:T(8,128)(2,1)}, u32[]{:S(2)}) copy-start(bf16[256,5120]{1,0:T(8,128)(2,1)} %get-tuple-element.56.own_ref) | copy-start | bytes 7864324
  202.2 14.6 %copy-start.8 = (bf16[128,2560]{1,0:T(8,128)(2,1)S(1)}, bf16[128,2560]{1,0:T(8,128)(2,1)}, u32[]{:S(2)}) copy-start(bf16[128,2560]{1,0:T(8,128)(2,1)} %copy-done.7) | copy-start | bytes 1966084
  217.0 4.0 %copy-start.3 = (bf16[1,1,256,5120]{3,2,1,0:T(8,128)(2,1)}, bf16[1,1,256,5120]{3,2,1,0:T(8,128)(2,1)S(1)}, u32[]{:S(2)}) copy-start(bf16[1,1,256,5120]{3,2,1,0:T(8,128)(2,1)S(1)} %fusion) | copy-start | bytes 7864324
Sparse Core Ops, SparseCore 0:
  23.6 73.5 all-gather.2
  182.9 23.8 all-gather.4
